TPU v7x, 256 devices: a whole 4x4x8 slice. The times are simulated.
256 devices in a mesh: col: 32 (over z, x), row: 8 (over y, core).
Axes of the slice: x: 4, y: 4, z: 8, core: 2. Of those that a mesh axis runs over, the one named last changes fastest.
Arguments:
- panel: bfloat16 [4096, 4096], P('row', 'col'), may hold values from -0.09375 to 0.09375
- inv_factor: bfloat16 [4096, 4096], P('col'), as said below
- fill: int32 [32, 32], replicated, may hold values from 0 to 1, as said below
- owner: int32 [32], replicated, may hold values from 0 to 31, as said below
- trailing: float32 [4096, 4096], P('row', 'col'), may hold values from -6 to 6
- cotangent: float32 [4096, 4096], P('row', 'col'), may hold values from -6 to 6
Outputs:
- updated: float32 [4096, 4096], P('row', 'col')
- panel_grad: float32 [4096, 4096], P('row', 'col')
Inputs may be any that keep to these rules, and one draw needn't show every extreme that they name: fill is 1 on the diagonal, 0 above it, and 0 or 1 below it. `owner`: every col index owns exactly 1 block column. inv_factor is upper triangular with a positive diagonal.
All inputs are finite; a program needn't handle non-finite values.
Results may differ from a plain program's by a relative error of at most 0.0047.
Values may be sent and summed in bfloat16 or wider, within the bound.
No kernel may reach another device: no remote copies, remote signals or barrier semaphores. Data moves between devices by JAX's collectives and lax.ppermute only.
A program may use at most 128 MiB of HBM per device.

v0:
```python
import jax
import jax.numpy as jnp
from jax import lax
from jax.sharding import PartitionSpec as P

BS = 128
BCOL = 1


def spread(value, axis, source):
    kept = jnp.where(lax.axis_index(axis) == source, value, 0).astype(value.dtype)
    return lax.psum(kept, axis)


def slot_columns(owner):
    count = owner.shape[0]
    index = jnp.arange(count, dtype=jnp.int32)
    same = (owner[:, None] == owner[None, :]) & (index[None, :] < index[:, None])
    rank = jnp.sum(same.astype(jnp.int32), axis=1)
    slot = owner * BCOL + rank
    hits = (slot[None, :] == index[:, None]).astype(jnp.int32)
    return jnp.sum(hits * index[None, :], axis=1)


def on_device(panel, inv_factor, fill, owner, trailing, cotangent):
    rows = panel.shape[0]
    per_row = rows // BS
    owned_count = trailing.shape[1] // BS
    total_blocks = owner.shape[0]
    col_index = lax.axis_index("col")
    row_index = lax.axis_index("row")
    column_of_slot = slot_columns(owner)
    mine = lax.dynamic_slice_in_dim(column_of_slot, col_index * owned_count, owned_count)
    first_block = row_index * per_row
    inside = [mine[0] // per_row == row_index]
    where_at = [jnp.clip(mine[0] - first_block, 0, per_row - 1)]
    holders = [mine[0] // per_row]
    kslice = inv_factor
    factor_piece = lax.psum_scatter(
        lax.dot_general(
            kslice, panel, (((0,), (1,)), ((), ())), preferred_element_type=jnp.float32
        ),
        "col",
        scatter_dimension=0,
        tiled=True,
    ).astype(jnp.bfloat16)
    factor_rows = lax.all_gather(factor_piece, "col", axis=0, tiled=True)
    k = 0
    candidate = lax.dynamic_slice_in_dim(factor_rows, where_at[k] * BS, BS, 1)
    pieces = spread(candidate, "row", holders[k])
    fill_rows = lax.dynamic_slice_in_dim(fill, first_block, per_row, 0).astype(jnp.float32)
    select = (jnp.arange(total_blocks, dtype=jnp.int32)[:, None] == mine[None, :]).astype(
        jnp.float32
    )
    block_mask = jnp.dot(fill_rows, select, precision=lax.Precision.HIGHEST)
    mask = jnp.broadcast_to(block_mask[:, None, :, None], (per_row, BS, owned_count, BS)).reshape(
        rows, owned_count * BS
    )
    products = lax.dot_general(
        factor_rows, pieces, (((0,), (0,)), ((), ())), preferred_element_type=jnp.float32
    )
    updated = trailing - mask * products
    weighted = (mask * cotangent).astype(jnp.bfloat16)
    column_part = lax.dot_general(
        factor_rows, weighted, (((1,), (0,)), ((), ())), preferred_element_type=jnp.float32
    )
    column_total = lax.psum(column_part, "row")
    total = lax.dot_general(
        pieces, weighted, (((1,), (1,)), ((), ())), preferred_element_type=jnp.float32
    )
    k = 0
    offset = where_at[k] * BS
    current = lax.dynamic_slice_in_dim(total, offset, BS, 1)
    extra = jnp.where(inside[k], column_total, 0.0)
    total = lax.dynamic_update_slice_in_dim(total, current + extra, offset, 1)
    grad_piece = lax.psum_scatter(-total, "col", scatter_dimension=0, tiled=True).astype(
        jnp.bfloat16
    )
    kslice = inv_factor
    panel_grad = lax.dot_general(
        lax.all_gather(grad_piece, "col", axis=0, tiled=True),
        kslice,
        (((0,), (1,)), ((), ())),
        preferred_element_type=jnp.float32,
    )
    return (updated, panel_grad)


def solution(mesh):
    return jax.shard_map(
        on_device,
        mesh=mesh,
        in_specs=(P("row", "col"), P("col", None), P(), P(), P("row", "col"), P("row", "col")),
        out_specs=(P("row", "col"), P("row", "col")),
        check_vma=False,
    )
```

profile of v0, /device:TPU:1, one launch (start us, length us, event | category | flops | bytes accessed | tf_op | source)
XLA Modules:
  0.0 802.8 jit_solution(14721560447647710391)
XLA Ops:
  7.2 0.0 copy-start
  7.2 0.0 reduce-scatter.3.cloned.1.call-start
  7.2 1.2 copy-done
  8.4 5.4 fusion.11
  13.8 0.0 copy-start.4
  13.8 0.0 copy-start.2
  13.8 0.0 reduce-scatter.3.cloned.1.call-update
  13.8 0.0 all-gather.3.cloned.1.call-start
  13.9 229.1 %reduce-scatter.3.cloned.1.call-done = f32[128,512]{1,0:T(8,128)} async-done(((f32[4096,512]{1,0:T(8,128)}), f32[128,512]{1,0:T(8,128)}) %reduce-scatter.3.cloned.1.call-update) | async-done | bytes 262160 | tf_op jit(solution)/shard_map/reduce_scatter | solution.py:39
  243.0 1.6 convert_element_type.21
  244.6 0.0 all-gather.3.cloned.1.call-update
  244.6 0.0 all-reduce.3.cloned.1.call-start
  244.7 0.0 copy-done.4
  244.7 0.2 convert_reduce_fusion
  244.9 0.1 select_reduce_fusion
  245.0 0.6 dynamic_slice.13
  248.9 1.5 convolution_bitcast_fusion
  250.3 77.7 %all-gather.3.cloned.1.call-done = bf16[4096,512]{1,0:T(8,128)(2,1)} async-done(((bf16[128,512]{1,0:T(8,128)(2,1)}), bf16[4096,512]{1,0:T(8,128)(2,1)}) %all-gather.3.cloned.1.call-update) | async-done | bytes 4194320 | tf_op jit(solution)/shard_map/all_gather | solution.py:47
  328.0 2.5 dynamic-slice_select_fusion
  330.4 0.0 all-reduce.3.cloned.1.call-update
  330.5 0.0 all-reduce.5.cloned.1.call-start
  330.5 0.1 broadcast_bitcast_fusion
  330.6 0.0 copy-done.2
  330.6 4.9 fusion.9
  335.5 0.0 all-reduce.5.cloned.1.call-update
  335.5 0.0 reduce-scatter.5.cloned.1.call-start
  335.5 60.6 %all-reduce.3.cloned.1.call-done = bf16[4096,128]{1,0:T(8,128)(2,1)} async-done(((bf16[4096,128]{1,0:T(8,128)(2,1)}), bf16[4096,128]{1,0:T(8,128)(2,1)}) %all-reduce.3.cloned.1.call-update) | async-done | bytes 1048592 | tf_op jit(solution)/shard_map/psum | solution.py:12
  396.2 5.8 fusion.10
  402.0 66.8 %all-reduce.5.cloned.1.call-done = f32[4096,128]{1,0:T(8,128)} async-done(((f32[4096,128]{1,0:T(8,128)}), f32[4096,128]{1,0:T(8,128)}) %all-reduce.5.cloned.1.call-update) | async-done | bytes 2097168 | tf_op jit(solution)/shard_map/psum | solution.py:67
  468.8 3.2 add_dynamic-update-slice_fusion
  472.0 7.6 neg.3
  479.6 0.0 copy-start.1
  479.6 0.0 copy-start.3
  479.6 0.0 reduce-scatter.5.cloned.1.call-update
  479.7 0.0 all-gather.5.cloned.1.call-start
  479.7 227.6 %reduce-scatter.5.cloned.1.call-done = f32[128,512]{1,0:T(8,128)} async-done(((f32[4096,512]{1,0:T(8,128)}), f32[128,512]{1,0:T(8,128)}) %reduce-scatter.5.cloned.1.call-update) | async-done | bytes 262160 | tf_op jit(solution)/shard_map/reduce_scatter | solution.py:76
  707.3 1.6 convert_element_type.23
  708.9 0.0 all-gather.5.cloned.1.call-update
  708.9 0.0 copy-done.1
  709.0 0.0 copy-done.3
  709.0 4.2 fusion
  713.1 78.6 %all-gather.5.cloned.1.call-done = bf16[4096,512]{1,0:T(8,128)(2,1)} async-done(((bf16[128,512]{1,0:T(8,128)(2,1)}), bf16[4096,512]{1,0:T(8,128)(2,1)}) %all-gather.5.cloned.1.call-update) | async-done | bytes 4194320 | tf_op jit(solution)/shard_map/all_gather | solution.py:81
  791.7 4.2 fusion.12
  (1 shorter events, 0.0 us)
Async XLA Ops:
  7.2 1.2 copy-start
  7.2 235.8 %reduce-scatter.3.cloned.1.call-start = ((), (), s32[]{:S(2)}) async-start(), calls=%async_computation.2 | async-start | bytes 8650752 | tf_op jit(solution)/shard_map/reduce_scatter | solution.py:39
  13.8 230.9 %copy-start.4 = (s32[32]{0:T(128)S(1)}, s32[32]{0:T(128)}, u32[]{:S(2)}) copy-start(s32[32]{0:T(128)} %param.9) | copy-start | bytes 388
  13.8 316.8 %copy-start.2 = (f32[512,128]{1,0:T(8,128)S(1)}, f32[512,128]{1,0:T(8,128)}, u32[]{:S(2)}) copy-start(f32[512,128]{1,0:T(8,128)} %param.11) | copy-start | bytes 786436
  13.8 314.1 %all-gather.3.cloned.1.call-start = ((), (), s32[]{:S(2)}) async-start(), calls=%async_computation.3 | async-start | bytes 4325376 | tf_op jit(solution)/shard_map/all_gather | solution.py:47
  244.6 151.5 %all-reduce.3.cloned.1.call-start = ((), (), s32[]{:S(2)}) async-start(), calls=%async_computation.4 | async-start | bytes 2097152 | tf_op jit(solution)/shard_map/psum | solution.py:12
  330.5 138.4 %all-reduce.5.cloned.1.call-start = ((), (), s32[]{:S(2)}) async-start(), calls=%async_computation.5 | async-start | bytes 4194304 | tf_op jit(solution)/shard_map/psum | solution.py:67
  335.5 371.8 %reduce-scatter.5.cloned.1.call-start = ((), (), s32[]{:S(2)}) async-start(), calls=%async_computation.6 | async-start | bytes 8650752 | tf_op jit(solution)/shard_map/reduce_scatter | solution.py:76
  479.6 229.3 %copy-start.1 = (bf16[4096,128]{1,0:T(8,128)(2,1)S(1)}, bf16[4096,128]{1,0:T(8,128)(2,1)}, u32[]{:S(2)}) copy-start(bf16[4096,128]{1,0:T(8,128)(2,1)} %all-reduce.3.cloned.1.call-done) | copy-start | bytes 3145732
  479.6 229.3 %copy-start.3 = (f32[512,128]{1,0:T(8,128)S(1)}, f32[512,128]{1,0:T(8,128)}, u32[]{:S(2)}) copy-start(f32[512,128]{1,0:T(8,128)} %param.10) | copy-start | bytes 786436
  479.7 312.1 %all-gather.5.cloned.1.call-start = ((), (), s32[]{:S(2)}) async-start(), calls=%async_computation.7 | async-start | bytes 4325376 | tf_op jit(solution)/shard_map/all_gather | solution.py:81
Sparse Core Ops, SparseCore 0:
  14.0 228.9 reduce-scatter.2
  246.5 81.4 all-gather.2
  330.6 65.5 all-reduce.2
  398.5 70.2 all-reduce.4
  479.8 227.4 reduce-scatter.4
  710.3 81.3 all-gather.4
where the time goes:
time: 805 us; the launch traced here: 803 us
  waiting for transfers between devices  741 us (92%)
  matrix products  25.9 us (3%)
  between operations  17.4 us (2%)
  other arithmetic  16.8 us (2%)
    reduce_scatter x1, waiting for transfers between devices, on_device(): lax.psum_scatter(lax.dot_general(kslice, panel, (((0,), (1,)), ((), ())),...  229 us
    reduce_scatter x1, waiting for transfers between devices, on_device(): lax.psum_scatter(-total, 'col', scatter_dimension=0, tiled=True)  228 us
    all_gather x1, waiting for transfers between devices, on_device(): lax.all_gather(grad_piece, 'col', axis=0, tiled=True)  78.6 us
    all_gather x1, waiting for transfers between devices, on_device(): factor_rows = lax.all_gather(factor_piece, 'col', axis=0, tiled=True)  77.7 us
    psum x1, waiting for transfers between devices, on_device(): column_total = lax.psum(column_part, 'row')  66.8 us
    psum x1, waiting for transfers between devices, spread(): return lax.psum(kept, axis)  60.6 us
  transfers between devices with their start and end apart: 6, of which 6 were waited for; matrix products, arithmetic and copies ran while one was open for 2% of the time, Pallas kernels for 0%

commit v1 on v0

v1 whole, which is shorter than its diff:
```python
import jax
import jax.numpy as jnp
from jax import lax
from jax.experimental import pallas as pl
from jax.experimental.pallas import tpu as pltpu
from jax.sharding import PartitionSpec as P

BS = 128
NZ = 8
NX = 4
NR = 8
NS = 32
ROWS = 512
BF = jnp.bfloat16
F32 = jnp.float32
X_GROUPS = [[z * NX + x for x in range(NX)] for z in range(NZ)]
Z_GROUPS = [[z * NX + x for z in range(NZ)] for x in range(NX)]
VMEM = pl.BlockSpec(memory_space=pltpu.VMEM)
SMEM = pl.BlockSpec(memory_space=pltpu.SMEM)


def call(kernel, out_shape, in_specs, flops, nbytes):
    many = isinstance(out_shape, (tuple, list))
    return pl.pallas_call(
        kernel,
        out_shape=out_shape,
        in_specs=in_specs,
        out_specs=[VMEM] * len(out_shape) if many else VMEM,
        compiler_params=pltpu.CompilerParams(vmem_limit_bytes=40 * 1024 * 1024),
        cost_estimate=pl.CostEstimate(flops=flops, bytes_accessed=nbytes, transcendentals=0),
    )


def exchange_x(value):
    return lax.all_to_all(value, "col", 0, 0, axis_index_groups=X_GROUPS)


def exchange_z(value):
    return lax.all_to_all(value, "col", 0, 0, axis_index_groups=Z_GROUPS)


def exchange_row(value):
    return lax.all_to_all(value, "row", 0, 0)


def factor_kernel(got_ref, out_ref):
    left = jnp.concatenate([got_ref[x, :ROWS, :] for x in range(NX)], axis=1)
    for z in range(0, NZ, 2):
        right = jnp.concatenate(
            [
                jnp.concatenate(
                    [got_ref[x, ROWS + (z + h) * BS : ROWS + (z + h + 1) * BS, :] for h in range(2)],
                    axis=1,
                )
                for x in range(NX)
            ],
            axis=0,
        )
        product = jnp.dot(left, right, preferred_element_type=F32).astype(BF)
        out_ref[z] = product[:, :BS]
        out_ref[z + 1] = product[:, BS:]


def pair_kernel(factor_ref, got_ref, owned_ref, out_ref):
    left = jnp.concatenate([factor_ref[z] for z in range(NZ)], axis=1)
    for x in range(NX):
        right = jnp.concatenate(
            [
                jnp.concatenate(
                    [got_ref[x, ROWS + z * BS : ROWS + (z + 1) * BS, :] for z in range(NZ)], axis=1
                ),
                jnp.concatenate([owned_ref[z, x] for z in range(NZ)], axis=1),
            ],
            axis=0,
        )
        product = lax.dot_general(
            left, right, (((1,), (1,)), ((), ())), preferred_element_type=F32
        ).astype(BF)
        out_ref[x, 0] = product[:, :BS]
        out_ref[x, 1] = product[:, BS:]


def column_kernel(perm_ref, weighted_ref, piece_ref, out_ref):
    piece = piece_ref[...]
    for s in range(0, NS, 2):
        left = jnp.concatenate([weighted_ref[s], weighted_ref[s + 1]], axis=1)
        product = lax.dot_general(
            left, piece, (((0,), (0,)), ((), ())), preferred_element_type=F32
        ).astype(BF)
        out_ref[perm_ref[s]] = product[:BS]
        out_ref[perm_ref[s + 1]] = product[BS:]


def own_kernel(perm_ref, weighted_ref, got_ref, out_ref):
    step = 4
    total = jnp.zeros((ROWS, BS), F32)
    for s in range(0, NS, step):
        left = jnp.concatenate([weighted_ref[s + h] for h in range(step)], axis=1)
        right = []
        for h in range(step):
            j = perm_ref[s + h]
            right.append(got_ref[j // 4, pl.ds(pl.multiple_of((j % 4) * BS, BS), BS), :])
        total += jnp.dot(left, jnp.concatenate(right, axis=0), preferred_element_type=F32)
    for r in range(NR):
        total += got_ref[r, ROWS:, :].astype(F32)
    out_ref[...] = -total


def on_device(panel, inv_factor, fill, owner, trailing, cotangent):
    col = lax.axis_index("col")
    row = lax.axis_index("row")
    index = jnp.arange(NS, dtype=jnp.int32)
    perm = jnp.sum(jnp.where(owner[None, :] == index[:, None], index[None, :], 0), axis=1)
    mine = lax.dynamic_slice_in_dim(perm, col, 1)
    fill_rows = lax.dynamic_slice_in_dim(fill, row * 4, 4, 0)
    block_mask = jnp.sum(jnp.where(index[None, :] == mine[None, :], fill_rows, 0), axis=1)
    mask = block_mask.astype(F32)[:, None, None]

    weighted = (mask * cotangent.reshape(4, BS, BS)).astype(BF).reshape(ROWS, BS)
    weighted_all = lax.all_gather(weighted, "col", axis=0)

    columns = inv_factor.reshape(BS, NZ, NX, BS).transpose(2, 1, 0, 3).reshape(NX, NZ * BS, BS)
    sent = jnp.concatenate([jnp.broadcast_to(panel[None], (NX, ROWS, BS)), columns], axis=1)
    got = exchange_x(sent)
    partial = call(
        factor_kernel, jax.ShapeDtypeStruct((NZ, ROWS, BS), BF), [VMEM], 2 * 512 * 512 * 1024, 3 << 20
    )(got)
    factor = jnp.sum(exchange_z(partial).astype(F32), axis=0).astype(BF)

    factor_k = exchange_z(jnp.broadcast_to(factor[None], (NZ, ROWS, BS)))
    factor_col = exchange_row(jnp.broadcast_to(factor[None], (NR, ROWS, BS)))
    picked = factor_col.reshape(NS, BS, BS)[perm].reshape(NZ, NX, BS, BS)
    owned = exchange_z(picked)
    pair = call(
        pair_kernel,
        jax.ShapeDtypeStruct((NX, 2, ROWS, BS), BF),
        [VMEM] * 3,
        2 * 512 * 1024 * 1024,
        5 << 20,
    )(factor_k, got, owned)
    pair_sum = jnp.sum(exchange_x(pair).astype(F32), axis=0)
    piece = pair_sum[0].astype(BF)
    updated = (
        trailing.reshape(4, BS, BS) - mask * pair_sum[1].reshape(4, BS, BS)
    ).reshape(ROWS, BS)

    column = call(
        column_kernel,
        jax.ShapeDtypeStruct((NS, BS, BS), BF),
        [SMEM, VMEM, VMEM],
        2 * 512 * 4096 * 128,
        6 << 20,
    )(perm, weighted_all, piece)
    last = exchange_row(
        jnp.concatenate(
            [jnp.broadcast_to(piece[None], (NR, ROWS, BS)), column.reshape(NR, ROWS, BS)], axis=1
        )
    )
    panel_grad = call(
        own_kernel,
        jax.ShapeDtypeStruct((ROWS, BS), F32),
        [SMEM, VMEM, VMEM],
        2 * 512 * 4096 * 128,
        7 << 20,
    )(perm, weighted_all, last)
    return updated, panel_grad


def solution(mesh):
    return jax.shard_map(
        on_device,
        mesh=mesh,
        in_specs=(P("row", "col"), P("col", None), P(), P(), P("row", "col"), P("row", "col")),
        out_specs=(P("row", "col"), P("row", "col")),
        check_vma=False,
    )
```

time: 805 us -> 300 us (0.37)
  waiting for transfers between devices: 741 us -> 114 us
  blocking collectives: 0 us -> 145 us
  matrix products: 25.9 us -> 0 us
  other arithmetic: 16.8 us -> 3.01 us
    reduce_scatter x2 -> x0, waiting for transfers between devices: 457 us -> none  [the longest x1 229 us: on_device(): lax.psum_scatter(lax.dot_general(kslice, panel, (((0,), (1,)), ((), ())),...]
    all_to_all x0 -> x5, blocking collectives: none -> 145 us  [the longest x2 63 us: exchange_z(): return lax.all_to_all(value, 'col', 0, 0, axis_index_groups=Z_GROUPS)]
    psum x2 -> x0, waiting for transfers between devices: 127 us -> none  [the longest x1 66.8 us: on_device(): column_total = lax.psum(column_part, 'row')]
    all_gather x2 -> x1, waiting for transfers between devices: 156 us -> 81.5 us  [on_device(): weighted_all = lax.all_gather(weighted, 'col', axis=0)]
    all_to_all x0 -> x2, waiting for transfers between devices: none -> 32.4 us  [the longest x1 23.9 us: exchange_z(): return lax.all_to_all(value, 'col', 0, 0, axis_index_groups=Z_GROUPS)]
    dot_general x6 -> x0, matrix products: 25.9 us -> none  [the longest x1 5.81 us: on_device(): lax.dot_general(pieces, weighted, (((1,), (1,)), ((), ())), preferred_ele...]
  transfers between devices with their start and end apart: 6 -> 3, of which waited for: 6 -> 3; matrix products, arithmetic and copies ran while one was open for 2% -> 2% of each run, Pallas kernels for 0% -> 0%
where the time goes in v1:
time: 300 us
  blocking collectives  145 us (48%)
  waiting for transfers between devices  114 us (38%)
  between operations  14.2 us (5%)
  local copies, waits for them, and re-layouts  9.34 us (3%)
  Pallas kernels  7.4 us (2%)
  starting transfers between devices  7.24 us (2%)
  other arithmetic  3.01 us (1%)
    all_gather x1, waiting for transfers between devices, on_device(): weighted_all = lax.all_gather(weighted, 'col', axis=0)  81.5 us
    all_to_all x2, blocking collectives, exchange_z(): return lax.all_to_all(value, 'col', 0, 0, axis_index_groups=Z_GROUPS)  63 us
    all_to_all x2, blocking collectives, exchange_row(): return lax.all_to_all(value, 'row', 0, 0)  57.3 us
    all_to_all x1, blocking collectives, exchange_x(): return lax.all_to_all(value, 'col', 0, 0, axis_index_groups=X_GROUPS)  24.3 us
    all_to_all x1, waiting for transfers between devices, exchange_z(): return lax.all_to_all(value, 'col', 0, 0, axis_index_groups=Z_GROUPS)  23.9 us
    all_to_all x1, waiting for transfers between devices, exchange_x(): return lax.all_to_all(value, 'col', 0, 0, axis_index_groups=X_GROUPS)  8.54 us
  transfers between devices with their start and end apart: 3, of which 3 were waited for; matrix products, arithmetic and copies ran while one was open for 2% of the time, Pallas kernels for 0%

profile of v1, /device:TPU:1, one launch (start us, length us, event | category | flops | bytes accessed | tf_op | source)
XLA Modules:
  0.0 299.8 jit_solution(13930703635848074553)
XLA Ops:
  7.2 0.0 copy-start.4
  7.2 1.8 reshape.56
  9.0 0.4 copy.9
  9.4 0.0 copy-done.4
  9.4 0.1 broadcast_in_dim.36
  9.5 0.1 pad_maximum_fusion.1
  9.6 24.3 %all_to_all.35.got_ref = bf16[4,1536,128]{2,1,0:T(8,128)(2,1)S(1)} all-to-all(bf16[4,1536,128]{2,1,0:T(8,128)(2,1)S(1)} %pad_maximum_fusion.1), channel_id=1, replica_groups={{0,8,16,24},{32,40,48,56},{64,72,80,88},{96,104,112,120},{128,136,144,1..., dimensions={0} | all-to-all | bytes 3145728 | tf_op jit(solution)/shard_map/all_to_all | solution.py:35
  34.0 0.7 shard_map.77
  34.7 33.9 %all_to_all.36 = bf16[8,512,128]{2,1,0:T(8,128)(2,1)S(1)} all-to-all(bf16[8,512,128]{2,1,0:T(8,128)(2,1)S(1)} %shard_map.77), channel_id=1, replica_groups={{0,32,64,96,128,160,192,224},{8,40,72,104,136,168,200,232},{16,48,80,11..., dimensions={0} | all-to-all | bytes 2097152 | tf_op jit(solution)/shard_map/all_to_all | solution.py:39
  68.6 0.1 reduce_sum.43
  68.8 0.1 broadcast_in_dim.37
  68.9 0.0 copy-start.1
  68.9 1.0 copy-done.1
  69.9 0.0 copy-start.5
  69.9 23.4 %all_to_all.37 = bf16[8,512,128]{2,1,0:T(8,128)(2,1)} all-to-all(bf16[8,512,128]{2,1,0:T(8,128)(2,1)S(1)} %broadcast_in_dim.37), channel_id=1, replica_groups=mesh['col'=32,'row'=8] {'row'}, dimensions={0} | all-to-all | bytes 2097152 | tf_op jit(solution)/shard_map/all_to_all | solution.py:43
  93.3 3.6 %all-to-all-start.2 = ((bf16[8,512,128]{2,1,0:T(8,128)(2,1)}), bf16[8,512,128]{2,1,0:T(8,128)(2,1)S(1)}, u32[]{:S(2)}, u32[]{:S(2)}) async-start(bf16[8,512,128]{2,1,0:T(8,128)(2,1)} %copy-done.1), calls=%async_computation.2 | async-start | bytes 2097152 | tf_op jit(solution)/shard_map/all_to_all | solution.py:39
  96.8 0.0 copy-done.5
  96.9 0.1 select_reduce_fusion.perm_ref
  97.0 2.9 gather_fusion
  99.9 23.9 %all-to-all-done.2.factor_ref = bf16[8,512,128]{2,1,0:T(8,128)(2,1)S(1)} async-done(((bf16[8,512,128]{2,1,0:T(8,128)(2,1)}), bf16[8,512,128]{2,1,0:T(8,128)(2,1)S(1)}, u32[]{:S(2)}, u32[]{:S(2)}) %all-to-all-start.2) | async-done | bytes 1048608 | tf_op jit(solution)/shard_map/all_to_all | solution.py:39
  123.8 29.1 %all_to_all.38.owned_ref = bf16[8,4,128,128]{3,2,1,0:T(8,128)(2,1)S(1)} all-to-all(bf16[8,4,128,128]{3,2,1,0:T(8,128)(2,1)} %bitcast.27), channel_id=1, replica_groups={{0,32,64,96,128,160,192,224},{8,40,72,104,136,168,200,232},{16,48,80,11..., dimensions={0} | all-to-all | bytes 2097152 | tf_op jit(solution)/shard_map/all_to_all | solution.py:39
  152.9 2.3 shard_map.78
  155.1 0.0 copy-start.2
  155.1 0.0 copy-start.3
  155.1 3.6 %all-to-all-start.5 = ((bf16[4,2,512,128]{3,2,1,0:T(8,128)(2,1)}), bf16[4,2,512,128]{3,2,1,0:T(8,128)(2,1)S(1)}, u32[]{:S(2)}, u32[]{:S(2)}) async-start(bf16[4,2,512,128]{3,2,1,0:T(8,128)(2,1)} %shard_map.78), calls=%async_computation.5 | async-start | bytes 2097152 | tf_op jit(solution)/shard_map/all_to_all | solution.py:35
  158.8 0.0 all-gather.3.cloned.1.call-start
  158.9 0.6 dynamic_slice.6
  159.4 0.6 iota_compare_fusion.1
  160.1 0.8 select_reduce_fusion.1
  160.9 0.1 broadcast_bitcast_fusion
  161.0 8.5 %all-to-all-done.5 = bf16[4,2,512,128]{3,2,1,0:T(8,128)(2,1)S(1)} async-done(((bf16[4,2,512,128]{3,2,1,0:T(8,128)(2,1)}), bf16[4,2,512,128]{3,2,1,0:T(8,128)(2,1)S(1)}, u32[]{:S(2)}, u32[]{:S(2)}) %all-to-all-start.5) | async-done | bytes 1048608 | tf_op jit(solution)/shard_map/all_to_all | solution.py:35
  169.5 0.1 convert_reduce_fusion
  169.7 0.0 copy-done.2
  169.7 0.0 copy-done.3
  169.7 0.9 multiply_convert_fusion
  170.6 0.0 all-gather.3.cloned.1.call-update
  170.6 81.5 %all-gather.3.cloned.1.call-done = bf16[16384,128]{1,0:T(8,128)(2,1)} async-done(((bf16[512,128]{1,0:T(8,128)(2,1)}), bf16[16384,128]{1,0:T(8,128)(2,1)}) %all-gather.3.cloned.1.call-update) | async-done | bytes 4194320 | tf_op jit(solution)/shard_map/all_gather | solution.py:120
  252.1 0.0 copy-start
  252.1 2.2 copy-done
  254.3 1.9 shard_map.79
  256.2 0.1 broadcast_in_dim.62
  256.3 0.1 pad_maximum_fusion
  256.5 33.9 %all_to_all.39.got_ref = bf16[8,1024,128]{2,1,0:T(8,128)(2,1)S(1)} all-to-all(bf16[8,1024,128]{2,1,0:T(8,128)(2,1)S(1)} %pad_maximum_fusion), channel_id=1, replica_groups=mesh['col'=32,'row'=8] {'row'}, dimensions={0} | all-to-all | bytes 4194304 | tf_op jit(solution)/shard_map/all_to_all | solution.py:43
  290.3 2.6 shard_map.80
  (4 shorter events, 0.0 us)
Async XLA Ops:
  7.2 2.3 copy-start.4
  68.9 1.0 copy-start.1
  69.9 27.0 %copy-start.5 = (s32[32]{0:T(128)S(1)}, s32[32]{0:T(128)}, u32[]{:S(2)}) copy-start(s32[32]{0:T(128)} %param.9) | copy-start | bytes 388
  93.3 30.5 %all-to-all-start.2 = ((bf16[8,512,128]{2,1,0:T(8,128)(2,1)}), bf16[8,512,128]{2,1,0:T(8,128)(2,1)S(1)}, u32[]{:S(2)}, u32[]{:S(2)}) async-start(bf16[8,512,128]{2,1,0:T(8,128)(2,1)} %copy-done.1), calls=%async_computation.2 | async-start | bytes 2097152 | tf_op jit(solution)/shard_map/all_to_all | solution.py:39
  155.1 14.5 %copy-start.2 = (f32[512,128]{1,0:T(8,128)S(1)}, f32[512,128]{1,0:T(8,128)}, u32[]{:S(2)}) copy-start(f32[512,128]{1,0:T(8,128)} %param.11) | copy-start | bytes 786436
  155.1 14.5 %copy-start.3 = (f32[512,128]{1,0:T(8,128)S(1)}, f32[512,128]{1,0:T(8,128)}, u32[]{:S(2)}) copy-start(f32[512,128]{1,0:T(8,128)} %param.10) | copy-start | bytes 786436
  155.1 14.4 %all-to-all-start.5 = ((bf16[4,2,512,128]{3,2,1,0:T(8,128)(2,1)}), bf16[4,2,512,128]{3,2,1,0:T(8,128)(2,1)S(1)}, u32[]{:S(2)}, u32[]{:S(2)}) async-start(bf16[4,2,512,128]{3,2,1,0:T(8,128)(2,1)} %shard_map.78), calls=%async_computation.5 | async-start | bytes 2097152 | tf_op jit(solution)/shard_map/all_to_all | solution.py:35
  158.8 93.3 %all-gather.3.cloned.1.call-start = ((), (), s32[]{:S(2)}) async-start(), calls=%async_computation.7 | async-start | bytes 4325376 | tf_op jit(solution)/shard_map/all_gather | solution.py:120
  252.1 2.2 copy-start
Sparse Core Ops, SparseCore 0:
  170.7 81.3 all-gather.2

commit v2 on v1

--- a/solution.py
+++ b/solution.py
@@ -117,11 +117,12 @@
     mask = block_mask.astype(F32)[:, None, None]
 
     weighted = (mask * cotangent.reshape(4, BS, BS)).astype(BF).reshape(ROWS, BS)
-    weighted_all = lax.all_gather(weighted, "col", axis=0)
 
     columns = inv_factor.reshape(BS, NZ, NX, BS).transpose(2, 1, 0, 3).reshape(NX, NZ * BS, BS)
     sent = jnp.concatenate([jnp.broadcast_to(panel[None], (NX, ROWS, BS)), columns], axis=1)
+    sent, weighted = lax.optimization_barrier((sent, weighted))
     got = exchange_x(sent)
+    weighted_all = lax.all_gather(weighted, "col", axis=0)
     partial = call(
         factor_kernel, jax.ShapeDtypeStruct((NZ, ROWS, BS), BF), [VMEM], 2 * 512 * 512 * 1024, 3 << 20
     )(got)

time: 300 us -> 234 us (0.78)
  waiting for transfers between devices: 114 us -> 72 us
  blocking collectives: 145 us -> 107 us
  starting transfers between devices: 7.24 us -> 16 us
  other arithmetic: 3.01 us -> 6.26 us
    all_gather x1, waiting for transfers between devices: 81.5 us -> 0.02 us  [on_device(): weighted_all = lax.all_gather(weighted, 'col', axis=0)]
    all_to_all x2 -> x1, blocking collectives: 57.3 us -> 22.6 us  [exchange_row(): return lax.all_to_all(value, 'row', 0, 0)]
    all_to_all x0 -> x1, waiting for transfers between devices: none -> 25.5 us  [exchange_row(): return lax.all_to_all(value, 'row', 0, 0)]
    all_to_all x1, waiting for transfers between devices: 8.54 us -> 18.1 us  [exchange_x(): return lax.all_to_all(value, 'col', 0, 0, axis_index_groups=X_GROUPS)]
    all_to_all x1, blocking collectives: 24.3 us -> 15.6 us  [exchange_x(): return lax.all_to_all(value, 'col', 0, 0, axis_index_groups=X_GROUPS)]
    all_to_all x0 -> x1, starting transfers between devices: none -> 7.57 us  [exchange_row(): return lax.all_to_all(value, 'row', 0, 0)]
    all_to_all x2, blocking collectives: 63 us -> 68.6 us  [exchange_z(): return lax.all_to_all(value, 'col', 0, 0, axis_index_groups=Z_GROUPS)]
    all_to_all x1, waiting for transfers between devices: 23.9 us -> 27.6 us  [exchange_z(): return lax.all_to_all(value, 'col', 0, 0, axis_index_groups=Z_GROUPS)]
  transfers between devices with their start and end apart: 3 -> 4, of which waited for: 3 -> 3; matrix products, arithmetic and copies ran while one was open for 2% -> 2% of each run, Pallas kernels for 0% -> 1%
where the time goes in v2:
time: 234 us; the launch traced here: 233 us
  blocking collectives  107 us (46%)
  waiting for transfers between devices  72 us (31%)
  starting transfers between devices  16 us (7%)
  between operations  14.2 us (6%)
  local copies, waits for them, and re-layouts  11.5 us (5%)
  Pallas kernels  6.41 us (3%)
  other arithmetic  6.26 us (3%)
    all_to_all x2, blocking collectives, exchange_z(): return lax.all_to_all(value, 'col', 0, 0, axis_index_groups=Z_GROUPS)  68.6 us
    all_to_all x1, waiting for transfers between devices, exchange_z(): return lax.all_to_all(value, 'col', 0, 0, axis_index_groups=Z_GROUPS)  27.6 us
    all_to_all x1, waiting for transfers between devices, exchange_row(): return lax.all_to_all(value, 'row', 0, 0)  25.5 us
    all_to_all x1, blocking collectives, exchange_row(): return lax.all_to_all(value, 'row', 0, 0)  22.6 us
    all_to_all x1, waiting for transfers between devices, exchange_x(): return lax.all_to_all(value, 'col', 0, 0, axis_index_groups=X_GROUPS)  18.1 us
    all_to_all x1, blocking collectives, exchange_x(): return lax.all_to_all(value, 'col', 0, 0, axis_index_groups=X_GROUPS)  15.6 us
    all_to_all x1, starting transfers between devices, exchange_row(): return lax.all_to_all(value, 'row', 0, 0)  7.57 us
    unnamed x14, local copies, waits for them, and re-layouts  5.36 us
  transfers between devices with their start and end apart: 4, of which 3 were waited for; matrix products, arithmetic and copies ran while one was open for 2% of the time, Pallas kernels for 1%

profile of v2, /device:TPU:1, one launch (start us, length us, event | category | flops | bytes accessed | tf_op | source)
XLA Modules:
  0.0 233.1 jit_solution(11297388339234353212)
XLA Ops:
  7.2 0.0 copy-start.6
  7.2 0.0 copy-start.5
  7.2 1.8 reshape.54
  9.0 0.4 copy.9
  9.4 0.0 copy-done.6
  9.4 0.0 copy-start.4
  9.5 0.1 select_reduce_fusion.perm_ref
  9.6 0.6 dynamic_slice.6
  10.2 0.6 iota_compare_fusion.1
  10.8 0.8 select_reduce_fusion.1
  11.6 0.1 broadcast_bitcast_fusion
  11.7 0.0 copy-done.5
  11.7 0.1 broadcast_in_dim.36
  11.8 1.3 pad_maximum_fusion.1
  13.1 0.0 copy-done.4
  13.1 0.8 multiply_convert_fusion
  13.9 4.8 %all-to-all-start = ((bf16[4,1536,128]{2,1,0:T(8,128)(2,1)}), bf16[4,1536,128]{2,1,0:T(8,128)(2,1)S(1)}, u32[]{:S(2)}, u32[]{:S(2)}) async-start(bf16[4,1536,128]{2,1,0:T(8,128)(2,1)} %pad_maximum_fusion.1), calls=%async_computation | async-start | bytes 3145728 | tf_op jit(solution)/shard_map/all_to_all | solution.py:35
  18.7 0.0 all-gather.3.cloned.1.call-start
  18.7 0.7 all-gather.3.cloned.1.call-update
  19.4 18.1 %all-to-all-done.got_ref = bf16[4,1536,128]{2,1,0:T(8,128)(2,1)S(1)} async-done(((bf16[4,1536,128]{2,1,0:T(8,128)(2,1)}), bf16[4,1536,128]{2,1,0:T(8,128)(2,1)S(1)}, u32[]{:S(2)}, u32[]{:S(2)}) %all-to-all-start) | async-done | bytes 1572896 | tf_op jit(solution)/shard_map/all_to_all | solution.py:35
  37.5 0.7 shard_map.77
  38.2 37.9 %all_to_all.35 = bf16[8,512,128]{2,1,0:T(8,128)(2,1)S(1)} all-to-all(bf16[8,512,128]{2,1,0:T(8,128)(2,1)S(1)} %shard_map.77), channel_id=1, replica_groups={{0,32,64,96,128,160,192,224},{8,40,72,104,136,168,200,232},{16,48,80,11..., dimensions={0} | all-to-all | bytes 2097152 | tf_op jit(solution)/shard_map/all_to_all | solution.py:39
  76.2 0.1 reduce_sum.43
  76.3 0.1 broadcast_in_dim.37
  76.5 0.0 copy-start.2
  76.5 1.0 copy-done.2
  77.5 22.6 %all_to_all.36 = bf16[8,512,128]{2,1,0:T(8,128)(2,1)} all-to-all(bf16[8,512,128]{2,1,0:T(8,128)(2,1)S(1)} %broadcast_in_dim.37), channel_id=1, replica_groups=mesh['col'=32,'row'=8] {'row'}, dimensions={0} | all-to-all | bytes 2097152 | tf_op jit(solution)/shard_map/all_to_all | solution.py:43
  100.0 3.6 %all-to-all-start.2 = ((bf16[8,512,128]{2,1,0:T(8,128)(2,1)}), bf16[8,512,128]{2,1,0:T(8,128)(2,1)S(1)}, u32[]{:S(2)}, u32[]{:S(2)}) async-start(bf16[8,512,128]{2,1,0:T(8,128)(2,1)} %copy-done.2), calls=%async_computation.2 | async-start | bytes 2097152 | tf_op jit(solution)/shard_map/all_to_all | solution.py:39
  103.6 2.9 %gather_fusion = bf16[32,128,128]{2,1,0:T(8,128)(2,1)} fusion(bf16[32,128,128]{2,1,0:T(8,128)(2,1)} %bitcast.26, s32[1024]{0:T(1024)S(1)} %pad_clamp_fusion), kind=kCustom, calls=%fused_computation | custom fusion | bytes 2097280 | tf_op jit(solution)/shard_map/gather | solution.py:133
  106.5 27.6 %all-to-all-done.2.factor_ref = bf16[8,512,128]{2,1,0:T(8,128)(2,1)S(1)} async-done(((bf16[8,512,128]{2,1,0:T(8,128)(2,1)}), bf16[8,512,128]{2,1,0:T(8,128)(2,1)S(1)}, u32[]{:S(2)}, u32[]{:S(2)}) %all-to-all-start.2) | async-done | bytes 1048608 | tf_op jit(solution)/shard_map/all_to_all | solution.py:39
  134.2 30.7 %all_to_all.37.owned_ref = bf16[8,4,128,128]{3,2,1,0:T(8,128)(2,1)S(1)} all-to-all(bf16[8,4,128,128]{3,2,1,0:T(8,128)(2,1)} %bitcast.27), channel_id=1, replica_groups={{0,32,64,96,128,160,192,224},{8,40,72,104,136,168,200,232},{16,48,80,11..., dimensions={0} | all-to-all | bytes 2097152 | tf_op jit(solution)/shard_map/all_to_all | solution.py:39
  164.8 1.3 shard_map.78
  166.1 15.6 %all_to_all.38 = bf16[4,2,512,128]{3,2,1,0:T(8,128)(2,1)S(1)} all-to-all(bf16[4,2,512,128]{3,2,1,0:T(8,128)(2,1)S(1)} %shard_map.78), channel_id=1, replica_groups={{0,8,16,24},{32,40,48,56},{64,72,80,88},{96,104,112,120},{128,136,144,1..., dimensions={0} | all-to-all | bytes 2097152 | tf_op jit(solution)/shard_map/all_to_all | solution.py:35
  181.7 0.1 convert_reduce_fusion
  181.9 0.0 all-gather.3.cloned.1.call-done
  181.9 0.0 copy-start
  181.9 2.2 copy-done
  184.1 1.9 shard_map.79
  186.0 0.1 broadcast_in_dim.62
  186.1 1.5 pad_maximum_fusion
  187.6 0.0 copy-start.3
  187.6 7.6 %all-to-all-start.6 = ((bf16[8,1024,128]{2,1,0:T(8,128)(2,1)}), bf16[8,1024,128]{2,1,0:T(8,128)(2,1)S(1)}, u32[]{:S(2)}, u32[]{:S(2)}) async-start(bf16[8,1024,128]{2,1,0:T(8,128)(2,1)} %pad_maximum_fusion), calls=%async_computation.6 | async-start | bytes 4194304 | tf_op jit(solution)/shard_map/all_to_all | solution.py:43
  195.1 0.0 copy-done.3
  195.1 0.8 fusion.1
  196.0 25.5 %all-to-all-done.6.got_ref = bf16[8,1024,128]{2,1,0:T(8,128)(2,1)S(1)} async-done(((bf16[8,1024,128]{2,1,0:T(8,128)(2,1)}), bf16[8,1024,128]{2,1,0:T(8,128)(2,1)S(1)}, u32[]{:S(2)}, u32[]{:S(2)}) %all-to-all-start.6) | async-done | bytes 2097184 | tf_op jit(solution)/shard_map/all_to_all | solution.py:43
  221.5 0.0 copy-start.1
  221.5 2.2 copy-done.1
  223.7 2.6 %shard_map.80 = f32[512,128]{1,0:T(8,128)} custom-call(s32[32]{0:T(128)S(1)} %select_reduce_fusion.perm_ref, bf16[32,512,128]{2,1,0:T(8,128)(2,1)S(1)} %bitcast.23, bf16[8,1024,128]{2,1,0:T(8,128)(2,1)S(1)} %all-to-all-done.6.got_ref), custom_call_target="tpu_custom_call" | custom-call | flops 536870912 | bytes 7340032 | tf_op jit(solution)/shard_map/pallas_call | solution.py:160
  (4 shorter events, 0.0 us)
Async XLA Ops:
  7.2 2.3 copy-start.6
  7.2 4.5 %copy-start.5 = (bf16[512,128]{1,0:T(8,128)(2,1)S(1)}, bf16[512,128]{1,0:T(8,128)(2,1)}, u32[]{:S(2)}) copy-start(bf16[512,128]{1,0:T(8,128)(2,1)} %param.6) | copy-start | bytes 393220
  9.4 3.6 %copy-start.4 = (f32[512,128]{1,0:T(8,128)S(1)}, f32[512,128]{1,0:T(8,128)}, u32[]{:S(2)}) copy-start(f32[512,128]{1,0:T(8,128)} %param.11) | copy-start | bytes 786436
  13.9 23.7 %all-to-all-start = ((bf16[4,1536,128]{2,1,0:T(8,128)(2,1)}), bf16[4,1536,128]{2,1,0:T(8,128)(2,1)S(1)}, u32[]{:S(2)}, u32[]{:S(2)}) async-start(bf16[4,1536,128]{2,1,0:T(8,128)(2,1)} %pad_maximum_fusion.1), calls=%async_computation | async-start | bytes 3145728 | tf_op jit(solution)/shard_map/all_to_all | solution.py:35
  18.7 163.2 %all-gather.3.cloned.1.call-start = ((), (), s32[]{:S(2)}) async-start(), calls=%async_computation.7 | async-start | bytes 4325376 | tf_op jit(solution)/shard_map/all_gather | solution.py:125
  76.5 1.0 copy-start.2
  100.0 34.2 %all-to-all-start.2 = ((bf16[8,512,128]{2,1,0:T(8,128)(2,1)}), bf16[8,512,128]{2,1,0:T(8,128)(2,1)S(1)}, u32[]{:S(2)}, u32[]{:S(2)}) async-start(bf16[8,512,128]{2,1,0:T(8,128)(2,1)} %copy-done.2), calls=%async_computation.2 | async-start | bytes 2097152 | tf_op jit(solution)/shard_map/all_to_all | solution.py:39
  181.9 2.2 copy-start
  187.6 7.6 %copy-start.3 = (f32[512,128]{1,0:T(8,128)S(1)}, f32[512,128]{1,0:T(8,128)}, u32[]{:S(2)}) copy-start(f32[512,128]{1,0:T(8,128)} %param.10) | copy-start | bytes 786436
  187.6 33.9 %all-to-all-start.6 = ((bf16[8,1024,128]{2,1,0:T(8,128)(2,1)}), bf16[8,1024,128]{2,1,0:T(8,128)(2,1)S(1)}, u32[]{:S(2)}, u32[]{:S(2)}) async-start(bf16[8,1024,128]{2,1,0:T(8,128)(2,1)} %pad_maximum_fusion), calls=%async_computation.6 | async-start | bytes 4194304 | tf_op jit(solution)/shard_map/all_to_all | solution.py:43
  221.5 2.2 copy-start.1
Sparse Core Ops, SparseCore 0:
  22.7 92.3 all-gather.2

commit v3 on v1

v3 whole, which is shorter than its diff:
```python
import jax
import jax.numpy as jnp
from jax import lax
from jax.experimental import pallas as pl
from jax.experimental.pallas import tpu as pltpu
from jax.sharding import PartitionSpec as P

BS = 128
NZ = 8
NX = 4
NY = 4
NS = 32
ROWS = 512
BF = jnp.bfloat16
F32 = jnp.float32
X_GROUPS = [[z * NX + x for x in range(NX)] for z in range(NZ)]
Z_GROUPS = [[z * NX + x for z in range(NZ)] for x in range(NX)]
VMEM = pl.BlockSpec(memory_space=pltpu.VMEM)
SMEM = pl.BlockSpec(memory_space=pltpu.SMEM)
TILE = jax.ShapeDtypeStruct((ROWS, BS), BF)
STACK = jax.ShapeDtypeStruct((NY, ROWS, BS), BF)


def call(kernel, out_shape, in_specs, flops, nbytes, vmem=24):
    many = isinstance(out_shape, (tuple, list))
    return pl.pallas_call(
        kernel,
        out_shape=out_shape,
        in_specs=in_specs,
        out_specs=[VMEM] * len(out_shape) if many else VMEM,
        compiler_params=pltpu.CompilerParams(vmem_limit_bytes=vmem * 1024 * 1024),
        cost_estimate=pl.CostEstimate(flops=flops, bytes_accessed=nbytes, transcendentals=0),
    )


def exchange_x(value):
    return lax.all_to_all(value, "col", 0, 0, axis_index_groups=X_GROUPS)


def exchange_z(value):
    return lax.all_to_all(value, "col", 0, 0, axis_index_groups=Z_GROUPS)


def shift_z(value, k):
    pairs = [(z * NX + x, (z + k) % NZ * NX + x) for z in range(NZ) for x in range(NX)]
    return lax.ppermute(value, "col", pairs)


def shift_x(value, k):
    pairs = [(z * NX + x, z * NX + (x + k) % NX) for z in range(NZ) for x in range(NX)]
    return lax.ppermute(value, "col", pairs)


def shift_y(value, k):
    pairs = [(y * 2 + c, (y + k) % NY * 2 + c) for y in range(NY) for c in range(2)]
    return lax.ppermute(value, "row", pairs)


def swap_core(value):
    return lax.ppermute(value, "row", [(r, r ^ 1) for r in range(2 * NY)])


def gather_y(value):
    return [value] + [shift_y(value, -k) for k in range(1, NY)]


def ring_z(value):
    up, down = [value], [value]
    half = value.shape[0] // 2
    for _ in range(3):
        up.append(shift_z(up[-1], 1))
        down.append(shift_z(down[-1], -1))
    last = jnp.concatenate([shift_z(up[-1][:half], 1), shift_z(down[-1][half:], -1)])
    return jnp.stack([value] + down[1:] + [last] + up[1:][::-1])


def factor_kernel(got_ref, out_ref):
    left = jnp.concatenate([got_ref[x, :ROWS, :] for x in range(NX)], axis=1)
    for z in range(0, NZ, 2):
        right = jnp.concatenate(
            [
                jnp.concatenate(
                    [got_ref[x, ROWS + (z + h) * BS : ROWS + (z + h + 1) * BS, :] for h in range(2)],
                    axis=1,
                )
                for x in range(NX)
            ],
            axis=0,
        )
        product = jnp.dot(left, right, preferred_element_type=F32).astype(BF)
        out_ref[z] = product[:, :BS]
        out_ref[z + 1] = product[:, BS:]


def sent_kernel(panel_ref, *refs):
    sent_ref = refs[-1]
    sent_ref[0, :ROWS, :] = panel_ref[...]
    for z in range(NZ):
        sent_ref[0, ROWS + z * BS : ROWS + (z + 1) * BS, :] = refs[z][...]


def weighted_kernel(at_ref, owner_ref, fill_ref, cotangent_ref, weighted_ref, perm_ref):
    for j in range(NS):
        perm_ref[owner_ref[j]] = j
    mine = perm_ref[at_ref[3]]
    for i in range(4):
        scale = fill_ref[at_ref[4] * 4 + i, mine].astype(F32)
        rows = slice(i * BS, (i + 1) * BS)
        weighted_ref[:, rows] = (scale * cotangent_ref[rows, :]).T.astype(BF)


def tail_kernel(at_ref, perm_ref, fill_ref, trailing_ref, got_ref, out_ref):
    mine = perm_ref[at_ref[3]]
    for i in range(4):
        scale = fill_ref[at_ref[4] * 4 + i, mine].astype(F32)
        rows = slice(i * BS, (i + 1) * BS)
        total = got_ref[0, rows, :].astype(F32)
        for x in range(1, NX):
            total += got_ref[x, rows, :].astype(F32)
        out_ref[rows, :] = trailing_ref[rows, :] - scale * total


def inner_kernel(at_ref, got_ref, factor_ref, *outs):
    right = jnp.concatenate([factor_ref[z] for z in range(NZ)], axis=1)
    for k in range(NX):
        x = lax.rem(at_ref[5] + k, NX)
        blocks = [got_ref[x, ROWS + z * BS : ROWS + (z + 1) * BS, :] for z in range(NZ)]
        left = jnp.concatenate(blocks, axis=1)
        product = lax.dot_general(
            left, right, (((1,), (1,)), ((), ())), preferred_element_type=F32
        )
        for i in range(4):
            outs[k][i] = product[:, i * BS : (i + 1) * BS].astype(outs[k].dtype)


def outer_kernel(at_ref, same_ref, other_ref, factor_ref, out_ref):
    left = jnp.concatenate([factor_ref[z] for z in range(NZ)], axis=1)
    for k, owned_ref in enumerate((same_ref, other_ref)):
        rows = []
        for h in range(2):
            blocks = [owned_ref[z, h] for z in range(NZ)]
            rows.append(jnp.concatenate(blocks, axis=1))
        right = jnp.concatenate(rows, axis=0)
        product = lax.dot_general(
            left, right, (((1,), (1,)), ((), ())), preferred_element_type=F32
        ).astype(BF)
        x = 2 * lax.rem(at_ref[2] + k, 2)
        out_ref[x] = product[:, :BS]
        out_ref[x + 1] = product[:, BS:]


def place(at_ref, j):
    y = lax.rem(j // 8 + NY - at_ref[1], NY)
    c = lax.rem(j // 4 + at_ref[2], 2)
    return c, y, j % 4


def pick_kernel(at_ref, perm_ref, both_ref, out_ref):
    for s in range(NS // 2):
        c, y, i = place(at_ref, perm_ref[s // 2 * NX + s % 2 + 2 * at_ref[2]])
        out_ref[s] = both_ref[c, y, i]


def quarters(at_ref, perm_ref, refs):
    own, one, two_a, two_b, three = refs
    for k, pair in enumerate(((own, own), (one, one), (two_a, two_b), (three, three))):
        for h in range(2):
            ref = pair[h]
            first = h * 4 if ref.shape[0] == NZ else 0
            places = []
            for d in range(4 * h, 4 * h + 4):
                z = lax.rem(at_ref[0] + d, NZ)
                x = lax.rem(at_ref[5] + k, NX)
                places.append(place(at_ref, perm_ref[z * NX + x]))
            yield places, ref[first : first + 4].reshape(4 * BS, ROWS)


def column_kernel(at_ref, perm_ref, *refs):
    piece_ref, out_ref = refs[5:]
    piece = jnp.concatenate([piece_ref[i] for i in range(4)], axis=1)
    for places, left in quarters(at_ref, perm_ref, refs[:5]):
        product = lax.dot_general(
            left, piece, (((1,), (1,)), ((), ())), preferred_element_type=F32
        ).astype(BF)
        for h, (c, y, i) in enumerate(places):
            out_ref[c, y, i] = product[h * BS : (h + 1) * BS]


def own_kernel(at_ref, perm_ref, *refs):
    both_ref, out_ref = refs[5:]
    total = jnp.zeros((BS, ROWS), F32)
    for places, right in quarters(at_ref, perm_ref, refs[:5]):
        left = jnp.concatenate([both_ref[c, y, i] for c, y, i in places], axis=1)
        total += jnp.dot(left, right, preferred_element_type=F32)
    out_ref[...] = total.T


def both_cores(pieces):
    same = jnp.stack(pieces).reshape(NY, 4, BS, BS)
    return jnp.stack([same, swap_core(same)])


def whole(shape):
    return pl.BlockSpec(shape, lambda g: (0,) * len(shape))


def sweep(kernel, out_shape, out_type, *args):
    return call(
        kernel,
        jax.ShapeDtypeStruct(out_shape, out_type),
        [SMEM] * 2 + [VMEM] * 6,
        2 * 512 * 4096 * 128,
        6 << 20,
        16,
    )(*args)


def on_device(panel, inv_factor, fill, owner, trailing, cotangent):
    col = lax.axis_index("col")
    row = lax.axis_index("row")
    at = jnp.stack([col // NX, row // 2, row % 2, col, row, col % NX]).astype(jnp.int32)
    sent = pl.pallas_call(
        sent_kernel,
        grid=(NX,),
        out_shape=jax.ShapeDtypeStruct((NX, ROWS + NZ * BS, BS), BF),
        in_specs=[whole((ROWS, BS))]
        + [pl.BlockSpec((BS, BS), lambda g, z=z: (0, z * NX + g)) for z in range(NZ)],
        out_specs=pl.BlockSpec((1, ROWS + NZ * BS, BS), lambda g: (g, 0, 0)),
        cost_estimate=pl.CostEstimate(flops=0, bytes_accessed=3 << 20, transcendentals=0),
    )(panel, *([inv_factor] * NZ))
    weighted, perm = pl.pallas_call(
        weighted_kernel,
        out_shape=[
            jax.ShapeDtypeStruct((BS, ROWS), BF),
            jax.ShapeDtypeStruct((NS,), jnp.int32),
        ],
        in_specs=[SMEM] * 3 + [VMEM],
        out_specs=[VMEM, SMEM],
        compiler_params=pltpu.CompilerParams(vmem_limit_bytes=16 * 1024 * 1024),
        cost_estimate=pl.CostEstimate(flops=0, bytes_accessed=1 << 19, transcendentals=0),
    )(at, owner, fill, cotangent)
    got, near = lax.optimization_barrier((exchange_x(sent), ring_z(weighted)))

    partial = call(
        factor_kernel, jax.ShapeDtypeStruct((NZ, ROWS, BS), BF), [VMEM], 2 * 512 * 512 * 1024, 3 << 20
    )(got)
    parts, one, three = lax.optimization_barrier(
        (exchange_z(partial), shift_x(near, -1), shift_x(near, 1))
    )
    factor = jnp.sum(parts.astype(F32), axis=0).astype(BF)
    two_a, two_b = shift_x(three[:4], 1), shift_x(one[4:], -1)

    factor_k = exchange_z(jnp.broadcast_to(factor[None], (NZ, ROWS, BS)))
    picked = call(
        pick_kernel, jax.ShapeDtypeStruct((NS // 2, BS, BS), BF), [SMEM] * 2 + [VMEM], 0, 2 << 20
    )(at, perm, both_cores(gather_y(factor))).reshape(NZ, 2, BS, BS)
    owned = exchange_z(picked)
    inner = call(
        inner_kernel,
        [jax.ShapeDtypeStruct((4, BS, BS), F32)] + [jax.ShapeDtypeStruct((4, BS, BS), BF)] * 3,
        [SMEM] + [VMEM] * 2,
        2 * 512 * 1024 * 512,
        4 << 20,
    )(at, got, factor_k)
    piece = inner[0]
    for k in range(1, NX):
        piece = piece + shift_x(inner[k], k).astype(F32)
    piece = piece.astype(BF)

    weights = (near, one, two_a, two_b, three)
    column = sweep(column_kernel, (2, NY, 4, BS, BS), BF, at, perm, *weights, piece)
    column, piece = lax.optimization_barrier((column, piece))
    column = column.reshape(2, NY, ROWS, BS)
    total = column[0].astype(F32) + swap_core(column[1]).astype(F32)
    moved = total[0]
    for k in range(1, NY):
        moved = moved + shift_y(total[k].astype(BF), k).astype(F32)
    both = both_cores(gather_y(piece))
    own = sweep(own_kernel, (ROWS, BS), F32, at, perm, *weights, both)

    owned, _ = lax.optimization_barrier((owned, column))
    owned_other = swap_core(owned)
    outer = call(outer_kernel, STACK, [SMEM] + [VMEM] * 3, 2 * 512 * 1024 * 512, 4 << 20)(
        at, owned, owned_other, factor_k
    )
    updated = call(
        tail_kernel, jax.ShapeDtypeStruct((ROWS, BS), F32), [SMEM] * 3 + [VMEM] * 2, 0, 1 << 20
    )(at, perm, fill, trailing, exchange_x(outer))
    return updated, -(own + moved)


def solution(mesh):
    return jax.shard_map(
        on_device,
        mesh=mesh,
        in_specs=(P("row", "col"), P("col", None), P(), P(), P("row", "col"), P("row", "col")),
        out_specs=(P("row", "col"), P("row", "col")),
        check_vma=False,
    )
```

time: 300 us -> 167 us (0.56)
  blocking collectives: 145 us -> 0 us
  starting transfers between devices: 7.24 us -> 70.2 us
  waiting for transfers between devices: 114 us -> 55.9 us
  between operations: 14.2 us -> 0.94 us
  Pallas kernels: 7.4 us -> 19.8 us
  other arithmetic: 3.01 us -> 7.84 us
    all_to_all x5 -> x0, blocking collectives: 145 us -> none  [the longest x2 63 us: exchange_z(): return lax.all_to_all(value, 'col', 0, 0, axis_index_groups=Z_GROUPS)]
    all_gather x1 -> x0, waiting for transfers between devices: 81.5 us -> none  [on_device(): weighted_all = lax.all_gather(weighted, 'col', axis=0)]
    ppermute x0 -> x28, starting transfers between devices: none -> 49.5 us  [the longest x4 15.9 us: swap_core(): return lax.ppermute(value, 'row', [(r, r ^ 1) for r in range(2 * NY)])]
    ppermute x0 -> x28, waiting for transfers between devices: none -> 41.4 us  [the longest x7 26 us: shift_x(): return lax.ppermute(value, 'col', pairs)]
    pallas_call x3 -> x8, Pallas kernels: 6.69 us -> 19.1 us  [the longest x2 5.51 us: sweep(): call(kernel, jax.ShapeDtypeStruct(out_shape, out_type), [SMEM] * 2 + [VME...]
    all_to_all x1 -> x3, waiting for transfers between devices: 23.9 us -> 13.1 us  [exchange_z(): return lax.all_to_all(value, 'col', 0, 0, axis_index_groups=Z_GROUPS)]
    all_to_all x1 -> x3, starting transfers between devices: 3.56 us -> 12 us  [exchange_z(): return lax.all_to_all(value, 'col', 0, 0, axis_index_groups=Z_GROUPS)]
    all_to_all x1 -> x2, waiting for transfers between devices: 8.54 us -> 1.39 us  [exchange_x(): return lax.all_to_all(value, 'col', 0, 0, axis_index_groups=X_GROUPS)]
  transfers between devices with their start and end apart: 3 -> 33, of which waited for: 3 -> 18; matrix products, arithmetic and copies ran while one was open for 2% -> 6% of each run, Pallas kernels for 0% -> 11%
where the time goes in v3:
time: 167 us; the launch traced here: 166 us
  starting transfers between devices  70.2 us (42%)
  waiting for transfers between devices  55.9 us (33%)
  Pallas kernels  19.8 us (12%)
  local copies, waits for them, and re-layouts  11.4 us (7%)
  other arithmetic  7.84 us (5%)
    ppermute x7, waiting for transfers between devices, shift_x(): return lax.ppermute(value, 'col', pairs)  26 us
    ppermute x4, starting transfers between devices, swap_core(): return lax.ppermute(value, 'row', [(r, r ^ 1) for r in range(2 * NY)])  15.9 us
    ppermute x8, starting transfers between devices, shift_z(): return lax.ppermute(value, 'col', pairs)  15.7 us
    all_to_all x3, waiting for transfers between devices, exchange_z(): return lax.all_to_all(value, 'col', 0, 0, axis_index_groups=Z_GROUPS)  13.1 us
    ppermute x9, starting transfers between devices, shift_y(): return lax.ppermute(value, 'row', pairs)  12.2 us
    all_to_all x3, starting transfers between devices, exchange_z(): return lax.all_to_all(value, 'col', 0, 0, axis_index_groups=Z_GROUPS)  12 us
    ppermute x8, waiting for transfers between devices, shift_z(): return lax.ppermute(value, 'col', pairs)  8.75 us
    all_to_all x2, starting transfers between devices, exchange_x(): return lax.all_to_all(value, 'col', 0, 0, axis_index_groups=X_GROUPS)  8.72 us
  transfers between devices with their start and end apart: 33, of which 18 were waited for; matrix products, arithmetic and copies ran while one was open for 6% of the time, Pallas kernels for 11%

profile of v3, /device:TPU:1, one launch (start us, length us, event | category | flops | bytes accessed | tf_op | source)
XLA Modules:
  0.0 166.1 jit_solution(14602004281971697970)
XLA Ops:
  0.8 1.0 copy-done.5
  1.7 0.7 copy-done.6
  2.4 0.7 copy-done.8
  3.1 1.4 shard_map.77
  4.5 6.5 %collective-permute-start = (bf16[128,512]{1,0:T(8,128)(2,1)S(1)}, bf16[128,512]{1,0:T(8,128)(2,1)S(1)}, u32[]{:S(2)}, u32[]{:S(2)}) collective-permute-start(bf16[128,512]{1,0:T(8,128)(2,1)S(1)} %get-tuple-element.16), channel_id=1, source_target_pairs={{0,224},{8,232},{16,240},{24,248},{32,0},{40,8},{48,16},{56,24},{6... | collective-permute-start | bytes 393224 | tf_op jit(solution)/shard_map/ppermute | solution.py:46
  11.0 3.7 %shard_map.78 = bf16[4,1536,128]{2,1,0:T(8,128)(2,1)} custom-call(bf16[512,128]{1,0:T(8,128)(2,1)} %panel_ref.1, bf16[128,4096]{1,0:T(8,128)(2,1)} %refs_7_.1, bf16[128,4096]{1,0:T(8,128)(2,1)} %refs_7_.1, bf16[128,4096]{1,0:T(8,128)(2,1)} %refs_7_.1, bf16[128,4096]{1,0:T(8,128)(2,1)} %refs_7_.1, bf16[128,4096]{1,0:T(8,128)(2,1)} %refs_7_.1, ...), custom_call_target="tpu_custom_call" | custom-call | bytes 3145728 | tf_op jit(solution)/shard_map/pallas_call | solution.py:222
  14.7 4.0 %all-to-all-start = ((bf16[4,1536,128]{2,1,0:T(8,128)(2,1)}), bf16[4,1536,128]{2,1,0:T(8,128)(2,1)S(1)}, u32[]{:S(2)}, u32[]{:S(2)}) async-start(bf16[4,1536,128]{2,1,0:T(8,128)(2,1)} %shard_map.78), calls=%async_computation | async-start | bytes 3145728 | tf_op jit(solution)/shard_map/all_to_all | solution.py:37
  18.7 2.7 %collective-permute-start.1 = (bf16[128,512]{1,0:T(8,128)(2,1)S(1)}, bf16[128,512]{1,0:T(8,128)(2,1)S(1)}, u32[]{:S(2)}, u32[]{:S(2)}) collective-permute-start(bf16[128,512]{1,0:T(8,128)(2,1)S(1)} %collective-permute-done), channel_id=1, source_target_pairs={{0,224},{8,232},{16,240},{24,248},{32,0},{40,8},{48,16},{56,24},{6... | collective-permute-start | bytes 393224 | tf_op jit(solution)/shard_map/ppermute | solution.py:46
  21.5 1.9 %collective-permute-done.1 = bf16[128,512]{1,0:T(8,128)(2,1)S(1)} collective-permute-done((bf16[128,512]{1,0:T(8,128)(2,1)S(1)}, bf16[128,512]{1,0:T(8,128)(2,1)S(1)}, u32[]{:S(2)}, u32[]{:S(2)}) %collective-permute-start.1) | collective-permute-done | bytes 131104 | tf_op jit(solution)/shard_map/ppermute | solution.py:46
  23.4 3.1 %collective-permute-start.2 = (bf16[128,512]{1,0:T(8,128)(2,1)S(1)}, bf16[128,512]{1,0:T(8,128)(2,1)S(1)}, u32[]{:S(2)}, u32[]{:S(2)}) collective-permute-start(bf16[128,512]{1,0:T(8,128)(2,1)S(1)} %collective-permute-done.1), channel_id=1, source_target_pairs={{0,224},{8,232},{16,240},{24,248},{32,0},{40,8},{48,16},{56,24},{6... | collective-permute-start | bytes 393224 | tf_op jit(solution)/shard_map/ppermute | solution.py:46
  26.5 0.3 collective-permute-done.4
  26.8 1.6 collective-permute-done.2
  28.4 3.4 %collective-permute-start.7 = (bf16[64,512]{1,0:T(8,128)(2,1)S(1)}, bf16[64,512]{1,0:T(8,128)(2,1)S(1)}, u32[]{:S(2)}, u32[]{:S(2)}) collective-permute-start(bf16[64,512]{1,0:T(8,128)(2,1)S(1)} %slice.46), channel_id=1, source_target_pairs={{0,224},{8,232},{16,240},{24,248},{32,0},{40,8},{48,16},{56,24},{6... | collective-permute-start | bytes 196616 | tf_op jit(solution)/shard_map/ppermute | solution.py:46
  31.8 0.3 collective-permute-done.5
  32.1 1.0 collective-permute-done.7
  33.1 3.6 %collective-permute-done.6 = bf16[64,512]{1,0:T(8,128)(2,1)S(1)} collective-permute-done((bf16[64,512]{1,0:T(8,128)(2,1)S(1)}, bf16[64,512]{1,0:T(8,128)(2,1)S(1)}, u32[]{:S(2)}, u32[]{:S(2)}) %collective-permute-start.6) | collective-permute-done | bytes 65568 | tf_op jit(solution)/shard_map/ppermute | solution.py:46
  36.8 1.4 all-to-all-done.got_ref
  38.2 0.7 shard_map.79
  38.9 1.0 copy-done.3
  39.9 4.2 %all-to-all-start.1 = ((bf16[8,512,128]{2,1,0:T(8,128)(2,1)}), bf16[8,512,128]{2,1,0:T(8,128)(2,1)}, u32[]{:S(2)}, u32[]{:S(2)}) async-start(bf16[8,512,128]{2,1,0:T(8,128)(2,1)} %copy-done.3), calls=%async_computation.1 | async-start | bytes 2097152 | tf_op jit(solution)/shard_map/all_to_all | solution.py:41
  44.2 1.5 collective-permute-start.8
  45.7 20.2 %collective-permute-done.8.refs_1_ = bf16[8,128,512]{2,1,0:T(8,128)(2,1)} collective-permute-done((bf16[8,128,512]{2,1,0:T(8,128)(2,1)S(1)}, bf16[8,128,512]{2,1,0:T(8,128)(2,1)}, u32[]{:S(2)}, u32[]{:S(2)}) %collective-permute-start.8) | collective-permute-done | bytes 1048608 | tf_op jit(solution)/shard_map/ppermute | solution.py:51
  65.9 0.7 collective-permute-done.9.refs_4_
  66.7 4.4 %all-to-all-done.1 = bf16[8,512,128]{2,1,0:T(8,128)(2,1)} async-done(((bf16[8,512,128]{2,1,0:T(8,128)(2,1)}), bf16[8,512,128]{2,1,0:T(8,128)(2,1)}, u32[]{:S(2)}, u32[]{:S(2)}) %all-to-all-start.1) | async-done | bytes 1048608 | tf_op jit(solution)/shard_map/all_to_all | solution.py:41
  71.1 1.4 reduce_sum.12
  72.5 1.1 broadcast_in_dim.2
  73.6 3.6 %all-to-all-start.3 = ((bf16[8,512,128]{2,1,0:T(8,128)(2,1)}), bf16[8,512,128]{2,1,0:T(8,128)(2,1)S(1)}, u32[]{:S(2)}, u32[]{:S(2)}) async-start(bf16[8,512,128]{2,1,0:T(8,128)(2,1)} %broadcast_in_dim.2), calls=%async_computation.3 | async-start | bytes 2097152 | tf_op jit(solution)/shard_map/all_to_all | solution.py:41
  77.1 1.4 collective-permute-start.12
  78.5 2.6 %collective-permute-start.11 = (bf16[512,128]{1,0:T(8,128)(2,1)S(1)}, bf16[512,128]{1,0:T(8,128)(2,1)S(1)}, u32[]{:S(2)}, u32[]{:S(2)}) collective-permute-start(bf16[512,128]{1,0:T(8,128)(2,1)S(1)} %reduce_sum.12), channel_id=1, source_target_pairs={{0,4},{1,5},{2,6},{3,7},{4,0},{5,1},{6,2},{7,3},{8,12},{9,13},{10,... | collective-permute-start | bytes 393224 | tf_op jit(solution)/shard_map/ppermute | solution.py:56
  81.1 1.1 collective-permute-start.10
  82.3 2.6 %collective-permute-done.11 = bf16[512,128]{1,0:T(8,128)(2,1)S(1)} collective-permute-done((bf16[512,128]{1,0:T(8,128)(2,1)S(1)}, bf16[512,128]{1,0:T(8,128)(2,1)S(1)}, u32[]{:S(2)}, u32[]{:S(2)}) %collective-permute-start.11) | collective-permute-done | bytes 131104 | tf_op jit(solution)/shard_map/ppermute | solution.py:56
  85.0 6.5 %collective-permute-start.13 = (bf16[4,4,128,128]{3,2,1,0:T(8,128)(2,1)S(1)}, bf16[4,4,128,128]{3,2,1,0:T(8,128)(2,1)S(1)}, u32[]{:S(2)}, u32[]{:S(2)}) collective-permute-start(bf16[4,4,128,128]{3,2,1,0:T(8,128)(2,1)S(1)} %pad_maximum_fusion.2), channel_id=1, source_target_pairs={{0,1},{1,0},{2,3},{3,2},{4,5},{5,4},{6,7},{7,6},{8,9},{9,8},{10,11... | collective-permute-start | bytes 1572872 | tf_op jit(solution)/shard_map/ppermute | solution.py:60
  91.5 1.5 collective-permute-done.13
  93.1 0.1 pad_maximum_fusion.both_ref
  93.2 1.6 shard_map.80
  94.8 7.5 %all-to-all-done.3.factor_ref = bf16[8,512,128]{2,1,0:T(8,128)(2,1)S(1)} async-done(((bf16[8,512,128]{2,1,0:T(8,128)(2,1)}), bf16[8,512,128]{2,1,0:T(8,128)(2,1)S(1)}, u32[]{:S(2)}, u32[]{:S(2)}) %all-to-all-start.3) | async-done | bytes 1048608 | tf_op jit(solution)/shard_map/all_to_all | solution.py:41
  102.3 4.2 %all-to-all-start.2 = ((bf16[8,2,128,128]{3,2,1,0:T(8,128)(2,1)}), bf16[8,2,128,128]{3,2,1,0:T(8,128)(2,1)}, u32[]{:S(2)}, u32[]{:S(2)}) async-start(bf16[8,2,128,128]{3,2,1,0:T(8,128)(2,1)} %bitcast.23), calls=%async_computation.2 | async-start | bytes 1048576 | tf_op jit(solution)/shard_map/all_to_all | solution.py:41
  106.5 1.9 %slice.37 = bf16[4,128,512]{2,1,0:T(8,128)(2,1)} slice(bf16[8,128,512]{2,1,0:T(8,128)(2,1)} %collective-permute-done.9.refs_4_), slice={[0:4], [0:128], [0:512]} | slice | bytes 1048576 | tf_op jit(solution)/shard_map/slice | solution.py:251
  108.4 1.9 %slice.38 = bf16[4,128,512]{2,1,0:T(8,128)(2,1)} slice(bf16[8,128,512]{2,1,0:T(8,128)(2,1)} %collective-permute-done.8.refs_1_), slice={[4:8], [0:128], [0:512]} | slice | bytes 1048576 | tf_op jit(solution)/shard_map/slice | solution.py:251
  110.2 2.7 %collective-permute-start.16 = (bf16[4,128,512]{2,1,0:T(8,128)(2,1)}, bf16[4,128,512]{2,1,0:T(8,128)(2,1)}, u32[]{:S(2)}, u32[]{:S(2)}) collective-permute-start(bf16[4,128,512]{2,1,0:T(8,128)(2,1)} %slice.38), channel_id=1, source_target_pairs={{0,24},{8,0},{16,8},{24,16},{32,56},{40,32},{48,40},{56,48},{64,88... | collective-permute-start | bytes 1572872 | tf_op jit(solution)/shard_map/ppermute | solution.py:51
  112.9 2.7 %shard_map.83 = (f32[4,128,128]{2,1,0:T(8,128)S(1)}, bf16[4,128,128]{2,1,0:T(8,128)(2,1)S(1)}, bf16[4,128,128]{2,1,0:T(8,128)(2,1)}, bf16[4,128,128]{2,1,0:T(8,128)(2,1)}) custom-call(s32[6]{0:T(128)S(1)} %stack.109.at_ref, bf16[4,1536,128]{2,1,0:T(8,128)(2,1)S(1)} %all-to-all-done.got_ref, bf16[8,512,128]{2,1,0:T(8,128)(2,1)S(1)} %all-to-all-done.3.factor_ref), custom_call_target="tpu_custom_call" | custom-call | flops 536870912 | bytes 4194304 | tf_op jit(solution)/shard_map/pallas_call | solution.py:258
  115.6 0.6 collective-permute-start.18
  116.2 0.9 collective-permute-start.17
  117.1 1.1 all-to-all-done.2.same_ref
  118.2 5.1 %collective-permute-done.19 = bf16[4,128,128]{2,1,0:T(8,128)(2,1)S(1)} collective-permute-done((bf16[4,128,128]{2,1,0:T(8,128)(2,1)}, bf16[4,128,128]{2,1,0:T(8,128)(2,1)S(1)}, u32[]{:S(2)}, u32[]{:S(2)}) %collective-permute-start.19) | collective-permute-done | bytes 131104 | tf_op jit(solution)/shard_map/ppermute | solution.py:51
  123.2 7.8 %collective-permute-start.14 = (bf16[8,2,128,128]{3,2,1,0:T(8,128)(2,1)}, bf16[8,2,128,128]{3,2,1,0:T(8,128)(2,1)S(1)}, u32[]{:S(2)}, u32[]{:S(2)}) collective-permute-start(bf16[8,2,128,128]{3,2,1,0:T(8,128)(2,1)} %all-to-all-done.2.same_ref), channel_id=1, source_target_pairs={{0,1},{1,0},{2,3},{3,2},{4,5},{5,4},{6,7},{7,6},{8,9},{9,8},{10,11... | collective-permute-start | bytes 1572872 | tf_op jit(solution)/shard_map/ppermute | solution.py:60
  131.1 1.2 copy-done.1
  132.3 3.0 %shard_map.84 = bf16[2,4,4,128,128]{4,3,2,1,0:T(8,128)(2,1)S(1)} custom-call(s32[6]{0:T(128)S(1)} %stack.109.at_ref, s32[32]{0:T(128)S(1)} %get-tuple-element.15.perm_ref, bf16[8,128,512]{2,1,0:T(8,128)(2,1)S(1)} %copy-done.1, bf16[8,128,512]{2,1,0:T(8,128)(2,1)} %collective-permute-done.8.refs_1_, bf16[4,128,512]{2,1,0:T(8,128)(2,1)S(1)} %collective-permute-done.15.refs_2_, ...), custom_call_target="tpu_custom_call" | custom-call | flops 536870912 | bytes 6291456 | tf_op jit(solution)/shard_map/pallas_call | solution.py:208
  135.3 1.1 fusion.8
  136.4 1.3 collective-permute-start.22
  137.7 2.6 %collective-permute-start.21 = (bf16[4,128,128]{2,1,0:T(8,128)(2,1)S(1)}, bf16[4,128,128]{2,1,0:T(8,128)(2,1)S(1)}, u32[]{:S(2)}, u32[]{:S(2)}) collective-permute-start(bf16[4,128,128]{2,1,0:T(8,128)(2,1)S(1)} %add_convert_fusion.refs_5_), channel_id=1, source_target_pairs={{0,4},{1,5},{2,6},{3,7},{4,0},{5,1},{6,2},{7,3},{8,12},{9,13},{10,... | collective-permute-start | bytes 393224 | tf_op jit(solution)/shard_map/ppermute | solution.py:56
  140.4 1.1 collective-permute-start.20
  141.4 2.6 %shard_map.81 = bf16[4,512,128]{2,1,0:T(8,128)(2,1)} custom-call(s32[6]{0:T(128)S(1)} %stack.109.at_ref, bf16[8,2,128,128]{3,2,1,0:T(8,128)(2,1)} %all-to-all-done.2.same_ref, bf16[8,2,128,128]{3,2,1,0:T(8,128)(2,1)S(1)} %collective-permute-done.14.other_ref, bf16[8,512,128]{2,1,0:T(8,128)(2,1)S(1)} %all-to-all-done.3.factor_ref), custom_call_target="tpu_custom_call" | custom-call | flops 536870912 | bytes 4194304 | tf_op jit(solution)/shard_map/pallas_call | solution.py:283
  144.1 4.7 %all-to-all-start.4 = ((bf16[4,512,128]{2,1,0:T(8,128)(2,1)}), bf16[4,512,128]{2,1,0:T(8,128)(2,1)S(1)}, u32[]{:S(2)}, u32[]{:S(2)}) async-start(bf16[4,512,128]{2,1,0:T(8,128)(2,1)} %shard_map.81), calls=%async_computation.4 | async-start | bytes 1048576 | tf_op jit(solution)/shard_map/all_to_all | solution.py:37
  148.8 1.1 fusion.7
  149.9 1.6 collective-permute-start.23
  151.5 2.2 %fusion.6 = (bf16[4,512,128]{2,1,0:T(8,128)(2,1)S(1)}, f32[4,512,128]{2,1,0:T(8,128)}) fusion(bf16[4,512,128]{2,1,0:T(8,128)(2,1)} %collective-permute-done.24, bf16[4,512,128]{2,1,0:T(8,128)(2,1)S(1)} %bitcast.63), kind=kLoop, calls=%fused_computation.24 | loop fusion | flops 1048576 | bytes 2621440 | tf_op jit(solution)/shard_map/convert.4
  153.7 0.7 slice_bitcast_fusion.3
  154.5 2.2 %collective-permute-start.26 = (bf16[512,128]{1,0:T(8,128)(2,1)}, bf16[512,128]{1,0:T(8,128)(2,1)S(1)}, u32[]{:S(2)}, u32[]{:S(2)}) collective-permute-start(bf16[512,128]{1,0:T(8,128)(2,1)} %get-tuple-element.34), channel_id=1, source_target_pairs={{0,4},{1,5},{2,6},{3,7},{4,0},{5,1},{6,2},{7,3},{8,12},{9,13},{10,... | collective-permute-start | bytes 393224 | tf_op jit(solution)/shard_map/ppermute | solution.py:56
  156.7 1.6 shard_map.82
  158.3 1.1 pad_maximum_fusion.1.refs_5_
  159.4 2.5 %shard_map.85 = f32[512,128]{1,0:T(8,128)S(1)} custom-call(s32[6]{0:T(128)S(1)} %stack.109.at_ref, s32[32]{0:T(128)S(1)} %get-tuple-element.15.perm_ref, bf16[8,128,512]{2,1,0:T(8,128)(2,1)S(1)} %copy-done.2, bf16[8,128,512]{2,1,0:T(8,128)(2,1)} %collective-permute-done.8.refs_1_, bf16[4,128,512]{2,1,0:T(8,128)(2,1)S(1)} %collective-permute-done.15.refs_2_, ...), custom_call_target="tpu_custom_call" | custom-call | flops 536870912 | bytes 6291456 | tf_op jit(solution)/shard_map/pallas_call | solution.py:208
  162.0 2.3 %collective-permute-done.25 = bf16[512,128]{1,0:T(8,128)(2,1)S(1)} collective-permute-done((bf16[512,128]{1,0:T(8,128)(2,1)S(1)}, bf16[512,128]{1,0:T(8,128)(2,1)S(1)}, u32[]{:S(2)}, u32[]{:S(2)}) %collective-permute-start.25) | collective-permute-done | bytes 131104 | tf_op jit(solution)/shard_map/ppermute | solution.py:56
  164.3 1.7 %fusion.4 = f32[512,128]{1,0:T(8,128)} fusion(f32[512,128]{1,0:T(8,128)S(1)} %shard_map.85, f32[4,512,128]{2,1,0:T(8,128)} %get-tuple-element.29, bf16[512,128]{1,0:T(8,128)(2,1)S(1)} %collective-permute-done.27, bf16[512,128]{1,0:T(8,128)(2,1)S(1)} %collective-permute-done.26, bf16[512,128]{1,0:T(8,128)(2,1)S(1)} %collective-permute-done.25), kind=kLoop, calls=%fused_computation.10 | loop fusion | flops 524288 | bytes 1179648 | tf_op jit(solution)/shard_map/neg | solution.py:289
  (57 shorter events, 0.7 us)
Async XLA Ops:
  0.7 1.0 copy-start.5
  1.7 0.7 copy-start.6
  2.4 0.7 copy-start.8
  4.5 14.2 %collective-permute-start = (bf16[128,512]{1,0:T(8,128)(2,1)S(1)}, bf16[128,512]{1,0:T(8,128)(2,1)S(1)}, u32[]{:S(2)}, u32[]{:S(2)}) collective-permute-start(bf16[128,512]{1,0:T(8,128)(2,1)S(1)} %get-tuple-element.16), channel_id=1, source_target_pairs={{0,224},{8,232},{16,240},{24,248},{32,0},{40,8},{48,16},{56,24},{6... | collective-permute-start | bytes 393224 | tf_op jit(solution)/shard_map/ppermute | solution.py:46
  11.0 10.4 %collective-permute-start.3 = (bf16[128,512]{1,0:T(8,128)(2,1)S(1)}, bf16[128,512]{1,0:T(8,128)(2,1)S(1)}, u32[]{:S(2)}, u32[]{:S(2)}) collective-permute-start(bf16[128,512]{1,0:T(8,128)(2,1)S(1)} %get-tuple-element.16), channel_id=1, source_target_pairs={{0,32},{8,40},{16,48},{24,56},{32,64},{40,72},{48,80},{56,88},{64,... | collective-permute-start | bytes 393224 | tf_op jit(solution)/shard_map/ppermute | solution.py:46
  14.7 23.5 %all-to-all-start = ((bf16[4,1536,128]{2,1,0:T(8,128)(2,1)}), bf16[4,1536,128]{2,1,0:T(8,128)(2,1)S(1)}, u32[]{:S(2)}, u32[]{:S(2)}) async-start(bf16[4,1536,128]{2,1,0:T(8,128)(2,1)} %shard_map.78), calls=%async_computation | async-start | bytes 3145728 | tf_op jit(solution)/shard_map/all_to_all | solution.py:37
  18.7 4.7 %collective-permute-start.1 = (bf16[128,512]{1,0:T(8,128)(2,1)S(1)}, bf16[128,512]{1,0:T(8,128)(2,1)S(1)}, u32[]{:S(2)}, u32[]{:S(2)}) collective-permute-start(bf16[128,512]{1,0:T(8,128)(2,1)S(1)} %collective-permute-done), channel_id=1, source_target_pairs={{0,224},{8,232},{16,240},{24,248},{32,0},{40,8},{48,16},{56,24},{6... | collective-permute-start | bytes 393224 | tf_op jit(solution)/shard_map/ppermute | solution.py:46
  21.5 5.3 %collective-permute-start.4 = (bf16[128,512]{1,0:T(8,128)(2,1)S(1)}, bf16[128,512]{1,0:T(8,128)(2,1)S(1)}, u32[]{:S(2)}, u32[]{:S(2)}) collective-permute-start(bf16[128,512]{1,0:T(8,128)(2,1)S(1)} %collective-permute-done.3), channel_id=1, source_target_pairs={{0,32},{8,40},{16,48},{24,56},{32,64},{40,72},{48,80},{56,88},{64,... | collective-permute-start | bytes 393224 | tf_op jit(solution)/shard_map/ppermute | solution.py:46
  23.4 5.0 %collective-permute-start.2 = (bf16[128,512]{1,0:T(8,128)(2,1)S(1)}, bf16[128,512]{1,0:T(8,128)(2,1)S(1)}, u32[]{:S(2)}, u32[]{:S(2)}) collective-permute-start(bf16[128,512]{1,0:T(8,128)(2,1)S(1)} %collective-permute-done.1), channel_id=1, source_target_pairs={{0,224},{8,232},{16,240},{24,248},{32,0},{40,8},{48,16},{56,24},{6... | collective-permute-start | bytes 393224 | tf_op jit(solution)/shard_map/ppermute | solution.py:46
  26.8 5.3 %collective-permute-start.5 = (bf16[128,512]{1,0:T(8,128)(2,1)S(1)}, bf16[128,512]{1,0:T(8,128)(2,1)S(1)}, u32[]{:S(2)}, u32[]{:S(2)}) collective-permute-start(bf16[128,512]{1,0:T(8,128)(2,1)S(1)} %collective-permute-done.4), channel_id=1, source_target_pairs={{0,32},{8,40},{16,48},{24,56},{32,64},{40,72},{48,80},{56,88},{64,... | collective-permute-start | bytes 393224 | tf_op jit(solution)/shard_map/ppermute | solution.py:46
  28.4 4.7 %collective-permute-start.7 = (bf16[64,512]{1,0:T(8,128)(2,1)S(1)}, bf16[64,512]{1,0:T(8,128)(2,1)S(1)}, u32[]{:S(2)}, u32[]{:S(2)}) collective-permute-start(bf16[64,512]{1,0:T(8,128)(2,1)S(1)} %slice.46), channel_id=1, source_target_pairs={{0,224},{8,232},{16,240},{24,248},{32,0},{40,8},{48,16},{56,24},{6... | collective-permute-start | bytes 196616 | tf_op jit(solution)/shard_map/ppermute | solution.py:46
  32.1 4.6 %collective-permute-start.6 = (bf16[64,512]{1,0:T(8,128)(2,1)S(1)}, bf16[64,512]{1,0:T(8,128)(2,1)S(1)}, u32[]{:S(2)}, u32[]{:S(2)}) collective-permute-start(bf16[64,512]{1,0:T(8,128)(2,1)S(1)} %slice.45), channel_id=1, source_target_pairs={{0,32},{8,40},{16,48},{24,56},{32,64},{40,72},{48,80},{56,88},{64,... | collective-permute-start | bytes 196616 | tf_op jit(solution)/shard_map/ppermute | solution.py:46
  36.8 8.8 %copy-start = (bf16[8,128,512]{2,1,0:T(8,128)(2,1)}, bf16[8,128,512]{2,1,0:T(8,128)(2,1)S(1)}, u32[]{:S(2)}) copy-start(bf16[8,128,512]{2,1,0:T(8,128)(2,1)S(1)} %bitcast_dynamic-update-slice_fusion.refs_0_) | copy-start | bytes 3145732
  38.9 1.0 copy-start.3
  39.9 31.2 %all-to-all-start.1 = ((bf16[8,512,128]{2,1,0:T(8,128)(2,1)}), bf16[8,512,128]{2,1,0:T(8,128)(2,1)}, u32[]{:S(2)}, u32[]{:S(2)}) async-start(bf16[8,512,128]{2,1,0:T(8,128)(2,1)} %copy-done.3), calls=%async_computation.1 | async-start | bytes 2097152 | tf_op jit(solution)/shard_map/all_to_all | solution.py:41
  44.2 21.8 %collective-permute-start.8 = (bf16[8,128,512]{2,1,0:T(8,128)(2,1)S(1)}, bf16[8,128,512]{2,1,0:T(8,128)(2,1)}, u32[]{:S(2)}, u32[]{:S(2)}) collective-permute-start(bf16[8,128,512]{2,1,0:T(8,128)(2,1)S(1)} %bitcast_dynamic-update-slice_fusion.refs_0_), channel_id=1, source_target_pairs={{0,24},{8,0},{16,8},{24,16},{32,56},{40,32},{48,40},{56,48},{64,88... | collective-permute-start | bytes 3145736 | tf_op jit(solution)/shard_map/ppermute | solution.py:51
  45.6 21.0 %collective-permute-start.9 = (bf16[8,128,512]{2,1,0:T(8,128)(2,1)S(1)}, bf16[8,128,512]{2,1,0:T(8,128)(2,1)}, u32[]{:S(2)}, u32[]{:S(2)}) collective-permute-start(bf16[8,128,512]{2,1,0:T(8,128)(2,1)S(1)} %bitcast_dynamic-update-slice_fusion.refs_0_), channel_id=1, source_target_pairs={{0,8},{8,16},{16,24},{24,0},{32,40},{40,48},{48,56},{56,32},{64,72... | collective-permute-start | bytes 3145736 | tf_op jit(solution)/shard_map/ppermute | solution.py:51
  73.6 28.7 %all-to-all-start.3 = ((bf16[8,512,128]{2,1,0:T(8,128)(2,1)}), bf16[8,512,128]{2,1,0:T(8,128)(2,1)S(1)}, u32[]{:S(2)}, u32[]{:S(2)}) async-start(bf16[8,512,128]{2,1,0:T(8,128)(2,1)} %broadcast_in_dim.2), calls=%async_computation.3 | async-start | bytes 2097152 | tf_op jit(solution)/shard_map/all_to_all | solution.py:41
  77.1 5.2 %collective-permute-start.12 = (bf16[512,128]{1,0:T(8,128)(2,1)S(1)}, bf16[512,128]{1,0:T(8,128)(2,1)S(1)}, u32[]{:S(2)}, u32[]{:S(2)}) collective-permute-start(bf16[512,128]{1,0:T(8,128)(2,1)S(1)} %reduce_sum.12), channel_id=1, source_target_pairs={{0,2},{1,3},{2,4},{3,5},{4,6},{5,7},{6,0},{7,1},{8,10},{9,11},{10,... | collective-permute-start | bytes 393224 | tf_op jit(solution)/shard_map/ppermute | solution.py:56
  78.5 6.4 %collective-permute-start.11 = (bf16[512,128]{1,0:T(8,128)(2,1)S(1)}, bf16[512,128]{1,0:T(8,128)(2,1)S(1)}, u32[]{:S(2)}, u32[]{:S(2)}) collective-permute-start(bf16[512,128]{1,0:T(8,128)(2,1)S(1)} %reduce_sum.12), channel_id=1, source_target_pairs={{0,4},{1,5},{2,6},{3,7},{4,0},{5,1},{6,2},{7,3},{8,12},{9,13},{10,... | collective-permute-start | bytes 393224 | tf_op jit(solution)/shard_map/ppermute | solution.py:56
  81.1 3.8 %collective-permute-start.10 = (bf16[512,128]{1,0:T(8,128)(2,1)S(1)}, bf16[512,128]{1,0:T(8,128)(2,1)S(1)}, u32[]{:S(2)}, u32[]{:S(2)}) collective-permute-start(bf16[512,128]{1,0:T(8,128)(2,1)S(1)} %reduce_sum.12), channel_id=1, source_target_pairs={{0,6},{1,7},{2,0},{3,1},{4,2},{5,3},{6,4},{7,5},{8,14},{9,15},{10,... | collective-permute-start | bytes 393224 | tf_op jit(solution)/shard_map/ppermute | solution.py:56
  85.0 8.1 %collective-permute-start.13 = (bf16[4,4,128,128]{3,2,1,0:T(8,128)(2,1)S(1)}, bf16[4,4,128,128]{3,2,1,0:T(8,128)(2,1)S(1)}, u32[]{:S(2)}, u32[]{:S(2)}) collective-permute-start(bf16[4,4,128,128]{3,2,1,0:T(8,128)(2,1)S(1)} %pad_maximum_fusion.2), channel_id=1, source_target_pairs={{0,1},{1,0},{2,3},{3,2},{4,5},{5,4},{6,7},{7,6},{8,9},{9,8},{10,11... | collective-permute-start | bytes 1572872 | tf_op jit(solution)/shard_map/ppermute | solution.py:60
  102.3 15.8 %all-to-all-start.2 = ((bf16[8,2,128,128]{3,2,1,0:T(8,128)(2,1)}), bf16[8,2,128,128]{3,2,1,0:T(8,128)(2,1)}, u32[]{:S(2)}, u32[]{:S(2)}) async-start(bf16[8,2,128,128]{3,2,1,0:T(8,128)(2,1)} %bitcast.23), calls=%async_computation.2 | async-start | bytes 1048576 | tf_op jit(solution)/shard_map/all_to_all | solution.py:41
  108.4 22.7 %collective-permute-start.15 = (bf16[4,128,512]{2,1,0:T(8,128)(2,1)}, bf16[4,128,512]{2,1,0:T(8,128)(2,1)S(1)}, u32[]{:S(2)}, u32[]{:S(2)}) collective-permute-start(bf16[4,128,512]{2,1,0:T(8,128)(2,1)} %slice.37), channel_id=1, source_target_pairs={{0,8},{8,16},{16,24},{24,0},{32,40},{40,48},{48,56},{56,32},{64,72... | collective-permute-start | bytes 1572872 | tf_op jit(solution)/shard_map/ppermute | solution.py:51
  110.2 20.8 %collective-permute-start.16 = (bf16[4,128,512]{2,1,0:T(8,128)(2,1)}, bf16[4,128,512]{2,1,0:T(8,128)(2,1)}, u32[]{:S(2)}, u32[]{:S(2)}) collective-permute-start(bf16[4,128,512]{2,1,0:T(8,128)(2,1)} %slice.38), channel_id=1, source_target_pairs={{0,24},{8,0},{16,8},{24,16},{32,56},{40,32},{48,40},{56,48},{64,88... | collective-permute-start | bytes 1572872 | tf_op jit(solution)/shard_map/ppermute | solution.py:51
  115.6 7.6 %collective-permute-start.19 = (bf16[4,128,128]{2,1,0:T(8,128)(2,1)}, bf16[4,128,128]{2,1,0:T(8,128)(2,1)S(1)}, u32[]{:S(2)}, u32[]{:S(2)}) collective-permute-start(bf16[4,128,128]{2,1,0:T(8,128)(2,1)} %get-tuple-element.25), channel_id=1, source_target_pairs={{0,24},{8,0},{16,8},{24,16},{32,56},{40,32},{48,40},{56,48},{64,88... | collective-permute-start | bytes 393224 | tf_op jit(solution)/shard_map/ppermute | solution.py:51
  115.6 15.4 %collective-permute-start.18 = (bf16[4,128,128]{2,1,0:T(8,128)(2,1)}, bf16[4,128,128]{2,1,0:T(8,128)(2,1)S(1)}, u32[]{:S(2)}, u32[]{:S(2)}) collective-permute-start(bf16[4,128,128]{2,1,0:T(8,128)(2,1)} %get-tuple-element.24), channel_id=1, source_target_pairs={{0,16},{8,24},{16,0},{24,8},{32,48},{40,56},{48,32},{56,40},{64,80... | collective-permute-start | bytes 393224 | tf_op jit(solution)/shard_map/ppermute | solution.py:51
  116.2 14.8 %collective-permute-start.17 = (bf16[4,128,128]{2,1,0:T(8,128)(2,1)S(1)}, bf16[4,128,128]{2,1,0:T(8,128)(2,1)S(1)}, u32[]{:S(2)}, u32[]{:S(2)}) collective-permute-start(bf16[4,128,128]{2,1,0:T(8,128)(2,1)S(1)} %get-tuple-element.23), channel_id=1, source_target_pairs={{0,8},{8,16},{16,24},{24,0},{32,40},{40,48},{48,56},{56,32},{64,72... | collective-permute-start | bytes 393224 | tf_op jit(solution)/shard_map/ppermute | solution.py:51
  123.2 18.2 %collective-permute-start.14 = (bf16[8,2,128,128]{3,2,1,0:T(8,128)(2,1)}, bf16[8,2,128,128]{3,2,1,0:T(8,128)(2,1)S(1)}, u32[]{:S(2)}, u32[]{:S(2)}) collective-permute-start(bf16[8,2,128,128]{3,2,1,0:T(8,128)(2,1)} %all-to-all-done.2.same_ref), channel_id=1, source_target_pairs={{0,1},{1,0},{2,3},{3,2},{4,5},{5,4},{6,7},{7,6},{8,9},{9,8},{10,11... | collective-permute-start | bytes 1572872 | tf_op jit(solution)/shard_map/ppermute | solution.py:60
  131.1 1.2 copy-start.1
  136.4 15.1 %collective-permute-start.24 = (bf16[4,512,128]{2,1,0:T(8,128)(2,1)}, bf16[4,512,128]{2,1,0:T(8,128)(2,1)}, u32[]{:S(2)}, u32[]{:S(2)}) collective-permute-start(bf16[4,512,128]{2,1,0:T(8,128)(2,1)} %bitcast.31), channel_id=1, source_target_pairs={{0,1},{1,0},{2,3},{3,2},{4,5},{5,4},{6,7},{7,6},{8,9},{9,8},{10,11... | collective-permute-start | bytes 1572872 | tf_op jit(solution)/shard_map/ppermute | solution.py:60
  136.4 12.3 %collective-permute-start.22 = (bf16[4,128,128]{2,1,0:T(8,128)(2,1)S(1)}, bf16[4,128,128]{2,1,0:T(8,128)(2,1)S(1)}, u32[]{:S(2)}, u32[]{:S(2)}) collective-permute-start(bf16[4,128,128]{2,1,0:T(8,128)(2,1)S(1)} %add_convert_fusion.refs_5_), channel_id=1, source_target_pairs={{0,2},{1,3},{2,4},{3,5},{4,6},{5,7},{6,0},{7,1},{8,10},{9,11},{10,... | collective-permute-start | bytes 393224 | tf_op jit(solution)/shard_map/ppermute | solution.py:56
  137.7 11.0 %collective-permute-start.21 = (bf16[4,128,128]{2,1,0:T(8,128)(2,1)S(1)}, bf16[4,128,128]{2,1,0:T(8,128)(2,1)S(1)}, u32[]{:S(2)}, u32[]{:S(2)}) collective-permute-start(bf16[4,128,128]{2,1,0:T(8,128)(2,1)S(1)} %add_convert_fusion.refs_5_), channel_id=1, source_target_pairs={{0,4},{1,5},{2,6},{3,7},{4,0},{5,1},{6,2},{7,3},{8,12},{9,13},{10,... | collective-permute-start | bytes 393224 | tf_op jit(solution)/shard_map/ppermute | solution.py:56
  140.4 8.4 %collective-permute-start.20 = (bf16[4,128,128]{2,1,0:T(8,128)(2,1)S(1)}, bf16[4,128,128]{2,1,0:T(8,128)(2,1)S(1)}, u32[]{:S(2)}, u32[]{:S(2)}) collective-permute-start(bf16[4,128,128]{2,1,0:T(8,128)(2,1)S(1)} %add_convert_fusion.refs_5_), channel_id=1, source_target_pairs={{0,6},{1,7},{2,0},{3,1},{4,2},{5,3},{6,4},{7,5},{8,14},{9,15},{10,... | collective-permute-start | bytes 393224 | tf_op jit(solution)/shard_map/ppermute | solution.py:56
  144.1 7.4 %copy-start.9 = (bf16[1,4,4,128,128]{4,3,2,1,0:T(8,128)(2,1)S(1)}, bf16[1,4,4,128,128]{4,3,2,1,0:T(8,128)(2,1)}, u32[]{:S(2)}) copy-start(bf16[1,4,4,128,128]{4,3,2,1,0:T(8,128)(2,1)} %get-tuple-element.31) | copy-start | bytes 1572868
  144.1 12.6 %all-to-all-start.4 = ((bf16[4,512,128]{2,1,0:T(8,128)(2,1)}), bf16[4,512,128]{2,1,0:T(8,128)(2,1)S(1)}, u32[]{:S(2)}, u32[]{:S(2)}) async-start(bf16[4,512,128]{2,1,0:T(8,128)(2,1)} %shard_map.81), calls=%async_computation.4 | async-start | bytes 1048576 | tf_op jit(solution)/shard_map/all_to_all | solution.py:37
  149.9 8.4 %collective-permute-start.23 = (bf16[4,4,128,128]{3,2,1,0:T(8,128)(2,1)}, bf16[4,4,128,128]{3,2,1,0:T(8,128)(2,1)}, u32[]{:S(2)}, u32[]{:S(2)}) collective-permute-start(bf16[4,4,128,128]{3,2,1,0:T(8,128)(2,1)} %get-tuple-element.36), channel_id=1, source_target_pairs={{0,1},{1,0},{2,3},{3,2},{4,5},{5,4},{6,7},{7,6},{8,9},{9,8},{10,11... | collective-permute-start | bytes 1572872 | tf_op jit(solution)/shard_map/ppermute | solution.py:60
  151.5 5.2 %copy-start.4 = (f32[512,128]{1,0:T(8,128)S(1)}, f32[512,128]{1,0:T(8,128)}, u32[]{:S(2)}) copy-start(f32[512,128]{1,0:T(8,128)} %trailing_ref.1) | copy-start | bytes 786436
  151.5 5.2 %copy-start.7 = (s32[32,32]{1,0:T(8,128)S(1)}, s32[32,32]{1,0:T(8,128)}, u32[]{:S(2)}) copy-start(s32[32,32]{1,0:T(8,128)} %fill_ref.3) | copy-start | bytes 12292
  153.7 4.5 %copy-start.10 = (bf16[1,4,4,128,128]{4,3,2,1,0:T(8,128)(2,1)S(1)}, bf16[1,4,4,128,128]{4,3,2,1,0:T(8,128)(2,1)}, u32[]{:S(2)}) copy-start(bf16[1,4,4,128,128]{4,3,2,1,0:T(8,128)(2,1)} %get-tuple-element.35) | copy-start | bytes 1572868
  154.5 7.5 %collective-permute-start.27 = (bf16[512,128]{1,0:T(8,128)(2,1)}, bf16[512,128]{1,0:T(8,128)(2,1)S(1)}, u32[]{:S(2)}, u32[]{:S(2)}) collective-permute-start(bf16[512,128]{1,0:T(8,128)(2,1)} %get-tuple-element.33), channel_id=1, source_target_pairs={{0,6},{1,7},{2,0},{3,1},{4,2},{5,3},{6,4},{7,5},{8,14},{9,15},{10,... | collective-permute-start | bytes 393224 | tf_op jit(solution)/shard_map/ppermute | solution.py:56
  154.5 7.5 %collective-permute-start.26 = (bf16[512,128]{1,0:T(8,128)(2,1)}, bf16[512,128]{1,0:T(8,128)(2,1)S(1)}, u32[]{:S(2)}, u32[]{:S(2)}) collective-permute-start(bf16[512,128]{1,0:T(8,128)(2,1)} %get-tuple-element.34), channel_id=1, source_target_pairs={{0,4},{1,5},{2,6},{3,7},{4,0},{5,1},{6,2},{7,3},{8,12},{9,13},{10,... | collective-permute-start | bytes 393224 | tf_op jit(solution)/shard_map/ppermute | solution.py:56
  156.6 2.8 %copy-start.2 = (bf16[8,128,512]{2,1,0:T(8,128)(2,1)S(1)}, bf16[8,128,512]{2,1,0:T(8,128)(2,1)}, u32[]{:S(2)}) copy-start(bf16[8,128,512]{2,1,0:T(8,128)(2,1)} %copy-done) | copy-start | bytes 3145732
  156.6 7.7 %collective-permute-start.25 = (bf16[512,128]{1,0:T(8,128)(2,1)S(1)}, bf16[512,128]{1,0:T(8,128)(2,1)S(1)}, u32[]{:S(2)}, u32[]{:S(2)}) collective-permute-start(bf16[512,128]{1,0:T(8,128)(2,1)S(1)} %get-tuple-element.32), channel_id=1, source_target_pairs={{0,2},{1,3},{2,4},{3,5},{4,6},{5,7},{6,0},{7,1},{8,10},{9,11},{10,... | collective-permute-start | bytes 393224 | tf_op jit(solution)/shard_map/ppermute | solution.py:56

commit v4 on v3

v4 whole, which is shorter than its diff:
```python
import jax
import jax.numpy as jnp
from jax import lax
from jax.experimental import pallas as pl
from jax.experimental.pallas import tpu as pltpu
from jax.sharding import PartitionSpec as P

BS = 128
NZ = 8
NX = 4
NY = 4
NS = 32
ROWS = 512
BF = jnp.bfloat16
F32 = jnp.float32
X_GROUPS = [[z * NX + x for x in range(NX)] for z in range(NZ)]
Z_GROUPS = [[z * NX + x for z in range(NZ)] for x in range(NX)]
VMEM = pl.BlockSpec(memory_space=pltpu.VMEM)
SMEM = pl.BlockSpec(memory_space=pltpu.SMEM)
ANY = pl.BlockSpec(memory_space=pl.ANY)
TILE = jax.ShapeDtypeStruct((ROWS, BS), BF)
STACK = jax.ShapeDtypeStruct((NY, ROWS, BS), BF)


def call(kernel, out_shape, in_specs, flops, nbytes, vmem=12, out_specs=None, scratch=()):
    many = isinstance(out_shape, (tuple, list))
    if out_specs is None:
        out_specs = [VMEM] * len(out_shape) if many else VMEM
    return pl.pallas_call(
        kernel,
        out_shape=out_shape,
        in_specs=in_specs,
        out_specs=out_specs,
        scratch_shapes=list(scratch),
        compiler_params=pltpu.CompilerParams(vmem_limit_bytes=vmem * 1024 * 1024),
        cost_estimate=pl.CostEstimate(flops=flops, bytes_accessed=nbytes, transcendentals=0),
    )


def exchange_x(value):
    return lax.all_to_all(value, "col", 0, 0, axis_index_groups=X_GROUPS)


def exchange_z(value):
    return lax.all_to_all(value, "col", 0, 0, axis_index_groups=Z_GROUPS)


def shift_z(value, k):
    pairs = [(z * NX + x, (z + k) % NZ * NX + x) for z in range(NZ) for x in range(NX)]
    return lax.ppermute(value, "col", pairs)


def shift_x(value, k):
    pairs = [(z * NX + x, z * NX + (x + k) % NX) for z in range(NZ) for x in range(NX)]
    return lax.ppermute(value, "col", pairs)


def shift_y(value, k):
    pairs = [(y * 2 + c, (y + k) % NY * 2 + c) for y in range(NY) for c in range(2)]
    return lax.ppermute(value, "row", pairs)


def swap_core(value):
    return lax.ppermute(value, "row", [(r, r ^ 1) for r in range(2 * NY)])


def gather_y(value):
    return [value] + [shift_y(value, -k) for k in range(1, NY)]


def spread_kernel(total_ref, *refs):
    out_ref = refs[-1]
    for i in range(4):
        total = total_ref[i]
        for ref in refs[:3]:
            total += ref[i].astype(F32)
        total = total.astype(BF)
        refs[3][i] = total
        for r in range(2 * NY):
            out_ref[r, i] = total


def sum_kernel(parts_ref, tile_ref, out_ref):
    total = parts_ref[0].astype(F32)
    for z in range(1, NZ):
        total += parts_ref[z].astype(F32)
    total = total.astype(BF)
    tile_ref[...] = total
    for z in range(NZ):
        out_ref[z] = total


def factor_kernel(got_ref, out_ref):
    left = jnp.concatenate([got_ref[x, :ROWS, :] for x in range(NX)], axis=1)
    for z in range(0, NZ, 2):
        right = jnp.concatenate(
            [
                jnp.concatenate(
                    [got_ref[x, ROWS + (z + h) * BS : ROWS + (z + h + 1) * BS, :] for h in range(2)],
                    axis=1,
                )
                for x in range(NX)
            ],
            axis=0,
        )
        product = jnp.dot(left, right, preferred_element_type=F32).astype(BF)
        out_ref[z] = product[:, :BS]
        out_ref[z + 1] = product[:, BS:]


def sent_kernel(panel_ref, *refs):
    sent_ref = refs[-1]
    sent_ref[0, :ROWS, :] = panel_ref[...]
    for z in range(NZ):
        sent_ref[0, ROWS + z * BS : ROWS + (z + 1) * BS, :] = refs[z][...]


def weighted_kernel(at_ref, owner_ref, fill_ref, cotangent_ref, weighted_ref, meta_ref):
    for j in range(6):
        meta_ref[j] = at_ref[j]
    for j in range(NS):
        meta_ref[6 + owner_ref[j]] = j
    mine = meta_ref[6 + at_ref[3]]
    for i in range(4):
        scale = fill_ref[at_ref[4] * 4 + i, mine].astype(F32)
        rows = slice(i * BS, (i + 1) * BS)
        weighted_ref[:, rows] = (scale * cotangent_ref[rows, :]).T.astype(BF)


def tail_kernel(at_ref, fill_ref, trailing_ref, *refs):
    out_ref = refs[-1]
    mine = at_ref[6 + at_ref[3]]
    for i in range(4):
        scale = fill_ref[at_ref[4] * 4 + i, mine].astype(F32)
        rows = slice(i * BS, (i + 1) * BS)
        total = refs[0][rows, :]
        for ref in refs[1:4]:
            total += ref[rows, :].astype(F32)
        out_ref[rows, :] = trailing_ref[rows, :] - scale * total


def inner_kernel(at_ref, got_ref, factor_ref, *outs):
    right = jnp.concatenate([factor_ref[z] for z in range(NZ)], axis=1)
    rows = []
    for k in range(NX):
        x = lax.rem(at_ref[5] + k, NX)
        blocks = [got_ref[x, ROWS + z * BS : ROWS + (z + 1) * BS, :] for z in range(NZ)]
        rows.append(jnp.concatenate(blocks, axis=1))
    left = jnp.concatenate(rows, axis=0)
    product = lax.dot_general(left, right, (((1,), (1,)), ((), ())), preferred_element_type=F32)
    for k in range(NX):
        for i in range(4):
            block = product[k * BS : (k + 1) * BS, i * BS : (i + 1) * BS]
            outs[k][i] = block.astype(outs[k].dtype)


def outer_kernel(at_ref, same_ref, other_ref, factor_ref, *outs):
    left = jnp.concatenate([factor_ref[z] for z in range(NZ)], axis=1)
    rows = []
    for k in range(NX):
        x = lax.rem(at_ref[5] + k, NX)
        mine = x // 2 == at_ref[2]
        h = lax.rem(x, 2)
        blocks = [jnp.where(mine, same_ref[z, h], other_ref[z, h]) for z in range(NZ)]
        rows.append(jnp.concatenate(blocks, axis=1))
    right = jnp.concatenate(rows, axis=0)
    product = lax.dot_general(left, right, (((1,), (1,)), ((), ())), preferred_element_type=F32)
    for k in range(NX):
        outs[k][...] = product[:, k * BS : (k + 1) * BS].astype(outs[k].dtype)


def place(at_ref, j):
    y = lax.rem(j // 8 + NY - at_ref[1], NY)
    c = lax.rem(j // 4 + at_ref[2], 2)
    return c, y, j % 4


def chosen(at_ref, j, same_ref, other_ref):
    c, y, i = place(at_ref, j)
    return jnp.where(c == 0, same_ref[y, i], other_ref[y, i])


def pick_kernel(at_ref, same_ref, other_ref, out_ref):
    for s in range(NS // 2):
        j = at_ref[6 + s // 2 * NX + s % 2 + 2 * at_ref[2]]
        out_ref[s] = chosen(at_ref, j, same_ref, other_ref)


def quarters(at_ref, refs):
    own, one, two_a, two_b, three = refs
    for k, pair in enumerate(((own, own), (one, one), (two_a, two_b), (three, three))):
        for h in range(2):
            ref = pair[h]
            first = 4 * h if ref.shape[0] == NZ else 0
            slots = []
            for d in range(4 * h, 4 * h + 4):
                z = lax.rem(at_ref[0] + d, NZ)
                x = lax.rem(at_ref[5] + k, NX)
                slots.append(at_ref[6 + z * NX + x])
            yield slots, ref[first : first + 4].reshape(4 * BS, ROWS)


def column_kernel(at_ref, *refs):
    piece_ref, same_ref, other_ref, token_ref = refs[5:]
    piece = jnp.concatenate([piece_ref[i] for i in range(4)], axis=1)
    for slots, left in quarters(at_ref, refs[:5]):
        product = lax.dot_general(
            left, piece, (((1,), (1,)), ((), ())), preferred_element_type=F32
        ).astype(BF)
        for h, j in enumerate(slots):
            c, y, i = place(at_ref, j)
            part = product[h * BS : (h + 1) * BS]
            same_ref[jnp.where(c == 0, y, NY), i] = part
            other_ref[jnp.where(c == 0, NY, y), i] = part
    token_ref[...] = jnp.zeros(token_ref.shape, F32)


def total_kernel(same_ref, got_ref, keep_ref, *outs):
    keep_ref[...] = same_ref[0].astype(F32) + got_ref[0].astype(F32)
    for k in range(1, NY):
        outs[k - 1][...] = (same_ref[k].astype(F32) + got_ref[k].astype(F32)).astype(BF)


def own_kernel(at_ref, *refs):
    all_ref, out_ref = refs[5:]
    total = jnp.zeros((BS, ROWS), F32)
    for slots, right in quarters(at_ref, refs[:5]):
        left = jnp.concatenate([all_ref[j // 4, j % 4] for j in slots], axis=1)
        total += jnp.dot(left, right, preferred_element_type=F32)
    out_ref[...] = total.T


def final_kernel(own_ref, keep_ref, *refs):
    out_ref = refs[-1]
    for i in range(4):
        rows = slice(i * BS, (i + 1) * BS)
        total = own_ref[rows, :] + keep_ref[i]
        for ref in refs[:-1]:
            total += ref[i].astype(F32)
        out_ref[rows, :] = -total


def stack_kernel(*refs):
    out_ref = refs[-1]
    for k in range(NY):
        out_ref[k] = refs[k][...]


def both_cores(pieces, *after):
    pieces = [piece.reshape(4, BS, BS) for piece in pieces]
    same = call(
        stack_kernel,
        jax.ShapeDtypeStruct((NY, 4, BS, BS), BF),
        [VMEM] * NY + [ANY] * len(after),
        0,
        1 << 20,
    )(*pieces, *after)
    return same, swap_core(same)


def whole(shape):
    return pl.BlockSpec(shape, lambda g: (0,) * len(shape))


def sweep(kernel, out_shape, *args):
    return call(
        kernel, out_shape, [SMEM] + [VMEM] * (len(args) - 1), 2 * 512 * 4096 * 128, 6 << 20
    )(*args)


def on_device(panel, inv_factor, fill, owner, trailing, cotangent):
    col = lax.axis_index("col")
    row = lax.axis_index("row")
    at = jnp.stack([col // NX, row // 2, row % 2, col, row, col % NX]).astype(jnp.int32)
    sent = pl.pallas_call(
        sent_kernel,
        grid=(NX,),
        out_shape=jax.ShapeDtypeStruct((NX, ROWS + NZ * BS, BS), BF),
        in_specs=[whole((ROWS, BS))]
        + [pl.BlockSpec((BS, BS), lambda g, z=z: (0, z * NX + g)) for z in range(NZ)],
        out_specs=pl.BlockSpec((1, ROWS + NZ * BS, BS), lambda g: (g, 0, 0)),
        cost_estimate=pl.CostEstimate(flops=0, bytes_accessed=3 << 20, transcendentals=0),
    )(panel, *([inv_factor] * NZ))
    sent, cotangent = lax.optimization_barrier((sent, cotangent))
    weighted, at = pl.pallas_call(
        weighted_kernel,
        out_shape=[
            jax.ShapeDtypeStruct((BS, ROWS), BF),
            jax.ShapeDtypeStruct((NS + 6,), jnp.int32),
        ],
        in_specs=[SMEM] * 3 + [VMEM],
        out_specs=[VMEM, SMEM],
        compiler_params=pltpu.CompilerParams(vmem_limit_bytes=16 * 1024 * 1024),
        cost_estimate=pl.CostEstimate(flops=0, bytes_accessed=1 << 19, transcendentals=0),
    )(at, owner, fill, cotangent)
    u1, d1 = shift_z(weighted, 1), shift_z(weighted, -1)
    u2, d2 = shift_z(weighted, 2), shift_z(weighted, -2)
    u1, d1, u2, d2 = lax.optimization_barrier((u1, d1, u2, d2))
    u3, d3, d4 = shift_z(u2, 1), shift_z(d2, -1), shift_z(d2, -2)
    got, u1, u2, u3, d1, d2, d3, d4 = lax.optimization_barrier(
        (exchange_x(sent), u1, u2, u3, d1, d2, d3, d4)
    )
    near = jnp.stack([weighted, d1, d2, d3, d4, u3, u2, u1])

    tiles = jax.ShapeDtypeStruct((NZ, ROWS, BS), BF)
    partial = call(factor_kernel, tiles, [VMEM], 2 * 512 * 512 * 1024, 3 << 20)(got)
    parts, one, three = lax.optimization_barrier(
        (exchange_z(partial), shift_x(near, -1), shift_x(near, 1))
    )
    two_a, two_b = shift_x(three[:4], 1), shift_x(one[4:], -1)
    factor, spread = call(sum_kernel, [TILE, tiles], [VMEM], 0, 2 << 20)(parts)
    picked = call(
        pick_kernel, jax.ShapeDtypeStruct((NS // 2, BS, BS), BF), [SMEM] + [VMEM] * 2, 0, 2 << 20
    )(at, *both_cores(gather_y(factor), two_a, two_b))
    tile = jax.ShapeDtypeStruct((4, BS, BS), BF)
    total = jax.ShapeDtypeStruct((4, BS, BS), F32)
    token = jax.ShapeDtypeStruct((8, BS), F32)
    factor_k = exchange_z(spread)
    inner = call(
        inner_kernel,
        [total, tile, tile, tile],
        [SMEM] + [VMEM] * 2,
        2 * 512 * 1024 * 512,
        4 << 20,
    )(at, got, factor_k)
    owned = exchange_z(picked.reshape(NZ, 2, BS, BS))
    piece, spread = call(
        spread_kernel,
        [tile, jax.ShapeDtypeStruct((2 * NY, 4, BS, BS), BF)],
        [VMEM] * 4,
        0,
        2 << 20,
    )(inner[0], *[shift_x(inner[k], k) for k in range(1, NX)])

    weights = (near, one, two_a, two_b, three)
    blocks = jax.ShapeDtypeStruct((NY + 1, 4, BS, BS), BF)
    same, other, after = sweep(column_kernel, [blocks, blocks, token], at, *weights, piece)
    keep, *leave = call(total_kernel, [total] + [tile] * 3, [VMEM] * 2, 0, 2 << 20)(
        same, swap_core(other)
    )
    own = sweep(
        own_kernel,
        jax.ShapeDtypeStruct((ROWS, BS), F32),
        at,
        *weights,
        lax.all_to_all(spread, "row", 0, 0),
    )
    moved = [shift_y(value, k + 1) for k, value in enumerate(leave)]
    panel_grad = call(
        final_kernel, jax.ShapeDtypeStruct((ROWS, BS), F32), [VMEM] * 5, 0, 1 << 20
    )(own, keep, *moved)

    outer = call(
        outer_kernel,
        [jax.ShapeDtypeStruct((ROWS, BS), F32), TILE, TILE, TILE],
        [SMEM] + [VMEM] * 3,
        2 * 512 * 1024 * 512,
        4 << 20,
    )(at, owned, swap_core(owned), factor_k)
    updated = call(
        tail_kernel, jax.ShapeDtypeStruct((ROWS, BS), F32), [SMEM] * 2 + [VMEM] * 5, 0, 1 << 20
    )(at, fill, trailing, outer[0], *[shift_x(outer[k], k) for k in range(1, NX)])
    return updated, panel_grad


def solution(mesh):
    return jax.shard_map(
        on_device,
        mesh=mesh,
        in_specs=(P("row", "col"), P("col", None), P(), P(), P("row", "col"), P("row", "col")),
        out_specs=(P("row", "col"), P("row", "col")),
        check_vma=False,
    )
```

time: 167 us -> 158 us (0.946)
  other arithmetic: 7.84 us -> 0 us
  waiting for transfers between devices: 55.9 us -> 60.2 us
  local copies, waits for them, and re-layouts: 11.4 us -> 7.81 us
  starting transfers between devices: 70.2 us -> 68 us
    ppermute x7 -> x10, starting transfers between devices: 5.69 us -> 19.2 us  [shift_x(): return lax.ppermute(value, 'col', pairs)]
    ppermute x4 -> x3, starting transfers between devices: 15.9 us -> 3.88 us  [swap_core(): return lax.ppermute(value, 'row', [(r, r ^ 1) for r in range(2 * NY)])]
    ppermute x8 -> x7, waiting for transfers between devices: 8.75 us -> 16.4 us  [shift_z(): return lax.ppermute(value, 'col', pairs)]
    all_to_all x0 -> x1, starting transfers between devices: none -> 6.89 us  [on_device(): lax.all_to_all(spread, 'row', 0, 0)]
    ppermute x8 -> x7, starting transfers between devices: 15.7 us -> 10.7 us  [shift_z(): return lax.ppermute(value, 'col', pairs)]
    another operation x5 -> x0, other arithmetic: 4.66 us -> none  [the longest x3 2.35 us: both_cores(): return jnp.stack([same, swap_core(same)])]
    all_to_all x3, waiting for transfers between devices: 13.1 us -> 9.23 us  [exchange_z(): return lax.all_to_all(value, 'col', 0, 0, axis_index_groups=Z_GROUPS)]
    all_to_all x2 -> x1, starting transfers between devices: 8.72 us -> 4.99 us  [exchange_x(): return lax.all_to_all(value, 'col', 0, 0, axis_index_groups=X_GROUPS)]
  transfers between devices with their start and end apart: 33 -> 31, of which waited for: 18 -> 19; matrix products, arithmetic and copies ran while one was open for 6% -> 2% of each run, Pallas kernels for 11% -> 9%
where the time goes in v4:
time: 158 us; the launch traced here: 157 us
  starting transfers between devices  68 us (43%)
  waiting for transfers between devices  60.2 us (38%)
  Pallas kernels  19.9 us (13%)
  local copies, waits for them, and re-layouts  7.81 us (5%)
    ppermute x10, waiting for transfers between devices, shift_x(): return lax.ppermute(value, 'col', pairs)  29.4 us
    ppermute x10, starting transfers between devices, shift_x(): return lax.ppermute(value, 'col', pairs)  19.2 us
    ppermute x7, waiting for transfers between devices, shift_z(): return lax.ppermute(value, 'col', pairs)  16.4 us
    all_to_all x3, starting transfers between devices, exchange_z(): return lax.all_to_all(value, 'col', 0, 0, axis_index_groups=Z_GROUPS)  12.1 us
    ppermute x7, starting transfers between devices, shift_z(): return lax.ppermute(value, 'col', pairs)  10.7 us
    ppermute x6, starting transfers between devices, shift_y(): return lax.ppermute(value, 'row', pairs)  10.2 us
    all_to_all x3, waiting for transfers between devices, exchange_z(): return lax.all_to_all(value, 'col', 0, 0, axis_index_groups=Z_GROUPS)  9.23 us
    all_to_all x1, starting transfers between devices, on_device(): lax.all_to_all(spread, 'row', 0, 0)  6.89 us
  transfers between devices with their start and end apart: 31, of which 19 were waited for; matrix products, arithmetic and copies ran while one was open for 2% of the time, Pallas kernels for 9%

profile of v4, /device:TPU:1, one launch (start us, length us, event | category | flops | bytes accessed | tf_op | source)
XLA Modules:
  0.0 156.8 jit_solution(14401601885276202845)
XLA Ops:
  0.6 3.7 %shard_map.77 = bf16[4,1536,128]{2,1,0:T(8,128)(2,1)} custom-call(bf16[512,128]{1,0:T(8,128)(2,1)} %panel_ref.1, bf16[128,4096]{1,0:T(8,128)(2,1)} %refs_7_.1, bf16[128,4096]{1,0:T(8,128)(2,1)} %refs_7_.1, bf16[128,4096]{1,0:T(8,128)(2,1)} %refs_7_.1, bf16[128,4096]{1,0:T(8,128)(2,1)} %refs_7_.1, bf16[128,4096]{1,0:T(8,128)(2,1)} %refs_7_.1, ...), custom_call_target="tpu_custom_call" | custom-call | bytes 3145728 | tf_op jit(solution)/shard_map/pallas_call | solution.py:275
  4.3 5.0 %all-to-all-start = ((bf16[4,1536,128]{2,1,0:T(8,128)(2,1)}), bf16[4,1536,128]{2,1,0:T(8,128)(2,1)S(1)}, u32[]{:S(2)}, u32[]{:S(2)}) async-start(bf16[4,1536,128]{2,1,0:T(8,128)(2,1)} %shard_map.77), calls=%async_computation | async-start | bytes 3145728 | tf_op jit(solution)/shard_map/all_to_all | solution.py:41
  9.4 1.5 shard_map.78
  10.9 6.1 %collective-permute-start.3 = (bf16[128,512]{1,0:T(8,128)(2,1)S(1)}, bf16[128,512]{1,0:T(8,128)(2,1)S(1)}, u32[]{:S(2)}, u32[]{:S(2)}) collective-permute-start(bf16[128,512]{1,0:T(8,128)(2,1)S(1)} %get-tuple-element.42), channel_id=1, source_target_pairs={{0,192},{8,200},{16,208},{24,216},{32,224},{40,232},{48,240},{56,2... | collective-permute-start | bytes 393224 | tf_op jit(solution)/shard_map/ppermute | solution.py:50
  17.0 3.1 %collective-permute-start.1 = (bf16[128,512]{1,0:T(8,128)(2,1)S(1)}, bf16[128,512]{1,0:T(8,128)(2,1)S(1)}, u32[]{:S(2)}, u32[]{:S(2)}) collective-permute-start(bf16[128,512]{1,0:T(8,128)(2,1)S(1)} %get-tuple-element.42), channel_id=1, source_target_pairs={{0,224},{8,232},{16,240},{24,248},{32,0},{40,8},{48,16},{56,24},{6... | collective-permute-start | bytes 393224 | tf_op jit(solution)/shard_map/ppermute | solution.py:50
  20.1 4.5 %collective-permute-done.2 = bf16[128,512]{1,0:T(8,128)(2,1)S(1)} collective-permute-done((bf16[128,512]{1,0:T(8,128)(2,1)S(1)}, bf16[128,512]{1,0:T(8,128)(2,1)S(1)}, u32[]{:S(2)}, u32[]{:S(2)}) %collective-permute-start.2) | collective-permute-done | bytes 131104 | tf_op jit(solution)/shard_map/ppermute | solution.py:50
  24.7 0.7 collective-permute-done.1
  25.4 3.6 %collective-permute-done = bf16[128,512]{1,0:T(8,128)(2,1)S(1)} collective-permute-done((bf16[128,512]{1,0:T(8,128)(2,1)S(1)}, bf16[128,512]{1,0:T(8,128)(2,1)S(1)}, u32[]{:S(2)}, u32[]{:S(2)}) %collective-permute-start) | collective-permute-done | bytes 131104 | tf_op jit(solution)/shard_map/ppermute | solution.py:50
  29.0 0.1 collective-permute-start.5
  29.1 1.3 collective-permute-start.4
  30.5 3.7 %collective-permute-done.4 = bf16[128,512]{1,0:T(8,128)(2,1)S(1)} collective-permute-done((bf16[128,512]{1,0:T(8,128)(2,1)S(1)}, bf16[128,512]{1,0:T(8,128)(2,1)S(1)}, u32[]{:S(2)}, u32[]{:S(2)}) %collective-permute-start.4) | collective-permute-done | bytes 131104 | tf_op jit(solution)/shard_map/ppermute | solution.py:50
  34.2 1.8 %collective-permute-done.6 = bf16[128,512]{1,0:T(8,128)(2,1)S(1)} collective-permute-done((bf16[128,512]{1,0:T(8,128)(2,1)S(1)}, bf16[128,512]{1,0:T(8,128)(2,1)S(1)}, u32[]{:S(2)}, u32[]{:S(2)}) %collective-permute-start.6) | collective-permute-done | bytes 131104 | tf_op jit(solution)/shard_map/ppermute | solution.py:50
  36.0 2.1 %collective-permute-done.5 = bf16[128,512]{1,0:T(8,128)(2,1)} collective-permute-done((bf16[128,512]{1,0:T(8,128)(2,1)S(1)}, bf16[128,512]{1,0:T(8,128)(2,1)}, u32[]{:S(2)}, u32[]{:S(2)}) %collective-permute-start.5) | collective-permute-done | bytes 131104 | tf_op jit(solution)/shard_map/ppermute | solution.py:50
  38.0 0.7 shard_map.79
  38.8 1.0 copy-done.4
  39.7 4.4 %all-to-all-start.1 = ((bf16[8,512,128]{2,1,0:T(8,128)(2,1)}), bf16[8,512,128]{2,1,0:T(8,128)(2,1)}, u32[]{:S(2)}, u32[]{:S(2)}) async-start(bf16[8,512,128]{2,1,0:T(8,128)(2,1)} %copy-done.4), calls=%async_computation.1 | async-start | bytes 2097152 | tf_op jit(solution)/shard_map/all_to_all | solution.py:45
  44.2 0.9 bitcast_dynamic-update-slice_fusion.4
  45.2 1.5 collective-permute-start.8
  46.6 1.3 collective-permute-start.7
  47.9 21.1 %collective-permute-done.8.refs_4_ = bf16[8,128,512]{2,1,0:T(8,128)(2,1)} collective-permute-done((bf16[8,128,512]{2,1,0:T(8,128)(2,1)S(1)}, bf16[8,128,512]{2,1,0:T(8,128)(2,1)}, u32[]{:S(2)}, u32[]{:S(2)}) %collective-permute-start.8) | collective-permute-done | bytes 1048608 | tf_op jit(solution)/shard_map/ppermute | solution.py:55
  69.2 4.3 %all-to-all-done.1.parts_ref = bf16[8,512,128]{2,1,0:T(8,128)(2,1)} async-done(((bf16[8,512,128]{2,1,0:T(8,128)(2,1)}), bf16[8,512,128]{2,1,0:T(8,128)(2,1)}, u32[]{:S(2)}, u32[]{:S(2)}) %all-to-all-start.1) | async-done | bytes 1048608 | tf_op jit(solution)/shard_map/all_to_all | solution.py:45
  73.4 1.4 shard_map.80
  74.8 1.0 copy-done.7
  75.8 3.6 %all-to-all-start.3 = ((bf16[8,512,128]{2,1,0:T(8,128)(2,1)}), bf16[8,512,128]{2,1,0:T(8,128)(2,1)S(1)}, u32[]{:S(2)}, u32[]{:S(2)}) async-start(bf16[8,512,128]{2,1,0:T(8,128)(2,1)} %copy-done.7), calls=%async_computation.3 | async-start | bytes 2097152 | tf_op jit(solution)/shard_map/all_to_all | solution.py:45
  79.4 1.1 slice.6
  80.4 1.1 slice.7
  81.5 2.7 %collective-permute-start.13 = (bf16[4,128,512]{2,1,0:T(8,128)(2,1)S(1)}, bf16[4,128,512]{2,1,0:T(8,128)(2,1)S(1)}, u32[]{:S(2)}, u32[]{:S(2)}) collective-permute-start(bf16[4,128,512]{2,1,0:T(8,128)(2,1)S(1)} %slice.7), channel_id=1, source_target_pairs={{0,24},{8,0},{16,8},{24,16},{32,56},{40,32},{48,40},{56,48},{64,88... | collective-permute-start | bytes 1572872 | tf_op jit(solution)/shard_map/ppermute | solution.py:55
  84.2 1.3 collective-permute-start.11
  85.5 2.8 %collective-permute-start.10 = (bf16[512,128]{1,0:T(8,128)(2,1)S(1)}, bf16[512,128]{1,0:T(8,128)(2,1)S(1)}, u32[]{:S(2)}, u32[]{:S(2)}) collective-permute-start(bf16[512,128]{1,0:T(8,128)(2,1)S(1)} %get-tuple-element.56), channel_id=1, source_target_pairs={{0,4},{1,5},{2,6},{3,7},{4,0},{5,1},{6,2},{7,3},{8,12},{9,13},{10,... | collective-permute-start | bytes 393224 | tf_op jit(solution)/shard_map/ppermute | solution.py:60
  88.3 1.1 collective-permute-start.9
  89.4 0.4 collective-permute-done.11
  89.8 2.6 %collective-permute-done.10 = bf16[512,128]{1,0:T(8,128)(2,1)S(1)} collective-permute-done((bf16[512,128]{1,0:T(8,128)(2,1)S(1)}, bf16[512,128]{1,0:T(8,128)(2,1)S(1)}, u32[]{:S(2)}, u32[]{:S(2)}) %collective-permute-start.10) | collective-permute-done | bytes 131104 | tf_op jit(solution)/shard_map/ppermute | solution.py:60
  92.4 0.6 collective-permute-done.9
  93.0 0.2 collective-permute-done.13.refs_5_.refs_3_
  93.3 3.1 %collective-permute-done.12.refs_4_.refs_2_ = bf16[4,128,512]{2,1,0:T(8,128)(2,1)S(1)} collective-permute-done((bf16[4,128,512]{2,1,0:T(8,128)(2,1)S(1)}, bf16[4,128,512]{2,1,0:T(8,128)(2,1)S(1)}, u32[]{:S(2)}, u32[]{:S(2)}) %collective-permute-start.12) | collective-permute-done | bytes 524320 | tf_op jit(solution)/shard_map/ppermute | solution.py:55
  96.4 0.8 copy-done.2
  97.2 3.4 %collective-permute-start.14 = (bf16[4,4,128,128]{3,2,1,0:T(8,128)(2,1)S(1)}, bf16[4,4,128,128]{3,2,1,0:T(8,128)(2,1)S(1)}, u32[]{:S(2)}, u32[]{:S(2)}) collective-permute-start(bf16[4,4,128,128]{3,2,1,0:T(8,128)(2,1)S(1)} %shard_map.81.same_ref), channel_id=1, source_target_pairs={{0,1},{1,0},{2,3},{3,2},{4,5},{5,4},{6,7},{7,6},{8,9},{9,8},{10,11... | collective-permute-start | bytes 1572872 | tf_op jit(solution)/shard_map/ppermute | solution.py:64
  100.6 1.5 collective-permute-done.14.other_ref
  102.1 0.9 shard_map.82
  103.0 0.8 copy-done.5
  103.8 3.1 %all-to-all-done.3.factor_ref = bf16[8,512,128]{2,1,0:T(8,128)(2,1)S(1)} async-done(((bf16[8,512,128]{2,1,0:T(8,128)(2,1)}), bf16[8,512,128]{2,1,0:T(8,128)(2,1)S(1)}, u32[]{:S(2)}, u32[]{:S(2)}) %all-to-all-start.3) | async-done | bytes 1048608 | tf_op jit(solution)/shard_map/all_to_all | solution.py:45
  106.9 4.1 %all-to-all-start.2 = ((bf16[8,2,128,128]{3,2,1,0:T(8,128)(2,1)}), bf16[8,2,128,128]{3,2,1,0:T(8,128)(2,1)}, u32[]{:S(2)}, u32[]{:S(2)}) async-start(bf16[8,2,128,128]{3,2,1,0:T(8,128)(2,1)} %bitcast.27), calls=%async_computation.2 | async-start | bytes 1048576 | tf_op jit(solution)/shard_map/all_to_all | solution.py:45
  111.1 1.3 shard_map.85
  112.4 3.0 %collective-permute-start.19 = (bf16[4,128,128]{2,1,0:T(8,128)(2,1)S(1)}, bf16[4,128,128]{2,1,0:T(8,128)(2,1)S(1)}, u32[]{:S(2)}, u32[]{:S(2)}) collective-permute-start(bf16[4,128,128]{2,1,0:T(8,128)(2,1)S(1)} %get-tuple-element.65), channel_id=1, source_target_pairs={{0,8},{8,16},{16,24},{24,0},{32,40},{40,48},{48,56},{56,32},{64,72... | collective-permute-start | bytes 393224 | tf_op jit(solution)/shard_map/ppermute | solution.py:55
  115.4 2.4 %collective-permute-start.20 = (bf16[4,128,128]{2,1,0:T(8,128)(2,1)S(1)}, bf16[4,128,128]{2,1,0:T(8,128)(2,1)S(1)}, u32[]{:S(2)}, u32[]{:S(2)}) collective-permute-start(bf16[4,128,128]{2,1,0:T(8,128)(2,1)S(1)} %get-tuple-element.66), channel_id=1, source_target_pairs={{0,16},{8,24},{16,0},{24,8},{32,48},{40,56},{48,32},{56,40},{64,80... | collective-permute-start | bytes 393224 | tf_op jit(solution)/shard_map/ppermute | solution.py:55
  117.8 1.2 collective-permute-start.21
  119.0 0.6 collective-permute-done.19.refs_0_
  119.6 4.1 %collective-permute-done.20.refs_1_ = bf16[4,128,128]{2,1,0:T(8,128)(2,1)S(1)} collective-permute-done((bf16[4,128,128]{2,1,0:T(8,128)(2,1)S(1)}, bf16[4,128,128]{2,1,0:T(8,128)(2,1)S(1)}, u32[]{:S(2)}, u32[]{:S(2)}) %collective-permute-start.20) | collective-permute-done | bytes 131104 | tf_op jit(solution)/shard_map/ppermute | solution.py:55
  123.9 1.0 copy-done.6
  124.9 1.9 %all-to-all-done.2.same_ref = bf16[8,2,128,128]{3,2,1,0:T(8,128)(2,1)} async-done(((bf16[8,2,128,128]{3,2,1,0:T(8,128)(2,1)}), bf16[8,2,128,128]{3,2,1,0:T(8,128)(2,1)}, u32[]{:S(2)}, u32[]{:S(2)}) %all-to-all-start.2) | async-done | bytes 524320 | tf_op jit(solution)/shard_map/all_to_all | solution.py:45
  126.8 6.9 %all-to-all-start.4 = ((bf16[8,4,128,128]{3,2,1,0:T(8,128)(2,1)}), bf16[8,4,128,128]{3,2,1,0:T(8,128)(2,1)}, u32[]{:S(2)}, u32[]{:S(2)}) async-start(bf16[8,4,128,128]{3,2,1,0:T(8,128)(2,1)} %copy-done.6), calls=%async_computation.4 | async-start | bytes 2097152 | tf_op jit(solution)/shard_map/all_to_all | solution.py:346
  133.7 0.2 collective-permute-start.15
  133.9 3.4 %shard_map.88 = (bf16[5,4,128,128]{3,2,1,0:T(8,128)(2,1)S(1)}, bf16[5,4,128,128]{3,2,1,0:T(8,128)(2,1)S(1)}, f32[8,128]{1,0:T(8,128)}) custom-call(s32[38]{0:T(128)S(1)} %get-tuple-element.40.at_ref, bf16[8,128,512]{2,1,0:T(8,128)(2,1)S(1)} %copy-done.1, bf16[8,128,512]{2,1,0:T(8,128)(2,1)} %collective-permute-done.7.refs_1_, ...), custom_call_target="tpu_custom_call" | custom-call | flops 536870912 | bytes 6291456 | tf_op jit(solution)/shard_map/pallas_call | solution.py:266
  137.3 0.3 collective-permute-start.22
  137.6 1.8 %shard_map.83 = (f32[512,128]{1,0:T(8,128)S(1)}, bf16[512,128]{1,0:T(8,128)(2,1)S(1)}, bf16[512,128]{1,0:T(8,128)(2,1)S(1)}, bf16[512,128]{1,0:T(8,128)(2,1)S(1)}) custom-call(s32[38]{0:T(128)S(1)} %get-tuple-element.40.at_ref, bf16[8,2,128,128]{3,2,1,0:T(8,128)(2,1)} %all-to-all-done.2.same_ref, ...), custom_call_target="tpu_custom_call" | custom-call | flops 536870912 | bytes 4194304 | tf_op jit(solution)/shard_map/pallas_call | solution.py:353
  139.4 3.6 %collective-permute-start.16 = (bf16[512,128]{1,0:T(8,128)(2,1)S(1)}, bf16[512,128]{1,0:T(8,128)(2,1)S(1)}, u32[]{:S(2)}, u32[]{:S(2)}) collective-permute-start(bf16[512,128]{1,0:T(8,128)(2,1)S(1)} %get-tuple-element.61), channel_id=1, source_target_pairs={{0,8},{8,16},{16,24},{24,0},{32,40},{40,48},{48,56},{56,32},{64,72... | collective-permute-start | bytes 393224 | tf_op jit(solution)/shard_map/ppermute | solution.py:55
  143.0 2.4 %collective-permute-start.17 = (bf16[512,128]{1,0:T(8,128)(2,1)S(1)}, bf16[512,128]{1,0:T(8,128)(2,1)S(1)}, u32[]{:S(2)}, u32[]{:S(2)}) collective-permute-start(bf16[512,128]{1,0:T(8,128)(2,1)S(1)} %get-tuple-element.62), channel_id=1, source_target_pairs={{0,16},{8,24},{16,0},{24,8},{32,48},{40,56},{48,32},{56,40},{64,80... | collective-permute-start | bytes 393224 | tf_op jit(solution)/shard_map/ppermute | solution.py:55
  145.3 1.2 collective-permute-start.18
  146.7 1.5 collective-permute-start.23
  148.1 2.4 %collective-permute-start.24 = (bf16[4,128,128]{2,1,0:T(8,128)(2,1)S(1)}, bf16[4,128,128]{2,1,0:T(8,128)(2,1)S(1)}, u32[]{:S(2)}, u32[]{:S(2)}) collective-permute-start(bf16[4,128,128]{2,1,0:T(8,128)(2,1)S(1)} %get-tuple-element.74), channel_id=1, source_target_pairs={{0,4},{1,5},{2,6},{3,7},{4,0},{5,1},{6,2},{7,3},{8,12},{9,13},{10,... | collective-permute-start | bytes 393224 | tf_op jit(solution)/shard_map/ppermute | solution.py:60
  150.5 1.2 collective-permute-start.25
  151.8 1.6 %shard_map.84 = f32[512,128]{1,0:T(8,128)} custom-call(s32[38]{0:T(128)S(1)} %get-tuple-element.40.at_ref, s32[32,32]{1,0:T(8,128)S(1)} %copy-done.10, f32[512,128]{1,0:T(8,128)S(1)} %copy-done.9, f32[512,128]{1,0:T(8,128)S(1)} %get-tuple-element.60.refs_0_, bf16[512,128]{1,0:T(8,128)(2,1)S(1)} %collective-permute-done.16.refs_1_, ...), custom_call_target="tpu_custom_call" | custom-call | bytes 1048576 | tf_op jit(solution)/shard_map/pallas_call | solution.py:360
  153.3 2.7 %shard_map.87.own_ref = f32[512,128]{1,0:T(8,128)S(1)} custom-call(s32[38]{0:T(128)S(1)} %get-tuple-element.40.at_ref, bf16[8,128,512]{2,1,0:T(8,128)(2,1)S(1)} %copy-done.1, bf16[8,128,512]{2,1,0:T(8,128)(2,1)} %collective-permute-done.7.refs_1_, bf16[4,128,512]{2,1,0:T(8,128)(2,1)S(1)} %copy-done.3, ...), custom_call_target="tpu_custom_call" | custom-call | flops 536870912 | bytes 6291456 | tf_op jit(solution)/shard_map/pallas_call | solution.py:266
  156.1 0.8 shard_map.90
  (47 shorter events, 0.6 us)
Async XLA Ops:
  4.3 5.1 %copy-start.8 = (f32[512,128]{1,0:T(8,128)S(1)}, f32[512,128]{1,0:T(8,128)}, u32[]{:S(2)}) copy-start(f32[512,128]{1,0:T(8,128)} %cotangent_ref) | copy-start | bytes 786436
  4.3 5.1 %copy-start.10 = (s32[32,32]{1,0:T(8,128)S(1)}, s32[32,32]{1,0:T(8,128)}, u32[]{:S(2)}) copy-start(s32[32,32]{1,0:T(8,128)} %fill_ref.3) | copy-start | bytes 12292
  4.3 5.1 %copy-start.11 = (s32[32]{0:T(128)S(1)}, s32[32]{0:T(128)}, u32[]{:S(2)}) copy-start(s32[32]{0:T(128)} %owner_ref.1) | copy-start | bytes 388
  4.3 33.7 %all-to-all-start = ((bf16[4,1536,128]{2,1,0:T(8,128)(2,1)}), bf16[4,1536,128]{2,1,0:T(8,128)(2,1)S(1)}, u32[]{:S(2)}, u32[]{:S(2)}) async-start(bf16[4,1536,128]{2,1,0:T(8,128)(2,1)} %shard_map.77), calls=%async_computation | async-start | bytes 3145728 | tf_op jit(solution)/shard_map/all_to_all | solution.py:41
  10.9 9.2 %collective-permute-start.3 = (bf16[128,512]{1,0:T(8,128)(2,1)S(1)}, bf16[128,512]{1,0:T(8,128)(2,1)S(1)}, u32[]{:S(2)}, u32[]{:S(2)}) collective-permute-start(bf16[128,512]{1,0:T(8,128)(2,1)S(1)} %get-tuple-element.42), channel_id=1, source_target_pairs={{0,192},{8,200},{16,208},{24,216},{32,224},{40,232},{48,240},{56,2... | collective-permute-start | bytes 393224 | tf_op jit(solution)/shard_map/ppermute | solution.py:50
  17.0 7.7 %collective-permute-start.2 = (bf16[128,512]{1,0:T(8,128)(2,1)S(1)}, bf16[128,512]{1,0:T(8,128)(2,1)S(1)}, u32[]{:S(2)}, u32[]{:S(2)}) collective-permute-start(bf16[128,512]{1,0:T(8,128)(2,1)S(1)} %get-tuple-element.42), channel_id=1, source_target_pairs={{0,64},{8,72},{16,80},{24,88},{32,96},{40,104},{48,112},{56,120},{... | collective-permute-start | bytes 393224 | tf_op jit(solution)/shard_map/ppermute | solution.py:50
  17.0 8.4 %collective-permute-start.1 = (bf16[128,512]{1,0:T(8,128)(2,1)S(1)}, bf16[128,512]{1,0:T(8,128)(2,1)S(1)}, u32[]{:S(2)}, u32[]{:S(2)}) collective-permute-start(bf16[128,512]{1,0:T(8,128)(2,1)S(1)} %get-tuple-element.42), channel_id=1, source_target_pairs={{0,224},{8,232},{16,240},{24,248},{32,0},{40,8},{48,16},{56,24},{6... | collective-permute-start | bytes 393224 | tf_op jit(solution)/shard_map/ppermute | solution.py:50
  20.1 8.9 %collective-permute-start = (bf16[128,512]{1,0:T(8,128)(2,1)S(1)}, bf16[128,512]{1,0:T(8,128)(2,1)S(1)}, u32[]{:S(2)}, u32[]{:S(2)}) collective-permute-start(bf16[128,512]{1,0:T(8,128)(2,1)S(1)} %get-tuple-element.42), channel_id=1, source_target_pairs={{0,32},{8,40},{16,48},{24,56},{32,64},{40,72},{48,80},{56,88},{64,... | collective-permute-start | bytes 393224 | tf_op jit(solution)/shard_map/ppermute | solution.py:50
  29.0 6.9 %collective-permute-start.6 = (bf16[128,512]{1,0:T(8,128)(2,1)S(1)}, bf16[128,512]{1,0:T(8,128)(2,1)S(1)}, u32[]{:S(2)}, u32[]{:S(2)}) collective-permute-start(bf16[128,512]{1,0:T(8,128)(2,1)S(1)} %collective-permute-done.3), channel_id=1, source_target_pairs={{0,192},{8,200},{16,208},{24,216},{32,224},{40,232},{48,240},{56,2... | collective-permute-start | bytes 393224 | tf_op jit(solution)/shard_map/ppermute | solution.py:50
  29.0 9.0 %collective-permute-start.5 = (bf16[128,512]{1,0:T(8,128)(2,1)S(1)}, bf16[128,512]{1,0:T(8,128)(2,1)}, u32[]{:S(2)}, u32[]{:S(2)}) collective-permute-start(bf16[128,512]{1,0:T(8,128)(2,1)S(1)} %collective-permute-done.3), channel_id=1, source_target_pairs={{0,224},{8,232},{16,240},{24,248},{32,0},{40,8},{48,16},{56,24},{6... | collective-permute-start | bytes 393224 | tf_op jit(solution)/shard_map/ppermute | solution.py:50
  29.1 5.0 %collective-permute-start.4 = (bf16[128,512]{1,0:T(8,128)(2,1)S(1)}, bf16[128,512]{1,0:T(8,128)(2,1)S(1)}, u32[]{:S(2)}, u32[]{:S(2)}) collective-permute-start(bf16[128,512]{1,0:T(8,128)(2,1)S(1)} %collective-permute-done.2), channel_id=1, source_target_pairs={{0,32},{8,40},{16,48},{24,56},{32,64},{40,72},{48,80},{56,88},{64,... | collective-permute-start | bytes 393224 | tf_op jit(solution)/shard_map/ppermute | solution.py:50
  38.7 1.0 copy-start.4
  39.7 33.7 %all-to-all-start.1 = ((bf16[8,512,128]{2,1,0:T(8,128)(2,1)}), bf16[8,512,128]{2,1,0:T(8,128)(2,1)}, u32[]{:S(2)}, u32[]{:S(2)}) async-start(bf16[8,512,128]{2,1,0:T(8,128)(2,1)} %copy-done.4), calls=%async_computation.1 | async-start | bytes 2097152 | tf_op jit(solution)/shard_map/all_to_all | solution.py:45
  45.1 30.6 %copy-start = (bf16[8,128,512]{2,1,0:T(8,128)(2,1)}, bf16[8,128,512]{2,1,0:T(8,128)(2,1)S(1)}, u32[]{:S(2)}) copy-start(bf16[8,128,512]{2,1,0:T(8,128)(2,1)S(1)} %bitcast_dynamic-update-slice_fusion.refs_0_) | copy-start | bytes 3145732
  45.2 23.9 %collective-permute-start.8 = (bf16[8,128,512]{2,1,0:T(8,128)(2,1)S(1)}, bf16[8,128,512]{2,1,0:T(8,128)(2,1)}, u32[]{:S(2)}, u32[]{:S(2)}) collective-permute-start(bf16[8,128,512]{2,1,0:T(8,128)(2,1)S(1)} %bitcast_dynamic-update-slice_fusion.refs_0_), channel_id=1, source_target_pairs={{0,8},{8,16},{16,24},{24,0},{32,40},{40,48},{48,56},{56,32},{64,72... | collective-permute-start | bytes 3145736 | tf_op jit(solution)/shard_map/ppermute | solution.py:55
  46.6 22.5 %collective-permute-start.7 = (bf16[8,128,512]{2,1,0:T(8,128)(2,1)S(1)}, bf16[8,128,512]{2,1,0:T(8,128)(2,1)}, u32[]{:S(2)}, u32[]{:S(2)}) collective-permute-start(bf16[8,128,512]{2,1,0:T(8,128)(2,1)S(1)} %bitcast_dynamic-update-slice_fusion.refs_0_), channel_id=1, source_target_pairs={{0,24},{8,0},{16,8},{24,16},{32,56},{40,32},{48,40},{56,48},{64,88... | collective-permute-start | bytes 3145736 | tf_op jit(solution)/shard_map/ppermute | solution.py:55
  74.8 1.0 copy-start.7
  75.8 31.1 %all-to-all-start.3 = ((bf16[8,512,128]{2,1,0:T(8,128)(2,1)}), bf16[8,512,128]{2,1,0:T(8,128)(2,1)S(1)}, u32[]{:S(2)}, u32[]{:S(2)}) async-start(bf16[8,512,128]{2,1,0:T(8,128)(2,1)} %copy-done.7), calls=%async_computation.3 | async-start | bytes 2097152 | tf_op jit(solution)/shard_map/all_to_all | solution.py:45
  81.5 11.7 %collective-permute-start.13 = (bf16[4,128,512]{2,1,0:T(8,128)(2,1)S(1)}, bf16[4,128,512]{2,1,0:T(8,128)(2,1)S(1)}, u32[]{:S(2)}, u32[]{:S(2)}) collective-permute-start(bf16[4,128,512]{2,1,0:T(8,128)(2,1)S(1)} %slice.7), channel_id=1, source_target_pairs={{0,24},{8,0},{16,8},{24,16},{32,56},{40,32},{48,40},{56,48},{64,88... | collective-permute-start | bytes 1572872 | tf_op jit(solution)/shard_map/ppermute | solution.py:55
  84.2 12.2 %collective-permute-start.12 = (bf16[4,128,512]{2,1,0:T(8,128)(2,1)S(1)}, bf16[4,128,512]{2,1,0:T(8,128)(2,1)S(1)}, u32[]{:S(2)}, u32[]{:S(2)}) collective-permute-start(bf16[4,128,512]{2,1,0:T(8,128)(2,1)S(1)} %slice.6), channel_id=1, source_target_pairs={{0,8},{8,16},{16,24},{24,0},{32,40},{40,48},{48,56},{56,32},{64,72... | collective-permute-start | bytes 1572872 | tf_op jit(solution)/shard_map/ppermute | solution.py:55
  84.2 5.6 %collective-permute-start.11 = (bf16[512,128]{1,0:T(8,128)(2,1)S(1)}, bf16[512,128]{1,0:T(8,128)(2,1)S(1)}, u32[]{:S(2)}, u32[]{:S(2)}) collective-permute-start(bf16[512,128]{1,0:T(8,128)(2,1)S(1)} %get-tuple-element.56), channel_id=1, source_target_pairs={{0,2},{1,3},{2,4},{3,5},{4,6},{5,7},{6,0},{7,1},{8,10},{9,11},{10,... | collective-permute-start | bytes 393224 | tf_op jit(solution)/shard_map/ppermute | solution.py:60
  85.5 6.9 %collective-permute-start.10 = (bf16[512,128]{1,0:T(8,128)(2,1)S(1)}, bf16[512,128]{1,0:T(8,128)(2,1)S(1)}, u32[]{:S(2)}, u32[]{:S(2)}) collective-permute-start(bf16[512,128]{1,0:T(8,128)(2,1)S(1)} %get-tuple-element.56), channel_id=1, source_target_pairs={{0,4},{1,5},{2,6},{3,7},{4,0},{5,1},{6,2},{7,3},{8,12},{9,13},{10,... | collective-permute-start | bytes 393224 | tf_op jit(solution)/shard_map/ppermute | solution.py:60
  88.3 4.7 %collective-permute-start.9 = (bf16[512,128]{1,0:T(8,128)(2,1)S(1)}, bf16[512,128]{1,0:T(8,128)(2,1)S(1)}, u32[]{:S(2)}, u32[]{:S(2)}) collective-permute-start(bf16[512,128]{1,0:T(8,128)(2,1)S(1)} %get-tuple-element.56), channel_id=1, source_target_pairs={{0,6},{1,7},{2,0},{3,1},{4,2},{5,3},{6,4},{7,5},{8,14},{9,15},{10,... | collective-permute-start | bytes 393224 | tf_op jit(solution)/shard_map/ppermute | solution.py:60
  96.4 0.8 copy-start.2
  97.2 4.9 %collective-permute-start.14 = (bf16[4,4,128,128]{3,2,1,0:T(8,128)(2,1)S(1)}, bf16[4,4,128,128]{3,2,1,0:T(8,128)(2,1)S(1)}, u32[]{:S(2)}, u32[]{:S(2)}) collective-permute-start(bf16[4,4,128,128]{3,2,1,0:T(8,128)(2,1)S(1)} %shard_map.81.same_ref), channel_id=1, source_target_pairs={{0,1},{1,0},{2,3},{3,2},{4,5},{5,4},{6,7},{7,6},{8,9},{9,8},{10,11... | collective-permute-start | bytes 1572872 | tf_op jit(solution)/shard_map/ppermute | solution.py:64
  103.0 0.8 copy-start.5
  106.9 19.9 %all-to-all-start.2 = ((bf16[8,2,128,128]{3,2,1,0:T(8,128)(2,1)}), bf16[8,2,128,128]{3,2,1,0:T(8,128)(2,1)}, u32[]{:S(2)}, u32[]{:S(2)}) async-start(bf16[8,2,128,128]{3,2,1,0:T(8,128)(2,1)} %bitcast.27), calls=%async_computation.2 | async-start | bytes 1048576 | tf_op jit(solution)/shard_map/all_to_all | solution.py:45
  112.3 21.5 %copy-start.1 = (bf16[8,128,512]{2,1,0:T(8,128)(2,1)S(1)}, bf16[8,128,512]{2,1,0:T(8,128)(2,1)}, u32[]{:S(2)}) copy-start(bf16[8,128,512]{2,1,0:T(8,128)(2,1)} %copy-done) | copy-start | bytes 3145732
  112.4 21.5 %copy-start.3 = (bf16[4,128,512]{2,1,0:T(8,128)(2,1)S(1)}, bf16[4,128,512]{2,1,0:T(8,128)(2,1)}, u32[]{:S(2)}) copy-start(bf16[4,128,512]{2,1,0:T(8,128)(2,1)} %copy-done.2) | copy-start | bytes 1572868
  112.4 7.3 %collective-permute-start.19 = (bf16[4,128,128]{2,1,0:T(8,128)(2,1)S(1)}, bf16[4,128,128]{2,1,0:T(8,128)(2,1)S(1)}, u32[]{:S(2)}, u32[]{:S(2)}) collective-permute-start(bf16[4,128,128]{2,1,0:T(8,128)(2,1)S(1)} %get-tuple-element.65), channel_id=1, source_target_pairs={{0,8},{8,16},{16,24},{24,0},{32,40},{40,48},{48,56},{56,32},{64,72... | collective-permute-start | bytes 393224 | tf_op jit(solution)/shard_map/ppermute | solution.py:55
  115.4 8.4 %collective-permute-start.20 = (bf16[4,128,128]{2,1,0:T(8,128)(2,1)S(1)}, bf16[4,128,128]{2,1,0:T(8,128)(2,1)S(1)}, u32[]{:S(2)}, u32[]{:S(2)}) collective-permute-start(bf16[4,128,128]{2,1,0:T(8,128)(2,1)S(1)} %get-tuple-element.66), channel_id=1, source_target_pairs={{0,16},{8,24},{16,0},{24,8},{32,48},{40,56},{48,32},{56,40},{64,80... | collective-permute-start | bytes 393224 | tf_op jit(solution)/shard_map/ppermute | solution.py:55
  117.8 6.0 %collective-permute-start.21 = (bf16[4,128,128]{2,1,0:T(8,128)(2,1)S(1)}, bf16[4,128,128]{2,1,0:T(8,128)(2,1)S(1)}, u32[]{:S(2)}, u32[]{:S(2)}) collective-permute-start(bf16[4,128,128]{2,1,0:T(8,128)(2,1)S(1)} %get-tuple-element.67), channel_id=1, source_target_pairs={{0,24},{8,0},{16,8},{24,16},{32,56},{40,32},{48,40},{56,48},{64,88... | collective-permute-start | bytes 393224 | tf_op jit(solution)/shard_map/ppermute | solution.py:55
  123.9 1.0 copy-start.6
  126.8 26.6 %all-to-all-start.4 = ((bf16[8,4,128,128]{3,2,1,0:T(8,128)(2,1)}), bf16[8,4,128,128]{3,2,1,0:T(8,128)(2,1)}, u32[]{:S(2)}, u32[]{:S(2)}) async-start(bf16[8,4,128,128]{3,2,1,0:T(8,128)(2,1)} %copy-done.6), calls=%async_computation.4 | async-start | bytes 2097152 | tf_op jit(solution)/shard_map/all_to_all | solution.py:346
  133.7 3.9 %collective-permute-start.15 = (bf16[8,2,128,128]{3,2,1,0:T(8,128)(2,1)}, bf16[8,2,128,128]{3,2,1,0:T(8,128)(2,1)S(1)}, u32[]{:S(2)}, u32[]{:S(2)}) collective-permute-start(bf16[8,2,128,128]{3,2,1,0:T(8,128)(2,1)} %all-to-all-done.2.same_ref), channel_id=1, source_target_pairs={{0,1},{1,0},{2,3},{3,2},{4,5},{5,4},{6,7},{7,6},{8,9},{9,8},{10,11... | collective-permute-start | bytes 1572872 | tf_op jit(solution)/shard_map/ppermute | solution.py:64
  137.3 14.5 %copy-start.9 = (f32[512,128]{1,0:T(8,128)S(1)}, f32[512,128]{1,0:T(8,128)}, u32[]{:S(2)}) copy-start(f32[512,128]{1,0:T(8,128)} %trailing_ref.1) | copy-start | bytes 786436
  137.3 9.3 %collective-permute-start.22 = (bf16[5,4,128,128]{3,2,1,0:T(8,128)(2,1)S(1)}, bf16[5,4,128,128]{3,2,1,0:T(8,128)(2,1)S(1)}, u32[]{:S(2)}, u32[]{:S(2)}) collective-permute-start(bf16[5,4,128,128]{3,2,1,0:T(8,128)(2,1)S(1)} %get-tuple-element.71), channel_id=1, source_target_pairs={{0,1},{1,0},{2,3},{3,2},{4,5},{5,4},{6,7},{7,6},{8,9},{9,8},{10,11... | collective-permute-start | bytes 1966088 | tf_op jit(solution)/shard_map/ppermute | solution.py:64
  139.4 11.1 %collective-permute-start.16 = (bf16[512,128]{1,0:T(8,128)(2,1)S(1)}, bf16[512,128]{1,0:T(8,128)(2,1)S(1)}, u32[]{:S(2)}, u32[]{:S(2)}) collective-permute-start(bf16[512,128]{1,0:T(8,128)(2,1)S(1)} %get-tuple-element.61), channel_id=1, source_target_pairs={{0,8},{8,16},{16,24},{24,0},{32,40},{40,48},{48,56},{56,32},{64,72... | collective-permute-start | bytes 393224 | tf_op jit(solution)/shard_map/ppermute | solution.py:55
  143.0 8.8 %collective-permute-start.17 = (bf16[512,128]{1,0:T(8,128)(2,1)S(1)}, bf16[512,128]{1,0:T(8,128)(2,1)S(1)}, u32[]{:S(2)}, u32[]{:S(2)}) collective-permute-start(bf16[512,128]{1,0:T(8,128)(2,1)S(1)} %get-tuple-element.62), channel_id=1, source_target_pairs={{0,16},{8,24},{16,0},{24,8},{32,48},{40,56},{48,32},{56,40},{64,80... | collective-permute-start | bytes 393224 | tf_op jit(solution)/shard_map/ppermute | solution.py:55
  145.3 6.4 %collective-permute-start.18 = (bf16[512,128]{1,0:T(8,128)(2,1)S(1)}, bf16[512,128]{1,0:T(8,128)(2,1)S(1)}, u32[]{:S(2)}, u32[]{:S(2)}) collective-permute-start(bf16[512,128]{1,0:T(8,128)(2,1)S(1)} %get-tuple-element.63), channel_id=1, source_target_pairs={{0,24},{8,0},{16,8},{24,16},{32,56},{40,32},{48,40},{56,48},{64,88... | collective-permute-start | bytes 393224 | tf_op jit(solution)/shard_map/ppermute | solution.py:55
  146.7 9.4 %collective-permute-start.23 = (bf16[4,128,128]{2,1,0:T(8,128)(2,1)S(1)}, bf16[4,128,128]{2,1,0:T(8,128)(2,1)S(1)}, u32[]{:S(2)}, u32[]{:S(2)}) collective-permute-start(bf16[4,128,128]{2,1,0:T(8,128)(2,1)S(1)} %get-tuple-element.73), channel_id=1, source_target_pairs={{0,2},{1,3},{2,4},{3,5},{4,6},{5,7},{6,0},{7,1},{8,10},{9,11},{10,... | collective-permute-start | bytes 393224 | tf_op jit(solution)/shard_map/ppermute | solution.py:60
  148.1 7.9 %collective-permute-start.24 = (bf16[4,128,128]{2,1,0:T(8,128)(2,1)S(1)}, bf16[4,128,128]{2,1,0:T(8,128)(2,1)S(1)}, u32[]{:S(2)}, u32[]{:S(2)}) collective-permute-start(bf16[4,128,128]{2,1,0:T(8,128)(2,1)S(1)} %get-tuple-element.74), channel_id=1, source_target_pairs={{0,4},{1,5},{2,6},{3,7},{4,0},{5,1},{6,2},{7,3},{8,12},{9,13},{10,... | collective-permute-start | bytes 393224 | tf_op jit(solution)/shard_map/ppermute | solution.py:60
  150.5 5.5 %collective-permute-start.25 = (bf16[4,128,128]{2,1,0:T(8,128)(2,1)S(1)}, bf16[4,128,128]{2,1,0:T(8,128)(2,1)S(1)}, u32[]{:S(2)}, u32[]{:S(2)}) collective-permute-start(bf16[4,128,128]{2,1,0:T(8,128)(2,1)S(1)} %get-tuple-element.75), channel_id=1, source_target_pairs={{0,6},{1,7},{2,0},{3,1},{4,2},{5,3},{6,4},{7,5},{8,14},{9,15},{10,... | collective-permute-start | bytes 393224 | tf_op jit(solution)/shard_map/ppermute | solution.py:60

commit v5 on v4

--- a/solution.py
+++ b/solution.py
@@ -154,7 +154,7 @@
             outs[k][i] = block.astype(outs[k].dtype)
 
 
-def outer_kernel(at_ref, same_ref, other_ref, factor_ref, *outs):
+def outer_kernel(at_ref, same_ref, other_ref, factor_ref, after_ref, *outs):
     left = jnp.concatenate([factor_ref[z] for z in range(NZ)], axis=1)
     rows = []
     for k in range(NX):
@@ -294,13 +294,13 @@
         cost_estimate=pl.CostEstimate(flops=0, bytes_accessed=1 << 19, transcendentals=0),
     )(at, owner, fill, cotangent)
     u1, d1 = shift_z(weighted, 1), shift_z(weighted, -1)
-    u2, d2 = shift_z(weighted, 2), shift_z(weighted, -2)
-    u1, d1, u2, d2 = lax.optimization_barrier((u1, d1, u2, d2))
-    u3, d3, d4 = shift_z(u2, 1), shift_z(d2, -1), shift_z(d2, -2)
-    got, u1, u2, u3, d1, d2, d3, d4 = lax.optimization_barrier(
-        (exchange_x(sent), u1, u2, u3, d1, d2, d3, d4)
-    )
-    near = jnp.stack([weighted, d1, d2, d3, d4, u3, u2, u1])
+    u2, d2 = shift_z(u1, 1), shift_z(d1, -1)
+    u3, d3 = shift_z(u2, 1), shift_z(d2, -1)
+    half = BS // 2
+    d4 = jnp.concatenate([shift_z(u3[:half], 1), shift_z(d3[half:], -1)])
+    got, near = lax.optimization_barrier(
+        (exchange_x(sent), jnp.stack([weighted, d1, d2, d3, d4, u3, u2, u1]))
+    )
 
     tiles = jax.ShapeDtypeStruct((NZ, ROWS, BS), BF)
     partial = call(factor_kernel, tiles, [VMEM], 2 * 512 * 512 * 1024, 3 << 20)(got)
@@ -338,6 +338,7 @@
     keep, *leave = call(total_kernel, [total] + [tile] * 3, [VMEM] * 2, 0, 2 << 20)(
         same, swap_core(other)
     )
+    spread, after = lax.optimization_barrier((spread, after))
     own = sweep(
         own_kernel,
         jax.ShapeDtypeStruct((ROWS, BS), F32),
@@ -353,10 +354,10 @@
     outer = call(
         outer_kernel,
         [jax.ShapeDtypeStruct((ROWS, BS), F32), TILE, TILE, TILE],
-        [SMEM] + [VMEM] * 3,
+        [SMEM] + [VMEM] * 3 + [ANY],
         2 * 512 * 1024 * 512,
         4 << 20,
-    )(at, owned, swap_core(owned), factor_k)
+    )(at, owned, swap_core(owned), factor_k, after)
     updated = call(
         tail_kernel, jax.ShapeDtypeStruct((ROWS, BS), F32), [SMEM] * 2 + [VMEM] * 5, 0, 1 << 20
     )(at, fill, trailing, outer[0], *[shift_x(outer[k], k) for k in range(1, NX)])

time: 158 us -> 152 us (0.962)
  waiting for transfers between devices: 60.2 us -> 55.3 us
    ppermute x10, starting transfers between devices: 19.2 us -> 9.86 us  [shift_x(): return lax.ppermute(value, 'col', pairs)]
    ppermute x7 -> x8, waiting for transfers between devices: 16.4 us -> 9.39 us  [shift_z(): return lax.ppermute(value, 'col', pairs)]
    ppermute x6, waiting for transfers between devices: 3.62 us -> 8.8 us  [shift_y(): return lax.ppermute(value, 'row', pairs)]
    ppermute x7 -> x8, starting transfers between devices: 10.7 us -> 15.1 us  [shift_z(): return lax.ppermute(value, 'col', pairs)]
    ppermute x10, waiting for transfers between devices: 29.4 us -> 26.1 us  [shift_x(): return lax.ppermute(value, 'col', pairs)]
    ppermute x3, starting transfers between devices: 3.88 us -> 7.11 us  [swap_core(): return lax.ppermute(value, 'row', [(r, r ^ 1) for r in range(2 * NY)])]
    all_to_all x3, waiting for transfers between devices: 9.23 us -> 6.1 us  [exchange_z(): return lax.all_to_all(value, 'col', 0, 0, axis_index_groups=Z_GROUPS)]
    all_to_all x3, starting transfers between devices: 12.1 us -> 14.7 us  [exchange_z(): return lax.all_to_all(value, 'col', 0, 0, axis_index_groups=Z_GROUPS)]
  transfers between devices with their start and end apart: 31 -> 32, of which waited for: 19 -> 20; matrix products, arithmetic and copies ran while one was open for 2% -> 1% of each run, Pallas kernels for 9% -> 8%
where the time goes in v5:
time: 152 us; the launch traced here: 151 us
  starting transfers between devices  66.7 us (44%)
  waiting for transfers between devices  55.3 us (36%)
  Pallas kernels  20.2 us (13%)
  local copies, waits for them, and re-layouts  7.78 us (5%)
    ppermute x10, waiting for transfers between devices, shift_x(): return lax.ppermute(value, 'col', pairs)  26.1 us
    ppermute x8, starting transfers between devices, shift_z(): return lax.ppermute(value, 'col', pairs)  15.1 us
    all_to_all x3, starting transfers between devices, exchange_z(): return lax.all_to_all(value, 'col', 0, 0, axis_index_groups=Z_GROUPS)  14.7 us
    ppermute x6, starting transfers between devices, shift_y(): return lax.ppermute(value, 'row', pairs)  10 us
    ppermute x10, starting transfers between devices, shift_x(): return lax.ppermute(value, 'col', pairs)  9.86 us
    ppermute x8, waiting for transfers between devices, shift_z(): return lax.ppermute(value, 'col', pairs)  9.39 us
    ppermute x6, waiting for transfers between devices, shift_y(): return lax.ppermute(value, 'row', pairs)  8.8 us
    ppermute x3, starting transfers between devices, swap_core(): return lax.ppermute(value, 'row', [(r, r ^ 1) for r in range(2 * NY)])  7.11 us
  transfers between devices with their start and end apart: 32, of which 20 were waited for; matrix products, arithmetic and copies ran while one was open for 1% of the time, Pallas kernels for 8%

profile of v5, /device:TPU:1, one launch (start us, length us, event | category | flops | bytes accessed | tf_op | source)
XLA Modules:
  0.0 151.0 jit_solution(8852255208037525746)
XLA Ops:
  0.7 3.7 %shard_map.77 = bf16[4,1536,128]{2,1,0:T(8,128)(2,1)} custom-call(bf16[512,128]{1,0:T(8,128)(2,1)} %panel_ref.1, bf16[128,4096]{1,0:T(8,128)(2,1)} %refs_7_.1, bf16[128,4096]{1,0:T(8,128)(2,1)} %refs_7_.1, bf16[128,4096]{1,0:T(8,128)(2,1)} %refs_7_.1, bf16[128,4096]{1,0:T(8,128)(2,1)} %refs_7_.1, bf16[128,4096]{1,0:T(8,128)(2,1)} %refs_7_.1, ...), custom_call_target="tpu_custom_call" | custom-call | bytes 3145728 | tf_op jit(solution)/shard_map/pallas_call | solution.py:275
  4.5 1.5 shard_map.78
  6.0 6.5 %collective-permute-start = (bf16[128,512]{1,0:T(8,128)(2,1)S(1)}, bf16[128,512]{1,0:T(8,128)(2,1)S(1)}, u32[]{:S(2)}, u32[]{:S(2)}) collective-permute-start(bf16[128,512]{1,0:T(8,128)(2,1)S(1)} %get-tuple-element.35), channel_id=1, source_target_pairs={{0,224},{8,232},{16,240},{24,248},{32,0},{40,8},{48,16},{56,24},{6... | collective-permute-start | bytes 393224 | tf_op jit(solution)/shard_map/ppermute | solution.py:50
  12.5 4.0 %all-to-all-start = ((bf16[4,1536,128]{2,1,0:T(8,128)(2,1)}), bf16[4,1536,128]{2,1,0:T(8,128)(2,1)S(1)}, u32[]{:S(2)}, u32[]{:S(2)}) async-start(bf16[4,1536,128]{2,1,0:T(8,128)(2,1)} %shard_map.77), calls=%async_computation | async-start | bytes 3145728 | tf_op jit(solution)/shard_map/all_to_all | solution.py:41
  16.5 2.7 %collective-permute-start.1 = (bf16[128,512]{1,0:T(8,128)(2,1)S(1)}, bf16[128,512]{1,0:T(8,128)(2,1)S(1)}, u32[]{:S(2)}, u32[]{:S(2)}) collective-permute-start(bf16[128,512]{1,0:T(8,128)(2,1)S(1)} %collective-permute-done), channel_id=1, source_target_pairs={{0,224},{8,232},{16,240},{24,248},{32,0},{40,8},{48,16},{56,24},{6... | collective-permute-start | bytes 393224 | tf_op jit(solution)/shard_map/ppermute | solution.py:50
  19.3 1.9 %collective-permute-done.1 = bf16[128,512]{1,0:T(8,128)(2,1)S(1)} collective-permute-done((bf16[128,512]{1,0:T(8,128)(2,1)S(1)}, bf16[128,512]{1,0:T(8,128)(2,1)S(1)}, u32[]{:S(2)}, u32[]{:S(2)}) %collective-permute-start.1) | collective-permute-done | bytes 131104 | tf_op jit(solution)/shard_map/ppermute | solution.py:50
  21.2 3.1 %collective-permute-start.2 = (bf16[128,512]{1,0:T(8,128)(2,1)S(1)}, bf16[128,512]{1,0:T(8,128)(2,1)S(1)}, u32[]{:S(2)}, u32[]{:S(2)}) collective-permute-start(bf16[128,512]{1,0:T(8,128)(2,1)S(1)} %collective-permute-done.1), channel_id=1, source_target_pairs={{0,224},{8,232},{16,240},{24,248},{32,0},{40,8},{48,16},{56,24},{6... | collective-permute-start | bytes 393224 | tf_op jit(solution)/shard_map/ppermute | solution.py:50
  24.3 0.3 collective-permute-done.4
  24.6 5.3 %collective-permute-done.5 = bf16[128,512]{1,0:T(8,128)(2,1)S(1)} collective-permute-done((bf16[128,512]{1,0:T(8,128)(2,1)S(1)}, bf16[128,512]{1,0:T(8,128)(2,1)S(1)}, u32[]{:S(2)}, u32[]{:S(2)}) %collective-permute-start.5) | collective-permute-done | bytes 131104 | tf_op jit(solution)/shard_map/ppermute | solution.py:50
  29.9 2.7 %collective-permute-start.7 = (bf16[64,512]{1,0:T(8,128)(2,1)S(1)}, bf16[64,512]{1,0:T(8,128)(2,1)S(1)}, u32[]{:S(2)}, u32[]{:S(2)}) collective-permute-start(bf16[64,512]{1,0:T(8,128)(2,1)S(1)} %slice.17), channel_id=1, source_target_pairs={{0,224},{8,232},{16,240},{24,248},{32,0},{40,8},{48,16},{56,24},{6... | collective-permute-start | bytes 196616 | tf_op jit(solution)/shard_map/ppermute | solution.py:50
  32.7 1.8 %collective-permute-done.6 = bf16[64,512]{1,0:T(8,128)(2,1)S(1)} collective-permute-done((bf16[64,512]{1,0:T(8,128)(2,1)S(1)}, bf16[64,512]{1,0:T(8,128)(2,1)S(1)}, u32[]{:S(2)}, u32[]{:S(2)}) %collective-permute-start.6) | collective-permute-done | bytes 65568 | tf_op jit(solution)/shard_map/ppermute | solution.py:50
  34.6 1.4 all-to-all-done.got_ref
  36.0 0.7 shard_map.79
  36.7 1.0 copy-done.6
  37.7 4.2 %all-to-all-start.1 = ((bf16[8,512,128]{2,1,0:T(8,128)(2,1)}), bf16[8,512,128]{2,1,0:T(8,128)(2,1)}, u32[]{:S(2)}, u32[]{:S(2)}) async-start(bf16[8,512,128]{2,1,0:T(8,128)(2,1)} %copy-done.6), calls=%async_computation.1 | async-start | bytes 2097152 | tf_op jit(solution)/shard_map/all_to_all | solution.py:45
  42.0 1.4 collective-permute-start.8
  43.4 0.1 collective-permute-start.9
  43.5 20.0 %collective-permute-done.8.refs_1_ = bf16[8,128,512]{2,1,0:T(8,128)(2,1)} collective-permute-done((bf16[8,128,512]{2,1,0:T(8,128)(2,1)S(1)}, bf16[8,128,512]{2,1,0:T(8,128)(2,1)}, u32[]{:S(2)}, u32[]{:S(2)}) %collective-permute-start.8) | collective-permute-done | bytes 1048608 | tf_op jit(solution)/shard_map/ppermute | solution.py:55
  63.5 0.6 collective-permute-done.9.refs_4_
  64.1 4.4 %all-to-all-done.1.parts_ref = bf16[8,512,128]{2,1,0:T(8,128)(2,1)} async-done(((bf16[8,512,128]{2,1,0:T(8,128)(2,1)}), bf16[8,512,128]{2,1,0:T(8,128)(2,1)}, u32[]{:S(2)}, u32[]{:S(2)}) %all-to-all-start.1) | async-done | bytes 1048608 | tf_op jit(solution)/shard_map/all_to_all | solution.py:45
  68.5 1.4 shard_map.80
  69.9 1.0 copy-done.9
  70.9 3.6 %all-to-all-start.3 = ((bf16[8,512,128]{2,1,0:T(8,128)(2,1)}), bf16[8,512,128]{2,1,0:T(8,128)(2,1)S(1)}, u32[]{:S(2)}, u32[]{:S(2)}) async-start(bf16[8,512,128]{2,1,0:T(8,128)(2,1)} %copy-done.9), calls=%async_computation.3 | async-start | bytes 2097152 | tf_op jit(solution)/shard_map/all_to_all | solution.py:45
  74.5 1.1 slice.14
  75.6 1.1 slice.15
  76.7 2.7 %collective-permute-start.14 = (bf16[4,128,512]{2,1,0:T(8,128)(2,1)S(1)}, bf16[4,128,512]{2,1,0:T(8,128)(2,1)S(1)}, u32[]{:S(2)}, u32[]{:S(2)}) collective-permute-start(bf16[4,128,512]{2,1,0:T(8,128)(2,1)S(1)} %slice.15), channel_id=1, source_target_pairs={{0,24},{8,0},{16,8},{24,16},{32,56},{40,32},{48,40},{56,48},{64,88... | collective-permute-start | bytes 1572872 | tf_op jit(solution)/shard_map/ppermute | solution.py:55
  79.5 2.7 %collective-permute-start.10 = (bf16[512,128]{1,0:T(8,128)(2,1)S(1)}, bf16[512,128]{1,0:T(8,128)(2,1)S(1)}, u32[]{:S(2)}, u32[]{:S(2)}) collective-permute-start(bf16[512,128]{1,0:T(8,128)(2,1)S(1)} %get-tuple-element.39), channel_id=1, source_target_pairs={{0,6},{1,7},{2,0},{3,1},{4,2},{5,3},{6,4},{7,5},{8,14},{9,15},{10,... | collective-permute-start | bytes 393224 | tf_op jit(solution)/shard_map/ppermute | solution.py:60
  82.2 0.3 collective-permute-start.11
  82.5 0.7 collective-permute-start.12
  83.2 2.3 %collective-permute-done.10 = bf16[512,128]{1,0:T(8,128)(2,1)S(1)} collective-permute-done((bf16[512,128]{1,0:T(8,128)(2,1)S(1)}, bf16[512,128]{1,0:T(8,128)(2,1)S(1)}, u32[]{:S(2)}, u32[]{:S(2)}) %collective-permute-start.10) | collective-permute-done | bytes 131104 | tf_op jit(solution)/shard_map/ppermute | solution.py:60
  85.5 2.3 %collective-permute-done.11 = bf16[512,128]{1,0:T(8,128)(2,1)S(1)} collective-permute-done((bf16[512,128]{1,0:T(8,128)(2,1)S(1)}, bf16[512,128]{1,0:T(8,128)(2,1)S(1)}, u32[]{:S(2)}, u32[]{:S(2)}) %collective-permute-start.11) | collective-permute-done | bytes 131104 | tf_op jit(solution)/shard_map/ppermute | solution.py:60
  87.8 1.4 collective-permute-done.12
  89.3 0.8 copy-done.3
  90.1 6.6 %collective-permute-start.15 = (bf16[4,4,128,128]{3,2,1,0:T(8,128)(2,1)S(1)}, bf16[4,4,128,128]{3,2,1,0:T(8,128)(2,1)S(1)}, u32[]{:S(2)}, u32[]{:S(2)}) collective-permute-start(bf16[4,4,128,128]{3,2,1,0:T(8,128)(2,1)S(1)} %shard_map.81.same_ref), channel_id=1, source_target_pairs={{0,1},{1,0},{2,3},{3,2},{4,5},{5,4},{6,7},{7,6},{8,9},{9,8},{10,11... | collective-permute-start | bytes 1572872 | tf_op jit(solution)/shard_map/ppermute | solution.py:64
  96.7 1.5 %collective-permute-done.15.other_ref = bf16[4,4,128,128]{3,2,1,0:T(8,128)(2,1)S(1)} collective-permute-done((bf16[4,4,128,128]{3,2,1,0:T(8,128)(2,1)S(1)}, bf16[4,4,128,128]{3,2,1,0:T(8,128)(2,1)S(1)}, u32[]{:S(2)}, u32[]{:S(2)}) %collective-permute-start.15) | collective-permute-done | bytes 524320 | tf_op jit(solution)/shard_map/ppermute | solution.py:64
  98.2 0.9 shard_map.82
  99.1 0.8 copy-done.7
  99.9 6.9 %all-to-all-start.2 = ((bf16[8,2,128,128]{3,2,1,0:T(8,128)(2,1)}), bf16[8,2,128,128]{3,2,1,0:T(8,128)(2,1)}, u32[]{:S(2)}, u32[]{:S(2)}) async-start(bf16[8,2,128,128]{3,2,1,0:T(8,128)(2,1)} %bitcast.29), calls=%async_computation.2 | async-start | bytes 1048576 | tf_op jit(solution)/shard_map/all_to_all | solution.py:45
  106.8 1.3 shard_map.83
  108.2 1.0 collective-permute-start.18
  109.2 1.7 %collective-permute-start.19 = (bf16[4,128,128]{2,1,0:T(8,128)(2,1)S(1)}, bf16[4,128,128]{2,1,0:T(8,128)(2,1)S(1)}, u32[]{:S(2)}, u32[]{:S(2)}) collective-permute-start(bf16[4,128,128]{2,1,0:T(8,128)(2,1)S(1)} %get-tuple-element.46), channel_id=1, source_target_pairs={{0,24},{8,0},{16,8},{24,16},{32,56},{40,32},{48,40},{56,48},{64,88... | collective-permute-start | bytes 393224 | tf_op jit(solution)/shard_map/ppermute | solution.py:55
  110.9 4.1 %collective-permute-done.17.refs_0_ = bf16[4,128,128]{2,1,0:T(8,128)(2,1)S(1)} collective-permute-done((bf16[4,128,128]{2,1,0:T(8,128)(2,1)S(1)}, bf16[4,128,128]{2,1,0:T(8,128)(2,1)S(1)}, u32[]{:S(2)}, u32[]{:S(2)}) %collective-permute-start.17) | collective-permute-done | bytes 131104 | tf_op jit(solution)/shard_map/ppermute | solution.py:55
  115.0 0.4 collective-permute-done.18.refs_1_
  115.4 0.8 collective-permute-done.19.refs_2_
  116.3 1.0 copy-done.8
  117.3 3.6 %shard_map.85 = (bf16[5,4,128,128]{3,2,1,0:T(8,128)(2,1)S(1)}, bf16[5,4,128,128]{3,2,1,0:T(8,128)(2,1)}, f32[8,128]{1,0:T(8,128)S(1)}) custom-call(s32[38]{0:T(128)S(1)} %get-tuple-element.33.at_ref, bf16[8,128,512]{2,1,0:T(8,128)(2,1)S(1)} %copy-done.1, bf16[8,128,512]{2,1,0:T(8,128)(2,1)} %collective-permute-done.8.refs_1_, ...), custom_call_target="tpu_custom_call" | custom-call | flops 536870912 | bytes 6291456 | tf_op jit(solution)/shard_map/pallas_call | solution.py:266
  121.0 0.9 copy-done.10
  121.8 1.7 %all-to-all-done.2.same_ref = bf16[8,2,128,128]{3,2,1,0:T(8,128)(2,1)} async-done(((bf16[8,2,128,128]{3,2,1,0:T(8,128)(2,1)}), bf16[8,2,128,128]{3,2,1,0:T(8,128)(2,1)}, u32[]{:S(2)}, u32[]{:S(2)}) %all-to-all-start.2) | async-done | bytes 524320 | tf_op jit(solution)/shard_map/all_to_all | solution.py:45
  123.6 5.9 %all-to-all-start.4 = ((bf16[8,4,128,128]{3,2,1,0:T(8,128)(2,1)}), bf16[8,4,128,128]{3,2,1,0:T(8,128)(2,1)}, u32[]{:S(2)}, u32[]{:S(2)}) async-start(bf16[8,4,128,128]{3,2,1,0:T(8,128)(2,1)} %copy-done.8), calls=%async_computation.4 | async-start | bytes 2097152 | tf_op jit(solution)/shard_map/all_to_all | solution.py:347
  129.5 0.2 collective-permute-start.16
  129.7 0.3 collective-permute-start.23
  130.0 1.6 %collective-permute-done.16.other_ref = bf16[8,2,128,128]{3,2,1,0:T(8,128)(2,1)S(1)} collective-permute-done((bf16[8,2,128,128]{3,2,1,0:T(8,128)(2,1)}, bf16[8,2,128,128]{3,2,1,0:T(8,128)(2,1)S(1)}, u32[]{:S(2)}, u32[]{:S(2)}) %collective-permute-start.16) | collective-permute-done | bytes 524320 | tf_op jit(solution)/shard_map/ppermute | solution.py:64
  131.6 1.8 %shard_map.86 = (f32[512,128]{1,0:T(8,128)S(1)}, bf16[512,128]{1,0:T(8,128)(2,1)S(1)}, bf16[512,128]{1,0:T(8,128)(2,1)S(1)}, bf16[512,128]{1,0:T(8,128)(2,1)S(1)}) custom-call(s32[38]{0:T(128)S(1)} %get-tuple-element.33.at_ref, bf16[8,2,128,128]{3,2,1,0:T(8,128)(2,1)} %all-to-all-done.2.same_ref, ...), custom_call_target="tpu_custom_call" | custom-call | flops 536870912 | bytes 4194304 | tf_op jit(solution)/shard_map/pallas_call | solution.py:354
  133.6 2.2 %collective-permute-start.21 = (bf16[512,128]{1,0:T(8,128)(2,1)S(1)}, bf16[512,128]{1,0:T(8,128)(2,1)S(1)}, u32[]{:S(2)}, u32[]{:S(2)}) collective-permute-start(bf16[512,128]{1,0:T(8,128)(2,1)S(1)} %get-tuple-element.53), channel_id=1, source_target_pairs={{0,16},{8,24},{16,0},{24,8},{32,48},{40,56},{48,32},{56,40},{64,80... | collective-permute-start | bytes 393224 | tf_op jit(solution)/shard_map/ppermute | solution.py:55
  135.8 0.4 collective-permute-start.22
  136.4 1.5 collective-permute-start.24
  137.9 2.4 %collective-permute-start.25 = (bf16[4,128,128]{2,1,0:T(8,128)(2,1)S(1)}, bf16[4,128,128]{2,1,0:T(8,128)(2,1)S(1)}, u32[]{:S(2)}, u32[]{:S(2)}) collective-permute-start(bf16[4,128,128]{2,1,0:T(8,128)(2,1)S(1)} %get-tuple-element.60), channel_id=1, source_target_pairs={{0,4},{1,5},{2,6},{3,7},{4,0},{5,1},{6,2},{7,3},{8,12},{9,13},{10,... | collective-permute-start | bytes 393224 | tf_op jit(solution)/shard_map/ppermute | solution.py:60
  140.3 2.3 %collective-permute-start.26 = (bf16[4,128,128]{2,1,0:T(8,128)(2,1)S(1)}, bf16[4,128,128]{2,1,0:T(8,128)(2,1)S(1)}, u32[]{:S(2)}, u32[]{:S(2)}) collective-permute-start(bf16[4,128,128]{2,1,0:T(8,128)(2,1)S(1)} %get-tuple-element.61), channel_id=1, source_target_pairs={{0,6},{1,7},{2,0},{3,1},{4,2},{5,3},{6,4},{7,5},{8,14},{9,15},{10,... | collective-permute-start | bytes 393224 | tf_op jit(solution)/shard_map/ppermute | solution.py:60
  142.6 0.1 collective-permute-done.22.refs_3_
  142.7 1.6 %shard_map.87 = f32[512,128]{1,0:T(8,128)} custom-call(s32[38]{0:T(128)S(1)} %get-tuple-element.33.at_ref, s32[32,32]{1,0:T(8,128)S(1)} %copy-done.14, f32[512,128]{1,0:T(8,128)S(1)} %copy-done.13, f32[512,128]{1,0:T(8,128)S(1)} %get-tuple-element.51.refs_0_, bf16[512,128]{1,0:T(8,128)(2,1)S(1)} %collective-permute-done.20.refs_1_, ...), custom_call_target="tpu_custom_call" | custom-call | bytes 1048576 | tf_op jit(solution)/shard_map/pallas_call | solution.py:361
  144.3 0.4 all-to-all-done.4.refs_5_
  144.8 2.7 %shard_map.88.own_ref = f32[512,128]{1,0:T(8,128)S(1)} custom-call(s32[38]{0:T(128)S(1)} %get-tuple-element.33.at_ref, bf16[8,128,512]{2,1,0:T(8,128)(2,1)S(1)} %copy-done.2, bf16[8,128,512]{2,1,0:T(8,128)(2,1)} %collective-permute-done.8.refs_1_, bf16[4,128,512]{2,1,0:T(8,128)(2,1)S(1)} %collective-permute-done.13.refs_4_.refs_2_, ...), custom_call_target="tpu_custom_call" | custom-call | flops 536870912 | bytes 6291456 | tf_op jit(solution)/shard_map/pallas_call | solution.py:266
  147.4 2.8 %collective-permute-done.25.refs_1_ = bf16[4,128,128]{2,1,0:T(8,128)(2,1)S(1)} collective-permute-done((bf16[4,128,128]{2,1,0:T(8,128)(2,1)S(1)}, bf16[4,128,128]{2,1,0:T(8,128)(2,1)S(1)}, u32[]{:S(2)}, u32[]{:S(2)}) %collective-permute-start.25) | collective-permute-done | bytes 131104 | tf_op jit(solution)/shard_map/ppermute | solution.py:60
  150.3 0.8 shard_map.90
  (59 shorter events, 0.8 us)
Async XLA Ops:
  0.7 3.8 %copy-start.12 = (f32[512,128]{1,0:T(8,128)S(1)}, f32[512,128]{1,0:T(8,128)}, u32[]{:S(2)}) copy-start(f32[512,128]{1,0:T(8,128)} %cotangent_ref) | copy-start | bytes 786436
  0.7 3.8 %copy-start.14 = (s32[32,32]{1,0:T(8,128)S(1)}, s32[32,32]{1,0:T(8,128)}, u32[]{:S(2)}) copy-start(s32[32,32]{1,0:T(8,128)} %fill_ref.3) | copy-start | bytes 12292
  0.7 3.8 %copy-start.15 = (s32[32]{0:T(128)S(1)}, s32[32]{0:T(128)}, u32[]{:S(2)}) copy-start(s32[32]{0:T(128)} %owner_ref.1) | copy-start | bytes 388
  6.0 10.5 %collective-permute-start = (bf16[128,512]{1,0:T(8,128)(2,1)S(1)}, bf16[128,512]{1,0:T(8,128)(2,1)S(1)}, u32[]{:S(2)}, u32[]{:S(2)}) collective-permute-start(bf16[128,512]{1,0:T(8,128)(2,1)S(1)} %get-tuple-element.35), channel_id=1, source_target_pairs={{0,224},{8,232},{16,240},{24,248},{32,0},{40,8},{48,16},{56,24},{6... | collective-permute-start | bytes 393224 | tf_op jit(solution)/shard_map/ppermute | solution.py:50
  12.5 6.8 %collective-permute-start.3 = (bf16[128,512]{1,0:T(8,128)(2,1)S(1)}, bf16[128,512]{1,0:T(8,128)(2,1)S(1)}, u32[]{:S(2)}, u32[]{:S(2)}) collective-permute-start(bf16[128,512]{1,0:T(8,128)(2,1)S(1)} %get-tuple-element.35), channel_id=1, source_target_pairs={{0,32},{8,40},{16,48},{24,56},{32,64},{40,72},{48,80},{56,88},{64,... | collective-permute-start | bytes 393224 | tf_op jit(solution)/shard_map/ppermute | solution.py:50
  12.5 23.5 %all-to-all-start = ((bf16[4,1536,128]{2,1,0:T(8,128)(2,1)}), bf16[4,1536,128]{2,1,0:T(8,128)(2,1)S(1)}, u32[]{:S(2)}, u32[]{:S(2)}) async-start(bf16[4,1536,128]{2,1,0:T(8,128)(2,1)} %shard_map.77), calls=%async_computation | async-start | bytes 3145728 | tf_op jit(solution)/shard_map/all_to_all | solution.py:41
  16.5 4.7 %collective-permute-start.1 = (bf16[128,512]{1,0:T(8,128)(2,1)S(1)}, bf16[128,512]{1,0:T(8,128)(2,1)S(1)}, u32[]{:S(2)}, u32[]{:S(2)}) collective-permute-start(bf16[128,512]{1,0:T(8,128)(2,1)S(1)} %collective-permute-done), channel_id=1, source_target_pairs={{0,224},{8,232},{16,240},{24,248},{32,0},{40,8},{48,16},{56,24},{6... | collective-permute-start | bytes 393224 | tf_op jit(solution)/shard_map/ppermute | solution.py:50
  19.3 5.3 %collective-permute-start.4 = (bf16[128,512]{1,0:T(8,128)(2,1)S(1)}, bf16[128,512]{1,0:T(8,128)(2,1)S(1)}, u32[]{:S(2)}, u32[]{:S(2)}) collective-permute-start(bf16[128,512]{1,0:T(8,128)(2,1)S(1)} %collective-permute-done.3), channel_id=1, source_target_pairs={{0,32},{8,40},{16,48},{24,56},{32,64},{40,72},{48,80},{56,88},{64,... | collective-permute-start | bytes 393224 | tf_op jit(solution)/shard_map/ppermute | solution.py:50
  21.2 8.7 %collective-permute-start.2 = (bf16[128,512]{1,0:T(8,128)(2,1)S(1)}, bf16[128,512]{1,0:T(8,128)(2,1)S(1)}, u32[]{:S(2)}, u32[]{:S(2)}) collective-permute-start(bf16[128,512]{1,0:T(8,128)(2,1)S(1)} %collective-permute-done.1), channel_id=1, source_target_pairs={{0,224},{8,232},{16,240},{24,248},{32,0},{40,8},{48,16},{56,24},{6... | collective-permute-start | bytes 393224 | tf_op jit(solution)/shard_map/ppermute | solution.py:50
  24.6 5.3 %collective-permute-start.5 = (bf16[128,512]{1,0:T(8,128)(2,1)S(1)}, bf16[128,512]{1,0:T(8,128)(2,1)S(1)}, u32[]{:S(2)}, u32[]{:S(2)}) collective-permute-start(bf16[128,512]{1,0:T(8,128)(2,1)S(1)} %collective-permute-done.4), channel_id=1, source_target_pairs={{0,32},{8,40},{16,48},{24,56},{32,64},{40,72},{48,80},{56,88},{64,... | collective-permute-start | bytes 393224 | tf_op jit(solution)/shard_map/ppermute | solution.py:50
  29.9 4.6 %collective-permute-start.6 = (bf16[64,512]{1,0:T(8,128)(2,1)S(1)}, bf16[64,512]{1,0:T(8,128)(2,1)S(1)}, u32[]{:S(2)}, u32[]{:S(2)}) collective-permute-start(bf16[64,512]{1,0:T(8,128)(2,1)S(1)} %slice.16), channel_id=1, source_target_pairs={{0,32},{8,40},{16,48},{24,56},{32,64},{40,72},{48,80},{56,88},{64,... | collective-permute-start | bytes 196616 | tf_op jit(solution)/shard_map/ppermute | solution.py:50
  29.9 4.6 %collective-permute-start.7 = (bf16[64,512]{1,0:T(8,128)(2,1)S(1)}, bf16[64,512]{1,0:T(8,128)(2,1)S(1)}, u32[]{:S(2)}, u32[]{:S(2)}) collective-permute-start(bf16[64,512]{1,0:T(8,128)(2,1)S(1)} %slice.17), channel_id=1, source_target_pairs={{0,224},{8,232},{16,240},{24,248},{32,0},{40,8},{48,16},{56,24},{6... | collective-permute-start | bytes 196616 | tf_op jit(solution)/shard_map/ppermute | solution.py:50
  34.6 8.7 %copy-start = (bf16[8,128,512]{2,1,0:T(8,128)(2,1)}, bf16[8,128,512]{2,1,0:T(8,128)(2,1)S(1)}, u32[]{:S(2)}) copy-start(bf16[8,128,512]{2,1,0:T(8,128)(2,1)S(1)} %bitcast_dynamic-update-slice_fusion.refs_0_) | copy-start | bytes 3145732
  36.7 1.0 copy-start.6
  37.7 30.8 %all-to-all-start.1 = ((bf16[8,512,128]{2,1,0:T(8,128)(2,1)}), bf16[8,512,128]{2,1,0:T(8,128)(2,1)}, u32[]{:S(2)}, u32[]{:S(2)}) async-start(bf16[8,512,128]{2,1,0:T(8,128)(2,1)} %copy-done.6), calls=%async_computation.1 | async-start | bytes 2097152 | tf_op jit(solution)/shard_map/all_to_all | solution.py:45
  42.0 21.6 %collective-permute-start.8 = (bf16[8,128,512]{2,1,0:T(8,128)(2,1)S(1)}, bf16[8,128,512]{2,1,0:T(8,128)(2,1)}, u32[]{:S(2)}, u32[]{:S(2)}) collective-permute-start(bf16[8,128,512]{2,1,0:T(8,128)(2,1)S(1)} %bitcast_dynamic-update-slice_fusion.refs_0_), channel_id=1, source_target_pairs={{0,24},{8,0},{16,8},{24,16},{32,56},{40,32},{48,40},{56,48},{64,88... | collective-permute-start | bytes 3145736 | tf_op jit(solution)/shard_map/ppermute | solution.py:55
  43.4 20.8 %collective-permute-start.9 = (bf16[8,128,512]{2,1,0:T(8,128)(2,1)S(1)}, bf16[8,128,512]{2,1,0:T(8,128)(2,1)}, u32[]{:S(2)}, u32[]{:S(2)}) collective-permute-start(bf16[8,128,512]{2,1,0:T(8,128)(2,1)S(1)} %bitcast_dynamic-update-slice_fusion.refs_0_), channel_id=1, source_target_pairs={{0,8},{8,16},{16,24},{24,0},{32,40},{40,48},{48,56},{56,32},{64,72... | collective-permute-start | bytes 3145736 | tf_op jit(solution)/shard_map/ppermute | solution.py:55
  69.9 1.0 copy-start.9
  70.9 29.0 %all-to-all-start.3 = ((bf16[8,512,128]{2,1,0:T(8,128)(2,1)}), bf16[8,512,128]{2,1,0:T(8,128)(2,1)S(1)}, u32[]{:S(2)}, u32[]{:S(2)}) async-start(bf16[8,512,128]{2,1,0:T(8,128)(2,1)} %copy-done.9), calls=%async_computation.3 | async-start | bytes 2097152 | tf_op jit(solution)/shard_map/all_to_all | solution.py:45
  75.5 13.7 %collective-permute-start.13 = (bf16[4,128,512]{2,1,0:T(8,128)(2,1)S(1)}, bf16[4,128,512]{2,1,0:T(8,128)(2,1)S(1)}, u32[]{:S(2)}, u32[]{:S(2)}) collective-permute-start(bf16[4,128,512]{2,1,0:T(8,128)(2,1)S(1)} %slice.14), channel_id=1, source_target_pairs={{0,8},{8,16},{16,24},{24,0},{32,40},{40,48},{48,56},{56,32},{64,72... | collective-permute-start | bytes 1572872 | tf_op jit(solution)/shard_map/ppermute | solution.py:55
  76.7 12.5 %collective-permute-start.14 = (bf16[4,128,512]{2,1,0:T(8,128)(2,1)S(1)}, bf16[4,128,512]{2,1,0:T(8,128)(2,1)S(1)}, u32[]{:S(2)}, u32[]{:S(2)}) collective-permute-start(bf16[4,128,512]{2,1,0:T(8,128)(2,1)S(1)} %slice.15), channel_id=1, source_target_pairs={{0,24},{8,0},{16,8},{24,16},{32,56},{40,32},{48,40},{56,48},{64,88... | collective-permute-start | bytes 1572872 | tf_op jit(solution)/shard_map/ppermute | solution.py:55
  79.5 6.1 %collective-permute-start.10 = (bf16[512,128]{1,0:T(8,128)(2,1)S(1)}, bf16[512,128]{1,0:T(8,128)(2,1)S(1)}, u32[]{:S(2)}, u32[]{:S(2)}) collective-permute-start(bf16[512,128]{1,0:T(8,128)(2,1)S(1)} %get-tuple-element.39), channel_id=1, source_target_pairs={{0,6},{1,7},{2,0},{3,1},{4,2},{5,3},{6,4},{7,5},{8,14},{9,15},{10,... | collective-permute-start | bytes 393224 | tf_op jit(solution)/shard_map/ppermute | solution.py:60
  82.2 5.6 %collective-permute-start.11 = (bf16[512,128]{1,0:T(8,128)(2,1)S(1)}, bf16[512,128]{1,0:T(8,128)(2,1)S(1)}, u32[]{:S(2)}, u32[]{:S(2)}) collective-permute-start(bf16[512,128]{1,0:T(8,128)(2,1)S(1)} %get-tuple-element.39), channel_id=1, source_target_pairs={{0,4},{1,5},{2,6},{3,7},{4,0},{5,1},{6,2},{7,3},{8,12},{9,13},{10,... | collective-permute-start | bytes 393224 | tf_op jit(solution)/shard_map/ppermute | solution.py:60
  82.5 6.7 %collective-permute-start.12 = (bf16[512,128]{1,0:T(8,128)(2,1)S(1)}, bf16[512,128]{1,0:T(8,128)(2,1)S(1)}, u32[]{:S(2)}, u32[]{:S(2)}) collective-permute-start(bf16[512,128]{1,0:T(8,128)(2,1)S(1)} %get-tuple-element.39), channel_id=1, source_target_pairs={{0,2},{1,3},{2,4},{3,5},{4,6},{5,7},{6,0},{7,1},{8,10},{9,11},{10,... | collective-permute-start | bytes 393224 | tf_op jit(solution)/shard_map/ppermute | solution.py:60
  89.3 0.8 copy-start.3
  90.1 8.1 %collective-permute-start.15 = (bf16[4,4,128,128]{3,2,1,0:T(8,128)(2,1)S(1)}, bf16[4,4,128,128]{3,2,1,0:T(8,128)(2,1)S(1)}, u32[]{:S(2)}, u32[]{:S(2)}) collective-permute-start(bf16[4,4,128,128]{3,2,1,0:T(8,128)(2,1)S(1)} %shard_map.81.same_ref), channel_id=1, source_target_pairs={{0,1},{1,0},{2,3},{3,2},{4,5},{5,4},{6,7},{7,6},{8,9},{9,8},{10,11... | collective-permute-start | bytes 1572872 | tf_op jit(solution)/shard_map/ppermute | solution.py:64
  99.1 0.8 copy-start.7
  99.9 23.7 %all-to-all-start.2 = ((bf16[8,2,128,128]{3,2,1,0:T(8,128)(2,1)}), bf16[8,2,128,128]{3,2,1,0:T(8,128)(2,1)}, u32[]{:S(2)}, u32[]{:S(2)}) async-start(bf16[8,2,128,128]{3,2,1,0:T(8,128)(2,1)} %bitcast.29), calls=%async_computation.2 | async-start | bytes 1048576 | tf_op jit(solution)/shard_map/all_to_all | solution.py:45
  106.8 10.5 %copy-start.1 = (bf16[8,128,512]{2,1,0:T(8,128)(2,1)S(1)}, bf16[8,128,512]{2,1,0:T(8,128)(2,1)}, u32[]{:S(2)}) copy-start(bf16[8,128,512]{2,1,0:T(8,128)(2,1)} %copy-done) | copy-start | bytes 3145732
  106.8 10.5 %copy-start.4 = (bf16[4,128,512]{2,1,0:T(8,128)(2,1)S(1)}, bf16[4,128,512]{2,1,0:T(8,128)(2,1)}, u32[]{:S(2)}) copy-start(bf16[4,128,512]{2,1,0:T(8,128)(2,1)} %copy-done.3) | copy-start | bytes 1572868
  108.1 6.9 %collective-permute-start.17 = (bf16[4,128,128]{2,1,0:T(8,128)(2,1)S(1)}, bf16[4,128,128]{2,1,0:T(8,128)(2,1)S(1)}, u32[]{:S(2)}, u32[]{:S(2)}) collective-permute-start(bf16[4,128,128]{2,1,0:T(8,128)(2,1)S(1)} %get-tuple-element.44), channel_id=1, source_target_pairs={{0,8},{8,16},{16,24},{24,0},{32,40},{40,48},{48,56},{56,32},{64,72... | collective-permute-start | bytes 393224 | tf_op jit(solution)/shard_map/ppermute | solution.py:55
  108.2 7.2 %collective-permute-start.18 = (bf16[4,128,128]{2,1,0:T(8,128)(2,1)S(1)}, bf16[4,128,128]{2,1,0:T(8,128)(2,1)S(1)}, u32[]{:S(2)}, u32[]{:S(2)}) collective-permute-start(bf16[4,128,128]{2,1,0:T(8,128)(2,1)S(1)} %get-tuple-element.45), channel_id=1, source_target_pairs={{0,16},{8,24},{16,0},{24,8},{32,48},{40,56},{48,32},{56,40},{64,80... | collective-permute-start | bytes 393224 | tf_op jit(solution)/shard_map/ppermute | solution.py:55
  109.2 7.0 %collective-permute-start.19 = (bf16[4,128,128]{2,1,0:T(8,128)(2,1)S(1)}, bf16[4,128,128]{2,1,0:T(8,128)(2,1)S(1)}, u32[]{:S(2)}, u32[]{:S(2)}) collective-permute-start(bf16[4,128,128]{2,1,0:T(8,128)(2,1)S(1)} %get-tuple-element.46), channel_id=1, source_target_pairs={{0,24},{8,0},{16,8},{24,16},{32,56},{40,32},{48,40},{56,48},{64,88... | collective-permute-start | bytes 393224 | tf_op jit(solution)/shard_map/ppermute | solution.py:55
  116.3 1.0 copy-start.8
  121.0 0.9 copy-start.10
  123.6 21.2 %all-to-all-start.4 = ((bf16[8,4,128,128]{3,2,1,0:T(8,128)(2,1)}), bf16[8,4,128,128]{3,2,1,0:T(8,128)(2,1)}, u32[]{:S(2)}, u32[]{:S(2)}) async-start(bf16[8,4,128,128]{3,2,1,0:T(8,128)(2,1)} %copy-done.8), calls=%async_computation.4 | async-start | bytes 2097152 | tf_op jit(solution)/shard_map/all_to_all | solution.py:347
  129.5 6.8 %copy-start.11 = (bf16[5,4,128,128]{3,2,1,0:T(8,128)(2,1)S(1)}, bf16[5,4,128,128]{3,2,1,0:T(8,128)(2,1)}, u32[]{:S(2)}) copy-start(bf16[5,4,128,128]{3,2,1,0:T(8,128)(2,1)} %copy-done.10) | copy-start | bytes 1966084
  129.5 2.1 %collective-permute-start.16 = (bf16[8,2,128,128]{3,2,1,0:T(8,128)(2,1)}, bf16[8,2,128,128]{3,2,1,0:T(8,128)(2,1)S(1)}, u32[]{:S(2)}, u32[]{:S(2)}) collective-permute-start(bf16[8,2,128,128]{3,2,1,0:T(8,128)(2,1)} %all-to-all-done.2.same_ref), channel_id=1, source_target_pairs={{0,1},{1,0},{2,3},{3,2},{4,5},{5,4},{6,7},{7,6},{8,9},{9,8},{10,11... | collective-permute-start | bytes 1572872 | tf_op jit(solution)/shard_map/ppermute | solution.py:64
  129.7 13.0 %copy-start.13 = (f32[512,128]{1,0:T(8,128)S(1)}, f32[512,128]{1,0:T(8,128)}, u32[]{:S(2)}) copy-start(f32[512,128]{1,0:T(8,128)} %trailing_ref.1) | copy-start | bytes 786436
  129.7 6.5 %collective-permute-start.23 = (bf16[5,4,128,128]{3,2,1,0:T(8,128)(2,1)}, bf16[5,4,128,128]{3,2,1,0:T(8,128)(2,1)S(1)}, u32[]{:S(2)}, u32[]{:S(2)}) collective-permute-start(bf16[5,4,128,128]{3,2,1,0:T(8,128)(2,1)} %get-tuple-element.57), channel_id=1, source_target_pairs={{0,1},{1,0},{2,3},{3,2},{4,5},{5,4},{6,7},{7,6},{8,9},{9,8},{10,11... | collective-permute-start | bytes 1966088 | tf_op jit(solution)/shard_map/ppermute | solution.py:64
  133.5 11.3 %copy-start.2 = (bf16[8,128,512]{2,1,0:T(8,128)(2,1)S(1)}, bf16[8,128,512]{2,1,0:T(8,128)(2,1)}, u32[]{:S(2)}) copy-start(bf16[8,128,512]{2,1,0:T(8,128)(2,1)} %copy-done) | copy-start | bytes 3145732
  133.5 11.3 %copy-start.5 = (bf16[4,128,512]{2,1,0:T(8,128)(2,1)S(1)}, bf16[4,128,512]{2,1,0:T(8,128)(2,1)}, u32[]{:S(2)}) copy-start(bf16[4,128,512]{2,1,0:T(8,128)(2,1)} %copy-done.3) | copy-start | bytes 1572868
  133.5 6.8 %collective-permute-start.20 = (bf16[512,128]{1,0:T(8,128)(2,1)S(1)}, bf16[512,128]{1,0:T(8,128)(2,1)S(1)}, u32[]{:S(2)}, u32[]{:S(2)}) collective-permute-start(bf16[512,128]{1,0:T(8,128)(2,1)S(1)} %get-tuple-element.52), channel_id=1, source_target_pairs={{0,8},{8,16},{16,24},{24,0},{32,40},{40,48},{48,56},{56,32},{64,72... | collective-permute-start | bytes 393224 | tf_op jit(solution)/shard_map/ppermute | solution.py:55
  133.6 9.1 %collective-permute-start.21 = (bf16[512,128]{1,0:T(8,128)(2,1)S(1)}, bf16[512,128]{1,0:T(8,128)(2,1)S(1)}, u32[]{:S(2)}, u32[]{:S(2)}) collective-permute-start(bf16[512,128]{1,0:T(8,128)(2,1)S(1)} %get-tuple-element.53), channel_id=1, source_target_pairs={{0,16},{8,24},{16,0},{24,8},{32,48},{40,56},{48,32},{56,40},{64,80... | collective-permute-start | bytes 393224 | tf_op jit(solution)/shard_map/ppermute | solution.py:55
  135.8 7.0 %collective-permute-start.22 = (bf16[512,128]{1,0:T(8,128)(2,1)S(1)}, bf16[512,128]{1,0:T(8,128)(2,1)S(1)}, u32[]{:S(2)}, u32[]{:S(2)}) collective-permute-start(bf16[512,128]{1,0:T(8,128)(2,1)S(1)} %get-tuple-element.54), channel_id=1, source_target_pairs={{0,24},{8,0},{16,8},{24,16},{32,56},{40,32},{48,40},{56,48},{64,88... | collective-permute-start | bytes 393224 | tf_op jit(solution)/shard_map/ppermute | solution.py:55
  136.4 11.1 %collective-permute-start.24 = (bf16[4,128,128]{2,1,0:T(8,128)(2,1)S(1)}, bf16[4,128,128]{2,1,0:T(8,128)(2,1)S(1)}, u32[]{:S(2)}, u32[]{:S(2)}) collective-permute-start(bf16[4,128,128]{2,1,0:T(8,128)(2,1)S(1)} %get-tuple-element.59), channel_id=1, source_target_pairs={{0,2},{1,3},{2,4},{3,5},{4,6},{5,7},{6,0},{7,1},{8,10},{9,11},{10,... | collective-permute-start | bytes 393224 | tf_op jit(solution)/shard_map/ppermute | solution.py:60
  137.9 12.4 %collective-permute-start.25 = (bf16[4,128,128]{2,1,0:T(8,128)(2,1)S(1)}, bf16[4,128,128]{2,1,0:T(8,128)(2,1)S(1)}, u32[]{:S(2)}, u32[]{:S(2)}) collective-permute-start(bf16[4,128,128]{2,1,0:T(8,128)(2,1)S(1)} %get-tuple-element.60), channel_id=1, source_target_pairs={{0,4},{1,5},{2,6},{3,7},{4,0},{5,1},{6,2},{7,3},{8,12},{9,13},{10,... | collective-permute-start | bytes 393224 | tf_op jit(solution)/shard_map/ppermute | solution.py:60
  140.3 10.0 %collective-permute-start.26 = (bf16[4,128,128]{2,1,0:T(8,128)(2,1)S(1)}, bf16[4,128,128]{2,1,0:T(8,128)(2,1)S(1)}, u32[]{:S(2)}, u32[]{:S(2)}) collective-permute-start(bf16[4,128,128]{2,1,0:T(8,128)(2,1)S(1)} %get-tuple-element.61), channel_id=1, source_target_pairs={{0,6},{1,7},{2,0},{3,1},{4,2},{5,3},{6,4},{7,5},{8,14},{9,15},{10,... | collective-permute-start | bytes 393224 | tf_op jit(solution)/shard_map/ppermute | solution.py:60

commit v6 on v5

--- a/solution.py
+++ b/solution.py
@@ -81,13 +81,16 @@
 
 
 def sum_kernel(parts_ref, tile_ref, out_ref):
-    total = parts_ref[0].astype(F32)
-    for z in range(1, NZ):
-        total += parts_ref[z].astype(F32)
-    total = total.astype(BF)
-    tile_ref[...] = total
-    for z in range(NZ):
-        out_ref[z] = total
+    step = 64
+    for first in range(0, ROWS, step):
+        rows = slice(first, first + step)
+        total = parts_ref[0, rows, :].astype(F32)
+        for z in range(1, NZ):
+            total += parts_ref[z, rows, :].astype(F32)
+        total = total.astype(BF)
+        tile_ref[rows, :] = total
+        for z in range(NZ):
+            out_ref[z, rows, :] = total
 
 
 def factor_kernel(got_ref, out_ref):

time: 152 us -> 152 us (level)
  no operation moved by 1% of the time
where the time goes in v6:
time: 152 us; the launch traced here: 151 us
  starting transfers between devices  66.7 us (44%)
  waiting for transfers between devices  55.3 us (36%)
  Pallas kernels  20.2 us (13%)
  local copies, waits for them, and re-layouts  7.78 us (5%)
    ppermute x10, waiting for transfers between devices, shift_x(): return lax.ppermute(value, 'col', pairs)  26.1 us
    ppermute x8, starting transfers between devices, shift_z(): return lax.ppermute(value, 'col', pairs)  15.1 us
    all_to_all x3, starting transfers between devices, exchange_z(): return lax.all_to_all(value, 'col', 0, 0, axis_index_groups=Z_GROUPS)  14.7 us
    ppermute x6, starting transfers between devices, shift_y(): return lax.ppermute(value, 'row', pairs)  10 us
    ppermute x10, starting transfers between devices, shift_x(): return lax.ppermute(value, 'col', pairs)  9.86 us
    ppermute x8, waiting for transfers between devices, shift_z(): return lax.ppermute(value, 'col', pairs)  9.39 us
    ppermute x6, waiting for transfers between devices, shift_y(): return lax.ppermute(value, 'row', pairs)  8.8 us
    ppermute x3, starting transfers between devices, swap_core(): return lax.ppermute(value, 'row', [(r, r ^ 1) for r in range(2 * NY)])  7.11 us
  transfers between devices with their start and end apart: 32, of which 20 were waited for; matrix products, arithmetic and copies ran while one was open for 1% of the time, Pallas kernels for 8%

profile of v6, /device:TPU:1, one launch (start us, length us, event | category | flops | bytes accessed | tf_op | source)
XLA Modules:
  0.0 151.0 jit_solution(8852255208037525746)
XLA Ops:
  0.7 3.7 %shard_map.77 = bf16[4,1536,128]{2,1,0:T(8,128)(2,1)} custom-call(bf16[512,128]{1,0:T(8,128)(2,1)} %panel_ref.1, bf16[128,4096]{1,0:T(8,128)(2,1)} %refs_7_.1, bf16[128,4096]{1,0:T(8,128)(2,1)} %refs_7_.1, bf16[128,4096]{1,0:T(8,128)(2,1)} %refs_7_.1, bf16[128,4096]{1,0:T(8,128)(2,1)} %refs_7_.1, bf16[128,4096]{1,0:T(8,128)(2,1)} %refs_7_.1, ...), custom_call_target="tpu_custom_call" | custom-call | bytes 3145728 | tf_op jit(solution)/shard_map/pallas_call | solution.py:278
  4.5 1.5 shard_map.78
  6.0 6.5 %collective-permute-start = (bf16[128,512]{1,0:T(8,128)(2,1)S(1)}, bf16[128,512]{1,0:T(8,128)(2,1)S(1)}, u32[]{:S(2)}, u32[]{:S(2)}) collective-permute-start(bf16[128,512]{1,0:T(8,128)(2,1)S(1)} %get-tuple-element.35), channel_id=1, source_target_pairs={{0,224},{8,232},{16,240},{24,248},{32,0},{40,8},{48,16},{56,24},{6... | collective-permute-start | bytes 393224 | tf_op jit(solution)/shard_map/ppermute | solution.py:50
  12.5 4.0 %all-to-all-start = ((bf16[4,1536,128]{2,1,0:T(8,128)(2,1)}), bf16[4,1536,128]{2,1,0:T(8,128)(2,1)S(1)}, u32[]{:S(2)}, u32[]{:S(2)}) async-start(bf16[4,1536,128]{2,1,0:T(8,128)(2,1)} %shard_map.77), calls=%async_computation | async-start | bytes 3145728 | tf_op jit(solution)/shard_map/all_to_all | solution.py:41
  16.5 2.7 %collective-permute-start.1 = (bf16[128,512]{1,0:T(8,128)(2,1)S(1)}, bf16[128,512]{1,0:T(8,128)(2,1)S(1)}, u32[]{:S(2)}, u32[]{:S(2)}) collective-permute-start(bf16[128,512]{1,0:T(8,128)(2,1)S(1)} %collective-permute-done), channel_id=1, source_target_pairs={{0,224},{8,232},{16,240},{24,248},{32,0},{40,8},{48,16},{56,24},{6... | collective-permute-start | bytes 393224 | tf_op jit(solution)/shard_map/ppermute | solution.py:50
  19.3 1.9 %collective-permute-done.1 = bf16[128,512]{1,0:T(8,128)(2,1)S(1)} collective-permute-done((bf16[128,512]{1,0:T(8,128)(2,1)S(1)}, bf16[128,512]{1,0:T(8,128)(2,1)S(1)}, u32[]{:S(2)}, u32[]{:S(2)}) %collective-permute-start.1) | collective-permute-done | bytes 131104 | tf_op jit(solution)/shard_map/ppermute | solution.py:50
  21.2 3.1 %collective-permute-start.2 = (bf16[128,512]{1,0:T(8,128)(2,1)S(1)}, bf16[128,512]{1,0:T(8,128)(2,1)S(1)}, u32[]{:S(2)}, u32[]{:S(2)}) collective-permute-start(bf16[128,512]{1,0:T(8,128)(2,1)S(1)} %collective-permute-done.1), channel_id=1, source_target_pairs={{0,224},{8,232},{16,240},{24,248},{32,0},{40,8},{48,16},{56,24},{6... | collective-permute-start | bytes 393224 | tf_op jit(solution)/shard_map/ppermute | solution.py:50
  24.3 0.3 collective-permute-done.4
  24.6 5.3 %collective-permute-done.5 = bf16[128,512]{1,0:T(8,128)(2,1)S(1)} collective-permute-done((bf16[128,512]{1,0:T(8,128)(2,1)S(1)}, bf16[128,512]{1,0:T(8,128)(2,1)S(1)}, u32[]{:S(2)}, u32[]{:S(2)}) %collective-permute-start.5) | collective-permute-done | bytes 131104 | tf_op jit(solution)/shard_map/ppermute | solution.py:50
  29.9 2.7 %collective-permute-start.7 = (bf16[64,512]{1,0:T(8,128)(2,1)S(1)}, bf16[64,512]{1,0:T(8,128)(2,1)S(1)}, u32[]{:S(2)}, u32[]{:S(2)}) collective-permute-start(bf16[64,512]{1,0:T(8,128)(2,1)S(1)} %slice.17), channel_id=1, source_target_pairs={{0,224},{8,232},{16,240},{24,248},{32,0},{40,8},{48,16},{56,24},{6... | collective-permute-start | bytes 196616 | tf_op jit(solution)/shard_map/ppermute | solution.py:50
  32.7 1.8 %collective-permute-done.6 = bf16[64,512]{1,0:T(8,128)(2,1)S(1)} collective-permute-done((bf16[64,512]{1,0:T(8,128)(2,1)S(1)}, bf16[64,512]{1,0:T(8,128)(2,1)S(1)}, u32[]{:S(2)}, u32[]{:S(2)}) %collective-permute-start.6) | collective-permute-done | bytes 65568 | tf_op jit(solution)/shard_map/ppermute | solution.py:50
  34.6 1.4 all-to-all-done.got_ref
  36.0 0.7 shard_map.79
  36.7 1.0 copy-done.6
  37.7 4.2 %all-to-all-start.1 = ((bf16[8,512,128]{2,1,0:T(8,128)(2,1)}), bf16[8,512,128]{2,1,0:T(8,128)(2,1)}, u32[]{:S(2)}, u32[]{:S(2)}) async-start(bf16[8,512,128]{2,1,0:T(8,128)(2,1)} %copy-done.6), calls=%async_computation.1 | async-start | bytes 2097152 | tf_op jit(solution)/shard_map/all_to_all | solution.py:45
  42.0 1.4 collective-permute-start.8
  43.4 0.1 collective-permute-start.9
  43.5 20.0 %collective-permute-done.8.refs_1_ = bf16[8,128,512]{2,1,0:T(8,128)(2,1)} collective-permute-done((bf16[8,128,512]{2,1,0:T(8,128)(2,1)S(1)}, bf16[8,128,512]{2,1,0:T(8,128)(2,1)}, u32[]{:S(2)}, u32[]{:S(2)}) %collective-permute-start.8) | collective-permute-done | bytes 1048608 | tf_op jit(solution)/shard_map/ppermute | solution.py:55
  63.5 0.6 collective-permute-done.9.refs_4_
  64.1 4.4 %all-to-all-done.1.parts_ref = bf16[8,512,128]{2,1,0:T(8,128)(2,1)} async-done(((bf16[8,512,128]{2,1,0:T(8,128)(2,1)}), bf16[8,512,128]{2,1,0:T(8,128)(2,1)}, u32[]{:S(2)}, u32[]{:S(2)}) %all-to-all-start.1) | async-done | bytes 1048608 | tf_op jit(solution)/shard_map/all_to_all | solution.py:45
  68.5 1.4 shard_map.80
  69.9 1.0 copy-done.9
  70.9 3.6 %all-to-all-start.3 = ((bf16[8,512,128]{2,1,0:T(8,128)(2,1)}), bf16[8,512,128]{2,1,0:T(8,128)(2,1)S(1)}, u32[]{:S(2)}, u32[]{:S(2)}) async-start(bf16[8,512,128]{2,1,0:T(8,128)(2,1)} %copy-done.9), calls=%async_computation.3 | async-start | bytes 2097152 | tf_op jit(solution)/shard_map/all_to_all | solution.py:45
  74.5 1.1 slice.14
  75.6 1.1 slice.15
  76.7 2.7 %collective-permute-start.14 = (bf16[4,128,512]{2,1,0:T(8,128)(2,1)S(1)}, bf16[4,128,512]{2,1,0:T(8,128)(2,1)S(1)}, u32[]{:S(2)}, u32[]{:S(2)}) collective-permute-start(bf16[4,128,512]{2,1,0:T(8,128)(2,1)S(1)} %slice.15), channel_id=1, source_target_pairs={{0,24},{8,0},{16,8},{24,16},{32,56},{40,32},{48,40},{56,48},{64,88... | collective-permute-start | bytes 1572872 | tf_op jit(solution)/shard_map/ppermute | solution.py:55
  79.5 2.7 %collective-permute-start.10 = (bf16[512,128]{1,0:T(8,128)(2,1)S(1)}, bf16[512,128]{1,0:T(8,128)(2,1)S(1)}, u32[]{:S(2)}, u32[]{:S(2)}) collective-permute-start(bf16[512,128]{1,0:T(8,128)(2,1)S(1)} %get-tuple-element.39), channel_id=1, source_target_pairs={{0,6},{1,7},{2,0},{3,1},{4,2},{5,3},{6,4},{7,5},{8,14},{9,15},{10,... | collective-permute-start | bytes 393224 | tf_op jit(solution)/shard_map/ppermute | solution.py:60
  82.2 0.3 collective-permute-start.11
  82.5 0.7 collective-permute-start.12
  83.2 2.3 %collective-permute-done.10 = bf16[512,128]{1,0:T(8,128)(2,1)S(1)} collective-permute-done((bf16[512,128]{1,0:T(8,128)(2,1)S(1)}, bf16[512,128]{1,0:T(8,128)(2,1)S(1)}, u32[]{:S(2)}, u32[]{:S(2)}) %collective-permute-start.10) | collective-permute-done | bytes 131104 | tf_op jit(solution)/shard_map/ppermute | solution.py:60
  85.5 2.3 %collective-permute-done.11 = bf16[512,128]{1,0:T(8,128)(2,1)S(1)} collective-permute-done((bf16[512,128]{1,0:T(8,128)(2,1)S(1)}, bf16[512,128]{1,0:T(8,128)(2,1)S(1)}, u32[]{:S(2)}, u32[]{:S(2)}) %collective-permute-start.11) | collective-permute-done | bytes 131104 | tf_op jit(solution)/shard_map/ppermute | solution.py:60
  87.8 1.4 collective-permute-done.12
  89.3 0.8 copy-done.3
  90.1 6.6 %collective-permute-start.15 = (bf16[4,4,128,128]{3,2,1,0:T(8,128)(2,1)S(1)}, bf16[4,4,128,128]{3,2,1,0:T(8,128)(2,1)S(1)}, u32[]{:S(2)}, u32[]{:S(2)}) collective-permute-start(bf16[4,4,128,128]{3,2,1,0:T(8,128)(2,1)S(1)} %shard_map.81.same_ref), channel_id=1, source_target_pairs={{0,1},{1,0},{2,3},{3,2},{4,5},{5,4},{6,7},{7,6},{8,9},{9,8},{10,11... | collective-permute-start | bytes 1572872 | tf_op jit(solution)/shard_map/ppermute | solution.py:64
  96.7 1.5 %collective-permute-done.15.other_ref = bf16[4,4,128,128]{3,2,1,0:T(8,128)(2,1)S(1)} collective-permute-done((bf16[4,4,128,128]{3,2,1,0:T(8,128)(2,1)S(1)}, bf16[4,4,128,128]{3,2,1,0:T(8,128)(2,1)S(1)}, u32[]{:S(2)}, u32[]{:S(2)}) %collective-permute-start.15) | collective-permute-done | bytes 524320 | tf_op jit(solution)/shard_map/ppermute | solution.py:64
  98.2 0.9 shard_map.82
  99.1 0.8 copy-done.7
  99.9 6.9 %all-to-all-start.2 = ((bf16[8,2,128,128]{3,2,1,0:T(8,128)(2,1)}), bf16[8,2,128,128]{3,2,1,0:T(8,128)(2,1)}, u32[]{:S(2)}, u32[]{:S(2)}) async-start(bf16[8,2,128,128]{3,2,1,0:T(8,128)(2,1)} %bitcast.29), calls=%async_computation.2 | async-start | bytes 1048576 | tf_op jit(solution)/shard_map/all_to_all | solution.py:45
  106.8 1.3 shard_map.83
  108.2 1.0 collective-permute-start.18
  109.2 1.7 %collective-permute-start.19 = (bf16[4,128,128]{2,1,0:T(8,128)(2,1)S(1)}, bf16[4,128,128]{2,1,0:T(8,128)(2,1)S(1)}, u32[]{:S(2)}, u32[]{:S(2)}) collective-permute-start(bf16[4,128,128]{2,1,0:T(8,128)(2,1)S(1)} %get-tuple-element.46), channel_id=1, source_target_pairs={{0,24},{8,0},{16,8},{24,16},{32,56},{40,32},{48,40},{56,48},{64,88... | collective-permute-start | bytes 393224 | tf_op jit(solution)/shard_map/ppermute | solution.py:55
  110.9 4.1 %collective-permute-done.17.refs_0_ = bf16[4,128,128]{2,1,0:T(8,128)(2,1)S(1)} collective-permute-done((bf16[4,128,128]{2,1,0:T(8,128)(2,1)S(1)}, bf16[4,128,128]{2,1,0:T(8,128)(2,1)S(1)}, u32[]{:S(2)}, u32[]{:S(2)}) %collective-permute-start.17) | collective-permute-done | bytes 131104 | tf_op jit(solution)/shard_map/ppermute | solution.py:55
  115.0 0.4 collective-permute-done.18.refs_1_
  115.4 0.8 collective-permute-done.19.refs_2_
  116.3 1.0 copy-done.8
  117.3 3.6 %shard_map.85 = (bf16[5,4,128,128]{3,2,1,0:T(8,128)(2,1)S(1)}, bf16[5,4,128,128]{3,2,1,0:T(8,128)(2,1)}, f32[8,128]{1,0:T(8,128)S(1)}) custom-call(s32[38]{0:T(128)S(1)} %get-tuple-element.33.at_ref, bf16[8,128,512]{2,1,0:T(8,128)(2,1)S(1)} %copy-done.1, bf16[8,128,512]{2,1,0:T(8,128)(2,1)} %collective-permute-done.8.refs_1_, ...), custom_call_target="tpu_custom_call" | custom-call | flops 536870912 | bytes 6291456 | tf_op jit(solution)/shard_map/pallas_call | solution.py:269
  121.0 0.9 copy-done.10
  121.8 1.7 %all-to-all-done.2.same_ref = bf16[8,2,128,128]{3,2,1,0:T(8,128)(2,1)} async-done(((bf16[8,2,128,128]{3,2,1,0:T(8,128)(2,1)}), bf16[8,2,128,128]{3,2,1,0:T(8,128)(2,1)}, u32[]{:S(2)}, u32[]{:S(2)}) %all-to-all-start.2) | async-done | bytes 524320 | tf_op jit(solution)/shard_map/all_to_all | solution.py:45
  123.6 5.9 %all-to-all-start.4 = ((bf16[8,4,128,128]{3,2,1,0:T(8,128)(2,1)}), bf16[8,4,128,128]{3,2,1,0:T(8,128)(2,1)}, u32[]{:S(2)}, u32[]{:S(2)}) async-start(bf16[8,4,128,128]{3,2,1,0:T(8,128)(2,1)} %copy-done.8), calls=%async_computation.4 | async-start | bytes 2097152 | tf_op jit(solution)/shard_map/all_to_all | solution.py:350
  129.5 0.2 collective-permute-start.16
  129.7 0.3 collective-permute-start.23
  130.0 1.6 %collective-permute-done.16.other_ref = bf16[8,2,128,128]{3,2,1,0:T(8,128)(2,1)S(1)} collective-permute-done((bf16[8,2,128,128]{3,2,1,0:T(8,128)(2,1)}, bf16[8,2,128,128]{3,2,1,0:T(8,128)(2,1)S(1)}, u32[]{:S(2)}, u32[]{:S(2)}) %collective-permute-start.16) | collective-permute-done | bytes 524320 | tf_op jit(solution)/shard_map/ppermute | solution.py:64
  131.6 1.8 %shard_map.86 = (f32[512,128]{1,0:T(8,128)S(1)}, bf16[512,128]{1,0:T(8,128)(2,1)S(1)}, bf16[512,128]{1,0:T(8,128)(2,1)S(1)}, bf16[512,128]{1,0:T(8,128)(2,1)S(1)}) custom-call(s32[38]{0:T(128)S(1)} %get-tuple-element.33.at_ref, bf16[8,2,128,128]{3,2,1,0:T(8,128)(2,1)} %all-to-all-done.2.same_ref, ...), custom_call_target="tpu_custom_call" | custom-call | flops 536870912 | bytes 4194304 | tf_op jit(solution)/shard_map/pallas_call | solution.py:357
  133.6 2.2 %collective-permute-start.21 = (bf16[512,128]{1,0:T(8,128)(2,1)S(1)}, bf16[512,128]{1,0:T(8,128)(2,1)S(1)}, u32[]{:S(2)}, u32[]{:S(2)}) collective-permute-start(bf16[512,128]{1,0:T(8,128)(2,1)S(1)} %get-tuple-element.53), channel_id=1, source_target_pairs={{0,16},{8,24},{16,0},{24,8},{32,48},{40,56},{48,32},{56,40},{64,80... | collective-permute-start | bytes 393224 | tf_op jit(solution)/shard_map/ppermute | solution.py:55
  135.8 0.4 collective-permute-start.22
  136.4 1.5 collective-permute-start.24
  137.9 2.4 %collective-permute-start.25 = (bf16[4,128,128]{2,1,0:T(8,128)(2,1)S(1)}, bf16[4,128,128]{2,1,0:T(8,128)(2,1)S(1)}, u32[]{:S(2)}, u32[]{:S(2)}) collective-permute-start(bf16[4,128,128]{2,1,0:T(8,128)(2,1)S(1)} %get-tuple-element.60), channel_id=1, source_target_pairs={{0,4},{1,5},{2,6},{3,7},{4,0},{5,1},{6,2},{7,3},{8,12},{9,13},{10,... | collective-permute-start | bytes 393224 | tf_op jit(solution)/shard_map/ppermute | solution.py:60
  140.3 2.3 %collective-permute-start.26 = (bf16[4,128,128]{2,1,0:T(8,128)(2,1)S(1)}, bf16[4,128,128]{2,1,0:T(8,128)(2,1)S(1)}, u32[]{:S(2)}, u32[]{:S(2)}) collective-permute-start(bf16[4,128,128]{2,1,0:T(8,128)(2,1)S(1)} %get-tuple-element.61), channel_id=1, source_target_pairs={{0,6},{1,7},{2,0},{3,1},{4,2},{5,3},{6,4},{7,5},{8,14},{9,15},{10,... | collective-permute-start | bytes 393224 | tf_op jit(solution)/shard_map/ppermute | solution.py:60
  142.6 0.1 collective-permute-done.22.refs_3_
  142.7 1.6 %shard_map.87 = f32[512,128]{1,0:T(8,128)} custom-call(s32[38]{0:T(128)S(1)} %get-tuple-element.33.at_ref, s32[32,32]{1,0:T(8,128)S(1)} %copy-done.14, f32[512,128]{1,0:T(8,128)S(1)} %copy-done.13, f32[512,128]{1,0:T(8,128)S(1)} %get-tuple-element.51.refs_0_, bf16[512,128]{1,0:T(8,128)(2,1)S(1)} %collective-permute-done.20.refs_1_, ...), custom_call_target="tpu_custom_call" | custom-call | bytes 1048576 | tf_op jit(solution)/shard_map/pallas_call | solution.py:364
  144.3 0.4 all-to-all-done.4.refs_5_
  144.8 2.7 %shard_map.88.own_ref = f32[512,128]{1,0:T(8,128)S(1)} custom-call(s32[38]{0:T(128)S(1)} %get-tuple-element.33.at_ref, bf16[8,128,512]{2,1,0:T(8,128)(2,1)S(1)} %copy-done.2, bf16[8,128,512]{2,1,0:T(8,128)(2,1)} %collective-permute-done.8.refs_1_, bf16[4,128,512]{2,1,0:T(8,128)(2,1)S(1)} %collective-permute-done.13.refs_4_.refs_2_, ...), custom_call_target="tpu_custom_call" | custom-call | flops 536870912 | bytes 6291456 | tf_op jit(solution)/shard_map/pallas_call | solution.py:269
  147.4 2.8 %collective-permute-done.25.refs_1_ = bf16[4,128,128]{2,1,0:T(8,128)(2,1)S(1)} collective-permute-done((bf16[4,128,128]{2,1,0:T(8,128)(2,1)S(1)}, bf16[4,128,128]{2,1,0:T(8,128)(2,1)S(1)}, u32[]{:S(2)}, u32[]{:S(2)}) %collective-permute-start.25) | collective-permute-done | bytes 131104 | tf_op jit(solution)/shard_map/ppermute | solution.py:60
  150.3 0.8 shard_map.90
  (59 shorter events, 0.8 us)
Async XLA Ops:
  0.7 3.8 %copy-start.12 = (f32[512,128]{1,0:T(8,128)S(1)}, f32[512,128]{1,0:T(8,128)}, u32[]{:S(2)}) copy-start(f32[512,128]{1,0:T(8,128)} %cotangent_ref) | copy-start | bytes 786436
  0.7 3.8 %copy-start.14 = (s32[32,32]{1,0:T(8,128)S(1)}, s32[32,32]{1,0:T(8,128)}, u32[]{:S(2)}) copy-start(s32[32,32]{1,0:T(8,128)} %fill_ref.3) | copy-start | bytes 12292
  0.7 3.8 %copy-start.15 = (s32[32]{0:T(128)S(1)}, s32[32]{0:T(128)}, u32[]{:S(2)}) copy-start(s32[32]{0:T(128)} %owner_ref.1) | copy-start | bytes 388
  6.0 10.5 %collective-permute-start = (bf16[128,512]{1,0:T(8,128)(2,1)S(1)}, bf16[128,512]{1,0:T(8,128)(2,1)S(1)}, u32[]{:S(2)}, u32[]{:S(2)}) collective-permute-start(bf16[128,512]{1,0:T(8,128)(2,1)S(1)} %get-tuple-element.35), channel_id=1, source_target_pairs={{0,224},{8,232},{16,240},{24,248},{32,0},{40,8},{48,16},{56,24},{6... | collective-permute-start | bytes 393224 | tf_op jit(solution)/shard_map/ppermute | solution.py:50
  12.5 6.8 %collective-permute-start.3 = (bf16[128,512]{1,0:T(8,128)(2,1)S(1)}, bf16[128,512]{1,0:T(8,128)(2,1)S(1)}, u32[]{:S(2)}, u32[]{:S(2)}) collective-permute-start(bf16[128,512]{1,0:T(8,128)(2,1)S(1)} %get-tuple-element.35), channel_id=1, source_target_pairs={{0,32},{8,40},{16,48},{24,56},{32,64},{40,72},{48,80},{56,88},{64,... | collective-permute-start | bytes 393224 | tf_op jit(solution)/shard_map/ppermute | solution.py:50
  12.5 23.5 %all-to-all-start = ((bf16[4,1536,128]{2,1,0:T(8,128)(2,1)}), bf16[4,1536,128]{2,1,0:T(8,128)(2,1)S(1)}, u32[]{:S(2)}, u32[]{:S(2)}) async-start(bf16[4,1536,128]{2,1,0:T(8,128)(2,1)} %shard_map.77), calls=%async_computation | async-start | bytes 3145728 | tf_op jit(solution)/shard_map/all_to_all | solution.py:41
  16.5 4.7 %collective-permute-start.1 = (bf16[128,512]{1,0:T(8,128)(2,1)S(1)}, bf16[128,512]{1,0:T(8,128)(2,1)S(1)}, u32[]{:S(2)}, u32[]{:S(2)}) collective-permute-start(bf16[128,512]{1,0:T(8,128)(2,1)S(1)} %collective-permute-done), channel_id=1, source_target_pairs={{0,224},{8,232},{16,240},{24,248},{32,0},{40,8},{48,16},{56,24},{6... | collective-permute-start | bytes 393224 | tf_op jit(solution)/shard_map/ppermute | solution.py:50
  19.3 5.3 %collective-permute-start.4 = (bf16[128,512]{1,0:T(8,128)(2,1)S(1)}, bf16[128,512]{1,0:T(8,128)(2,1)S(1)}, u32[]{:S(2)}, u32[]{:S(2)}) collective-permute-start(bf16[128,512]{1,0:T(8,128)(2,1)S(1)} %collective-permute-done.3), channel_id=1, source_target_pairs={{0,32},{8,40},{16,48},{24,56},{32,64},{40,72},{48,80},{56,88},{64,... | collective-permute-start | bytes 393224 | tf_op jit(solution)/shard_map/ppermute | solution.py:50
  21.2 8.7 %collective-permute-start.2 = (bf16[128,512]{1,0:T(8,128)(2,1)S(1)}, bf16[128,512]{1,0:T(8,128)(2,1)S(1)}, u32[]{:S(2)}, u32[]{:S(2)}) collective-permute-start(bf16[128,512]{1,0:T(8,128)(2,1)S(1)} %collective-permute-done.1), channel_id=1, source_target_pairs={{0,224},{8,232},{16,240},{24,248},{32,0},{40,8},{48,16},{56,24},{6... | collective-permute-start | bytes 393224 | tf_op jit(solution)/shard_map/ppermute | solution.py:50
  24.6 5.3 %collective-permute-start.5 = (bf16[128,512]{1,0:T(8,128)(2,1)S(1)}, bf16[128,512]{1,0:T(8,128)(2,1)S(1)}, u32[]{:S(2)}, u32[]{:S(2)}) collective-permute-start(bf16[128,512]{1,0:T(8,128)(2,1)S(1)} %collective-permute-done.4), channel_id=1, source_target_pairs={{0,32},{8,40},{16,48},{24,56},{32,64},{40,72},{48,80},{56,88},{64,... | collective-permute-start | bytes 393224 | tf_op jit(solution)/shard_map/ppermute | solution.py:50
  29.9 4.6 %collective-permute-start.6 = (bf16[64,512]{1,0:T(8,128)(2,1)S(1)}, bf16[64,512]{1,0:T(8,128)(2,1)S(1)}, u32[]{:S(2)}, u32[]{:S(2)}) collective-permute-start(bf16[64,512]{1,0:T(8,128)(2,1)S(1)} %slice.16), channel_id=1, source_target_pairs={{0,32},{8,40},{16,48},{24,56},{32,64},{40,72},{48,80},{56,88},{64,... | collective-permute-start | bytes 196616 | tf_op jit(solution)/shard_map/ppermute | solution.py:50
  29.9 4.6 %collective-permute-start.7 = (bf16[64,512]{1,0:T(8,128)(2,1)S(1)}, bf16[64,512]{1,0:T(8,128)(2,1)S(1)}, u32[]{:S(2)}, u32[]{:S(2)}) collective-permute-start(bf16[64,512]{1,0:T(8,128)(2,1)S(1)} %slice.17), channel_id=1, source_target_pairs={{0,224},{8,232},{16,240},{24,248},{32,0},{40,8},{48,16},{56,24},{6... | collective-permute-start | bytes 196616 | tf_op jit(solution)/shard_map/ppermute | solution.py:50
  34.6 8.7 %copy-start = (bf16[8,128,512]{2,1,0:T(8,128)(2,1)}, bf16[8,128,512]{2,1,0:T(8,128)(2,1)S(1)}, u32[]{:S(2)}) copy-start(bf16[8,128,512]{2,1,0:T(8,128)(2,1)S(1)} %bitcast_dynamic-update-slice_fusion.refs_0_) | copy-start | bytes 3145732
  36.7 1.0 copy-start.6
  37.7 30.8 %all-to-all-start.1 = ((bf16[8,512,128]{2,1,0:T(8,128)(2,1)}), bf16[8,512,128]{2,1,0:T(8,128)(2,1)}, u32[]{:S(2)}, u32[]{:S(2)}) async-start(bf16[8,512,128]{2,1,0:T(8,128)(2,1)} %copy-done.6), calls=%async_computation.1 | async-start | bytes 2097152 | tf_op jit(solution)/shard_map/all_to_all | solution.py:45
  42.0 21.6 %collective-permute-start.8 = (bf16[8,128,512]{2,1,0:T(8,128)(2,1)S(1)}, bf16[8,128,512]{2,1,0:T(8,128)(2,1)}, u32[]{:S(2)}, u32[]{:S(2)}) collective-permute-start(bf16[8,128,512]{2,1,0:T(8,128)(2,1)S(1)} %bitcast_dynamic-update-slice_fusion.refs_0_), channel_id=1, source_target_pairs={{0,24},{8,0},{16,8},{24,16},{32,56},{40,32},{48,40},{56,48},{64,88... | collective-permute-start | bytes 3145736 | tf_op jit(solution)/shard_map/ppermute | solution.py:55
  43.4 20.8 %collective-permute-start.9 = (bf16[8,128,512]{2,1,0:T(8,128)(2,1)S(1)}, bf16[8,128,512]{2,1,0:T(8,128)(2,1)}, u32[]{:S(2)}, u32[]{:S(2)}) collective-permute-start(bf16[8,128,512]{2,1,0:T(8,128)(2,1)S(1)} %bitcast_dynamic-update-slice_fusion.refs_0_), channel_id=1, source_target_pairs={{0,8},{8,16},{16,24},{24,0},{32,40},{40,48},{48,56},{56,32},{64,72... | collective-permute-start | bytes 3145736 | tf_op jit(solution)/shard_map/ppermute | solution.py:55
  69.9 1.0 copy-start.9
  70.9 29.0 %all-to-all-start.3 = ((bf16[8,512,128]{2,1,0:T(8,128)(2,1)}), bf16[8,512,128]{2,1,0:T(8,128)(2,1)S(1)}, u32[]{:S(2)}, u32[]{:S(2)}) async-start(bf16[8,512,128]{2,1,0:T(8,128)(2,1)} %copy-done.9), calls=%async_computation.3 | async-start | bytes 2097152 | tf_op jit(solution)/shard_map/all_to_all | solution.py:45
  75.5 13.7 %collective-permute-start.13 = (bf16[4,128,512]{2,1,0:T(8,128)(2,1)S(1)}, bf16[4,128,512]{2,1,0:T(8,128)(2,1)S(1)}, u32[]{:S(2)}, u32[]{:S(2)}) collective-permute-start(bf16[4,128,512]{2,1,0:T(8,128)(2,1)S(1)} %slice.14), channel_id=1, source_target_pairs={{0,8},{8,16},{16,24},{24,0},{32,40},{40,48},{48,56},{56,32},{64,72... | collective-permute-start | bytes 1572872 | tf_op jit(solution)/shard_map/ppermute | solution.py:55
  76.7 12.5 %collective-permute-start.14 = (bf16[4,128,512]{2,1,0:T(8,128)(2,1)S(1)}, bf16[4,128,512]{2,1,0:T(8,128)(2,1)S(1)}, u32[]{:S(2)}, u32[]{:S(2)}) collective-permute-start(bf16[4,128,512]{2,1,0:T(8,128)(2,1)S(1)} %slice.15), channel_id=1, source_target_pairs={{0,24},{8,0},{16,8},{24,16},{32,56},{40,32},{48,40},{56,48},{64,88... | collective-permute-start | bytes 1572872 | tf_op jit(solution)/shard_map/ppermute | solution.py:55
  79.5 6.1 %collective-permute-start.10 = (bf16[512,128]{1,0:T(8,128)(2,1)S(1)}, bf16[512,128]{1,0:T(8,128)(2,1)S(1)}, u32[]{:S(2)}, u32[]{:S(2)}) collective-permute-start(bf16[512,128]{1,0:T(8,128)(2,1)S(1)} %get-tuple-element.39), channel_id=1, source_target_pairs={{0,6},{1,7},{2,0},{3,1},{4,2},{5,3},{6,4},{7,5},{8,14},{9,15},{10,... | collective-permute-start | bytes 393224 | tf_op jit(solution)/shard_map/ppermute | solution.py:60
  82.2 5.6 %collective-permute-start.11 = (bf16[512,128]{1,0:T(8,128)(2,1)S(1)}, bf16[512,128]{1,0:T(8,128)(2,1)S(1)}, u32[]{:S(2)}, u32[]{:S(2)}) collective-permute-start(bf16[512,128]{1,0:T(8,128)(2,1)S(1)} %get-tuple-element.39), channel_id=1, source_target_pairs={{0,4},{1,5},{2,6},{3,7},{4,0},{5,1},{6,2},{7,3},{8,12},{9,13},{10,... | collective-permute-start | bytes 393224 | tf_op jit(solution)/shard_map/ppermute | solution.py:60
  82.5 6.7 %collective-permute-start.12 = (bf16[512,128]{1,0:T(8,128)(2,1)S(1)}, bf16[512,128]{1,0:T(8,128)(2,1)S(1)}, u32[]{:S(2)}, u32[]{:S(2)}) collective-permute-start(bf16[512,128]{1,0:T(8,128)(2,1)S(1)} %get-tuple-element.39), channel_id=1, source_target_pairs={{0,2},{1,3},{2,4},{3,5},{4,6},{5,7},{6,0},{7,1},{8,10},{9,11},{10,... | collective-permute-start | bytes 393224 | tf_op jit(solution)/shard_map/ppermute | solution.py:60
  89.3 0.8 copy-start.3
  90.1 8.1 %collective-permute-start.15 = (bf16[4,4,128,128]{3,2,1,0:T(8,128)(2,1)S(1)}, bf16[4,4,128,128]{3,2,1,0:T(8,128)(2,1)S(1)}, u32[]{:S(2)}, u32[]{:S(2)}) collective-permute-start(bf16[4,4,128,128]{3,2,1,0:T(8,128)(2,1)S(1)} %shard_map.81.same_ref), channel_id=1, source_target_pairs={{0,1},{1,0},{2,3},{3,2},{4,5},{5,4},{6,7},{7,6},{8,9},{9,8},{10,11... | collective-permute-start | bytes 1572872 | tf_op jit(solution)/shard_map/ppermute | solution.py:64
  99.1 0.8 copy-start.7
  99.9 23.7 %all-to-all-start.2 = ((bf16[8,2,128,128]{3,2,1,0:T(8,128)(2,1)}), bf16[8,2,128,128]{3,2,1,0:T(8,128)(2,1)}, u32[]{:S(2)}, u32[]{:S(2)}) async-start(bf16[8,2,128,128]{3,2,1,0:T(8,128)(2,1)} %bitcast.29), calls=%async_computation.2 | async-start | bytes 1048576 | tf_op jit(solution)/shard_map/all_to_all | solution.py:45
  106.8 10.5 %copy-start.1 = (bf16[8,128,512]{2,1,0:T(8,128)(2,1)S(1)}, bf16[8,128,512]{2,1,0:T(8,128)(2,1)}, u32[]{:S(2)}) copy-start(bf16[8,128,512]{2,1,0:T(8,128)(2,1)} %copy-done) | copy-start | bytes 3145732
  106.8 10.5 %copy-start.4 = (bf16[4,128,512]{2,1,0:T(8,128)(2,1)S(1)}, bf16[4,128,512]{2,1,0:T(8,128)(2,1)}, u32[]{:S(2)}) copy-start(bf16[4,128,512]{2,1,0:T(8,128)(2,1)} %copy-done.3) | copy-start | bytes 1572868
  108.1 6.9 %collective-permute-start.17 = (bf16[4,128,128]{2,1,0:T(8,128)(2,1)S(1)}, bf16[4,128,128]{2,1,0:T(8,128)(2,1)S(1)}, u32[]{:S(2)}, u32[]{:S(2)}) collective-permute-start(bf16[4,128,128]{2,1,0:T(8,128)(2,1)S(1)} %get-tuple-element.44), channel_id=1, source_target_pairs={{0,8},{8,16},{16,24},{24,0},{32,40},{40,48},{48,56},{56,32},{64,72... | collective-permute-start | bytes 393224 | tf_op jit(solution)/shard_map/ppermute | solution.py:55
  108.2 7.2 %collective-permute-start.18 = (bf16[4,128,128]{2,1,0:T(8,128)(2,1)S(1)}, bf16[4,128,128]{2,1,0:T(8,128)(2,1)S(1)}, u32[]{:S(2)}, u32[]{:S(2)}) collective-permute-start(bf16[4,128,128]{2,1,0:T(8,128)(2,1)S(1)} %get-tuple-element.45), channel_id=1, source_target_pairs={{0,16},{8,24},{16,0},{24,8},{32,48},{40,56},{48,32},{56,40},{64,80... | collective-permute-start | bytes 393224 | tf_op jit(solution)/shard_map/ppermute | solution.py:55
  109.2 7.0 %collective-permute-start.19 = (bf16[4,128,128]{2,1,0:T(8,128)(2,1)S(1)}, bf16[4,128,128]{2,1,0:T(8,128)(2,1)S(1)}, u32[]{:S(2)}, u32[]{:S(2)}) collective-permute-start(bf16[4,128,128]{2,1,0:T(8,128)(2,1)S(1)} %get-tuple-element.46), channel_id=1, source_target_pairs={{0,24},{8,0},{16,8},{24,16},{32,56},{40,32},{48,40},{56,48},{64,88... | collective-permute-start | bytes 393224 | tf_op jit(solution)/shard_map/ppermute | solution.py:55
  116.3 1.0 copy-start.8
  121.0 0.9 copy-start.10
  123.6 21.2 %all-to-all-start.4 = ((bf16[8,4,128,128]{3,2,1,0:T(8,128)(2,1)}), bf16[8,4,128,128]{3,2,1,0:T(8,128)(2,1)}, u32[]{:S(2)}, u32[]{:S(2)}) async-start(bf16[8,4,128,128]{3,2,1,0:T(8,128)(2,1)} %copy-done.8), calls=%async_computation.4 | async-start | bytes 2097152 | tf_op jit(solution)/shard_map/all_to_all | solution.py:350
  129.5 6.8 %copy-start.11 = (bf16[5,4,128,128]{3,2,1,0:T(8,128)(2,1)S(1)}, bf16[5,4,128,128]{3,2,1,0:T(8,128)(2,1)}, u32[]{:S(2)}) copy-start(bf16[5,4,128,128]{3,2,1,0:T(8,128)(2,1)} %copy-done.10) | copy-start | bytes 1966084
  129.5 2.1 %collective-permute-start.16 = (bf16[8,2,128,128]{3,2,1,0:T(8,128)(2,1)}, bf16[8,2,128,128]{3,2,1,0:T(8,128)(2,1)S(1)}, u32[]{:S(2)}, u32[]{:S(2)}) collective-permute-start(bf16[8,2,128,128]{3,2,1,0:T(8,128)(2,1)} %all-to-all-done.2.same_ref), channel_id=1, source_target_pairs={{0,1},{1,0},{2,3},{3,2},{4,5},{5,4},{6,7},{7,6},{8,9},{9,8},{10,11... | collective-permute-start | bytes 1572872 | tf_op jit(solution)/shard_map/ppermute | solution.py:64
  129.7 13.0 %copy-start.13 = (f32[512,128]{1,0:T(8,128)S(1)}, f32[512,128]{1,0:T(8,128)}, u32[]{:S(2)}) copy-start(f32[512,128]{1,0:T(8,128)} %trailing_ref.1) | copy-start | bytes 786436
  129.7 6.5 %collective-permute-start.23 = (bf16[5,4,128,128]{3,2,1,0:T(8,128)(2,1)}, bf16[5,4,128,128]{3,2,1,0:T(8,128)(2,1)S(1)}, u32[]{:S(2)}, u32[]{:S(2)}) collective-permute-start(bf16[5,4,128,128]{3,2,1,0:T(8,128)(2,1)} %get-tuple-element.57), channel_id=1, source_target_pairs={{0,1},{1,0},{2,3},{3,2},{4,5},{5,4},{6,7},{7,6},{8,9},{9,8},{10,11... | collective-permute-start | bytes 1966088 | tf_op jit(solution)/shard_map/ppermute | solution.py:64
  133.5 11.3 %copy-start.2 = (bf16[8,128,512]{2,1,0:T(8,128)(2,1)S(1)}, bf16[8,128,512]{2,1,0:T(8,128)(2,1)}, u32[]{:S(2)}) copy-start(bf16[8,128,512]{2,1,0:T(8,128)(2,1)} %copy-done) | copy-start | bytes 3145732
  133.5 11.3 %copy-start.5 = (bf16[4,128,512]{2,1,0:T(8,128)(2,1)S(1)}, bf16[4,128,512]{2,1,0:T(8,128)(2,1)}, u32[]{:S(2)}) copy-start(bf16[4,128,512]{2,1,0:T(8,128)(2,1)} %copy-done.3) | copy-start | bytes 1572868
  133.5 6.8 %collective-permute-start.20 = (bf16[512,128]{1,0:T(8,128)(2,1)S(1)}, bf16[512,128]{1,0:T(8,128)(2,1)S(1)}, u32[]{:S(2)}, u32[]{:S(2)}) collective-permute-start(bf16[512,128]{1,0:T(8,128)(2,1)S(1)} %get-tuple-element.52), channel_id=1, source_target_pairs={{0,8},{8,16},{16,24},{24,0},{32,40},{40,48},{48,56},{56,32},{64,72... | collective-permute-start | bytes 393224 | tf_op jit(solution)/shard_map/ppermute | solution.py:55
  133.6 9.1 %collective-permute-start.21 = (bf16[512,128]{1,0:T(8,128)(2,1)S(1)}, bf16[512,128]{1,0:T(8,128)(2,1)S(1)}, u32[]{:S(2)}, u32[]{:S(2)}) collective-permute-start(bf16[512,128]{1,0:T(8,128)(2,1)S(1)} %get-tuple-element.53), channel_id=1, source_target_pairs={{0,16},{8,24},{16,0},{24,8},{32,48},{40,56},{48,32},{56,40},{64,80... | collective-permute-start | bytes 393224 | tf_op jit(solution)/shard_map/ppermute | solution.py:55
  135.8 7.0 %collective-permute-start.22 = (bf16[512,128]{1,0:T(8,128)(2,1)S(1)}, bf16[512,128]{1,0:T(8,128)(2,1)S(1)}, u32[]{:S(2)}, u32[]{:S(2)}) collective-permute-start(bf16[512,128]{1,0:T(8,128)(2,1)S(1)} %get-tuple-element.54), channel_id=1, source_target_pairs={{0,24},{8,0},{16,8},{24,16},{32,56},{40,32},{48,40},{56,48},{64,88... | collective-permute-start | bytes 393224 | tf_op jit(solution)/shard_map/ppermute | solution.py:55
  136.4 11.1 %collective-permute-start.24 = (bf16[4,128,128]{2,1,0:T(8,128)(2,1)S(1)}, bf16[4,128,128]{2,1,0:T(8,128)(2,1)S(1)}, u32[]{:S(2)}, u32[]{:S(2)}) collective-permute-start(bf16[4,128,128]{2,1,0:T(8,128)(2,1)S(1)} %get-tuple-element.59), channel_id=1, source_target_pairs={{0,2},{1,3},{2,4},{3,5},{4,6},{5,7},{6,0},{7,1},{8,10},{9,11},{10,... | collective-permute-start | bytes 393224 | tf_op jit(solution)/shard_map/ppermute | solution.py:60
  137.9 12.4 %collective-permute-start.25 = (bf16[4,128,128]{2,1,0:T(8,128)(2,1)S(1)}, bf16[4,128,128]{2,1,0:T(8,128)(2,1)S(1)}, u32[]{:S(2)}, u32[]{:S(2)}) collective-permute-start(bf16[4,128,128]{2,1,0:T(8,128)(2,1)S(1)} %get-tuple-element.60), channel_id=1, source_target_pairs={{0,4},{1,5},{2,6},{3,7},{4,0},{5,1},{6,2},{7,3},{8,12},{9,13},{10,... | collective-permute-start | bytes 393224 | tf_op jit(solution)/shard_map/ppermute | solution.py:60
  140.3 10.0 %collective-permute-start.26 = (bf16[4,128,128]{2,1,0:T(8,128)(2,1)S(1)}, bf16[4,128,128]{2,1,0:T(8,128)(2,1)S(1)}, u32[]{:S(2)}, u32[]{:S(2)}) collective-permute-start(bf16[4,128,128]{2,1,0:T(8,128)(2,1)S(1)} %get-tuple-element.61), channel_id=1, source_target_pairs={{0,6},{1,7},{2,0},{3,1},{4,2},{5,3},{6,4},{7,5},{8,14},{9,15},{10,... | collective-permute-start | bytes 393224 | tf_op jit(solution)/shard_map/ppermute | solution.py:60
